TPU v7x, 512 devices: a whole 4x4x16 slice. The times are simulated.
512 devices in a mesh: group: 16 (over x_hi, y, core), tensor: 32 (over x_lo, z).
Axes of the slice: x: 4 (x_hi: 2, x_lo: 2; x = x_hi * 2 + x_lo), y: 4, z: 16, core: 2. Of those that a mesh axis runs over, the one named last changes fastest.
Arguments:
- teacher_feat: bfloat16 [4096, 4096], P(('group', 'tensor')), may hold values from -6 to 6
- teacher_gain: float32 [4096], replicated, may hold values from 0.5 to 1.5
- teacher_proj: bfloat16 [4096, 256], P('tensor'), may hold values from -0.09375 to 0.09375
- teacher_proto: bfloat16 [256, 32768], P(None, 'tensor')
- center: float32 [32768], P('tensor'), may hold values from -3 to 3
- routes: int32 [256, 1], replicated, may hold values from 0 to 15; in each aligned block of 16 rows (0 to 15, 16 to 31, ...) at most 2 rows name the same one
- large_groups: int32 [1], replicated, may hold values from 1 to 15
- feat_large: bfloat16 [8192, 1024], P(('group', 'tensor')), may hold values from -6 to 6
- feat_huge: bfloat16 [8192, 1280], P(('group', 'tensor')), may hold values from -6 to 6
- gain_large: float32 [1024], replicated, may hold values from 0.5 to 1.5
- gain_huge: float32 [1280], replicated, may hold values from 0.5 to 1.5
- proj_large: bfloat16 [1024, 256], P('tensor'), may hold values from -0.1875 to 0.1875
- proj_huge: bfloat16 [1280, 256], P('tensor'), may hold values from -0.15625 to 0.15625
- proto_large: bfloat16 [256, 32768], P(None, 'tensor')
- proto_huge: bfloat16 [256, 32768], P(None, 'tensor')
Outputs:
- loss: float32 [1], replicated
- grad_large: bfloat16 [256, 32768], P(None, 'tensor')
- grad_huge: bfloat16 [256, 32768], P(None, 'tensor')
Inputs may be any that keep to these rules, and one draw needn't show every extreme that they name: `routes`: of the 16 crops of one sending group, at most 2 name the same receiving group, and 2 is reached. `large_groups`: groups below this number train the large student, the rest the huge one.
All inputs are finite; a program needn't handle non-finite values.
Results may differ from a plain program's by a relative error of at most 0.012.
The roundings to bfloat16 on the way count: a program that leaves them out, or rounds other values in their place, can miss the bound.
Values may be sent and summed in bfloat16 or wider, within the bound.
No kernel may reach another device: no remote copies, remote signals or barrier semaphores. Data moves between devices by JAX's collectives and lax.ppermute only.
A program may use at most 64 MiB of HBM per device.

v0:
```python
import jax
import jax.numpy as jnp
from jax import lax
from jax.sharding import PartitionSpec as P

PATCH = 16
CG = 16


TEACHER_TEMP = 0.07
STUDENT_TEMP = 0.1
EPSILON = 1e-06


def layer_norm(values, gains):
    widened = values.astype(jnp.float32)
    row_mean = jnp.mean(widened, axis=-1, keepdims=True)
    centred = widened - row_mean
    spread = jnp.mean(centred * centred, axis=-1, keepdims=True)
    return (centred * lax.rsqrt(spread + EPSILON) * gains).astype(jnp.bfloat16)


def unit_rows(middle):
    return (middle * lax.rsqrt(jnp.mean(middle * middle, axis=-1, keepdims=True) + EPSILON)).astype(
        jnp.bfloat16
    )


def slot_table(routes):
    target_group = routes[:, 0].reshape(-1, CG)
    earlier = jnp.arange(CG)[:, None] > jnp.arange(CG)[None, :]
    matching = target_group[:, :, None] == target_group[:, None, :]
    slot_rank = jnp.sum((matching & earlier).astype(jnp.int32), axis=2)
    return (target_group, slot_rank)


def spread_stats(values):
    local_top = jnp.max(values, axis=-1)
    row_top = lax.pmax(local_top, "tensor")
    row_total = lax.psum(jnp.sum(jnp.exp(values - row_top[:, None]), axis=-1), "tensor")
    return (row_top, row_total)


def teacher_targets(units, teacher_proto, center):
    shifted = (
        jnp.dot(units, teacher_proto, preferred_element_type=jnp.float32) - center[None, :]
    ) / TEACHER_TEMP
    row_top, row_total = spread_stats(shifted)
    return (jnp.exp(shifted - row_top[:, None]) / row_total[:, None]).astype(jnp.bfloat16)


def shards(
    teacher_feat,
    teacher_gain,
    teacher_proj,
    teacher_proto,
    center,
    routes,
    large_groups,
    feat_large,
    feat_huge,
    gain_large,
    gain_huge,
    proj_large,
    proj_huge,
    proto_large,
    proto_huge,
):
    groups = lax.axis_size("group")
    own_group = lax.axis_index("group")
    protos = teacher_proto.shape[1]
    slots_per = feat_large.shape[0] * lax.axis_size("tensor") // (groups * PATCH)
    own_normed = layer_norm(teacher_feat, teacher_gain)
    teacher_cols = lax.all_to_all(own_normed, "tensor", split_axis=1, concat_axis=0, tiled=True)
    teacher_mid = lax.psum_scatter(
        jnp.dot(teacher_cols, teacher_proj, preferred_element_type=jnp.float32),
        "tensor",
        scatter_dimension=0,
        tiled=True,
    )
    group_units = lax.all_gather(unit_rows(teacher_mid), "tensor", axis=0, tiled=True)
    target_group, slot_rank = slot_table(routes)
    slot_ids = jnp.arange(slots_per, dtype=jnp.int32)
    wanted_here = (target_group == own_group)[:, None, :] & (
        slot_rank[:, None, :] == slot_ids[None, :, None]
    )
    own_targets = lax.dynamic_index_in_dim(target_group, own_group, 0, keepdims=False)
    own_slots = lax.dynamic_index_in_dim(slot_rank, own_group, 0, keepdims=False)
    group_ids = jnp.arange(groups, dtype=jnp.int32)
    sending = (
        (own_targets[None, None, :] == group_ids[:, None, None])
        & (own_slots[None, None, :] == slot_ids[None, :, None])
    ).astype(jnp.bfloat16)
    filled = jnp.any(wanted_here, axis=2).astype(jnp.float32)
    usable = jnp.broadcast_to(filled[:, :, None], (groups, slots_per, PATCH)).reshape(-1)
    target = teacher_targets(group_units, teacher_proto, center)
    packed = jnp.einsum(
        "jki,ipx->jkpx",
        sending,
        target.reshape(CG, PATCH, protos),
        preferred_element_type=jnp.float32,
    ).astype(jnp.bfloat16)
    received = lax.all_to_all(packed, "group", split_axis=0, concat_axis=0, tiled=True).reshape(
        -1, protos
    )
    wanted = received.astype(jnp.float32) * usable[:, None]

    def learn_head(units, weights):
        scores = jnp.dot(units, weights, preferred_element_type=jnp.float32) / STUDENT_TEMP
        row_top, row_total = spread_stats(scores)
        log_prob = scores - row_top[:, None] - jnp.log(row_total)[:, None]
        student_prob = jnp.exp(scores - row_top[:, None]) / row_total[:, None]
        cross_sum = -jnp.sum(wanted * log_prob)
        deltas = ((student_prob * usable[:, None] - wanted) / STUDENT_TEMP).astype(jnp.bfloat16)
        head_grad = (
            lax.dot_general(
                units, deltas, (((0,), (0,)), ((), ())), preferred_element_type=jnp.float32
            )
            / PATCH
        )
        return (cross_sum, head_grad)

    def large_side():
        large_cols = lax.all_to_all(
            layer_norm(feat_large, gain_large), "tensor", split_axis=1, concat_axis=0, tiled=True
        )
        large_mid = lax.psum_scatter(
            jnp.dot(large_cols, proj_large, preferred_element_type=jnp.float32),
            "tensor",
            scatter_dimension=0,
            tiled=True,
        )
        units = lax.all_gather(unit_rows(large_mid), "tensor", axis=0, tiled=True)
        cross_sum, head_grad = learn_head(units, proto_large)
        return (cross_sum, head_grad, jnp.zeros_like(head_grad))

    def huge_side():
        huge_cols = lax.all_to_all(
            layer_norm(feat_huge, gain_huge), "tensor", split_axis=1, concat_axis=0, tiled=True
        )
        huge_mid = lax.psum_scatter(
            jnp.dot(huge_cols, proj_huge, preferred_element_type=jnp.float32),
            "tensor",
            scatter_dimension=0,
            tiled=True,
        )
        units = lax.all_gather(unit_rows(huge_mid), "tensor", axis=0, tiled=True)
        cross_sum, head_grad = learn_head(units, proto_huge)
        return (cross_sum, jnp.zeros_like(head_grad), head_grad)

    cross_sum, grad_large, grad_huge = lax.cond(own_group < large_groups[0], large_side, huge_side)
    grad_large, grad_huge = lax.psum((grad_large, grad_huge), "group")
    loss_sum = lax.psum(cross_sum, ("group", "tensor"))
    loss = (loss_sum / (routes.shape[0] * PATCH)).reshape(1)
    return (loss, grad_large.astype(jnp.bfloat16), grad_huge.astype(jnp.bfloat16))


def solution(mesh):
    placed = (
        P(("group", "tensor"), None),
        P(),
        P("tensor", None),
        P(None, "tensor"),
        P("tensor"),
        P(),
        P(),
        P(("group", "tensor"), None),
        P(("group", "tensor"), None),
        P(),
        P(),
        P("tensor", None),
        P("tensor", None),
        P(None, "tensor"),
        P(None, "tensor"),
    )
    return jax.shard_map(
        shards,
        mesh=mesh,
        in_specs=placed,
        out_specs=(P(), P(None, "tensor"), P(None, "tensor")),
        check_vma=False,
    )
```

profile of v0, /device:TPU:1, one launch (start us, length us, event | category | flops | bytes accessed | tf_op | source)
XLA Modules:
  0.0 907.4 jit_solution(12455767269943170096)
XLA Ops:
  7.2 1.0 convert_reduce_fusion.2
  8.2 1.1 fusion.18
  9.3 1.6 fusion.21
  10.9 17.0 %all-to-all-start.2 = ((bf16[8,32,128]{2,0,1:T(8,128)(2,1)}), bf16[8,32,128]{2,0,1:T(8,128)(2,1)S(1)}, u32[]{:S(2)}, u32[]{:S(2)}) async-start(bf16[8,32,128]{2,0,1:T(8,128)(2,1)} %fusion.21), calls=%async_computation.4 | async-start | bytes 131072 | tf_op jit(solution)/shard_map/all_to_all | solution.py:74
  28.4 1.3 reduce.3
  30.3 10.8 %all-to-all-done.2 = bf16[8,32,128]{2,0,1:T(8,128)(2,1)S(1)} async-done(((bf16[8,32,128]{2,0,1:T(8,128)(2,1)}), bf16[8,32,128]{2,0,1:T(8,128)(2,1)S(1)}, u32[]{:S(2)}, u32[]{:S(2)}) %all-to-all-start.2) | async-done | bytes 65568 | tf_op jit(solution)/shard_map/all_to_all | solution.py:74
  41.0 1.7 fusion.22
  42.8 102.2 %reduce-scatter.8.cloned.1.call-done = f32[8,256]{1,0:T(8,128)} async-done(((f32[256,256]{1,0:T(8,128)}), f32[8,256]{1,0:T(8,128)}) %reduce-scatter.8.cloned.1.call-update) | async-done | bytes 8208 | tf_op jit(solution)/shard_map/reduce_scatter | solution.py:75
  145.1 0.8 multiply_reduce_fusion.5
  146.7 47.2 %all_gather.9 = bf16[256,256]{1,0:T(8,128)(2,1)S(1)} all-gather(bf16[8,256]{1,0:T(8,128)(2,1)S(1)} %multiply_convert_fusion.6), channel_id=1, replica_groups=mesh['group'=16,'tensor'=32] {'tensor'}, dimensions={0}, use_global_device_ids=true | all-gather | bytes 135168 | tf_op jit(solution)/shard_map/all_gather | solution.py:81
  193.9 1.1 fusion.30
  194.9 46.6 %pmax.21 = f32[256]{0:T(256)S(1)} all-reduce(f32[256]{0:T(256)S(1)} %get-tuple-element.86), channel_id=1, replica_groups=mesh['group'=16,'tensor'=32] {'tensor'}, use_global_device_ids=true, to_apply=%region_6.7 | all-reduce | flops 256 | bytes 2048 | tf_op jit(solution)/shard_map/pmax | solution.py:39
  241.8 47.4 %psum.42 = f32[256]{0:T(256)S(1)} all-reduce(f32[256]{0:T(256)S(1)} %fusion.13), channel_id=1, replica_groups=mesh['group'=16,'tensor'=32] {'tensor'}, use_global_device_ids=true, to_apply=%region_8.9 | all-reduce | flops 256 | bytes 2048 | tf_op jit(solution)/shard_map/psum | solution.py:40
  290.0 1.6 copy.39
  291.6 73.3 %all-to-all-start.3 = ((bf16[16,2,16,1024]{3,2,1,0:T(8,128)(2,1)}), bf16[16,2,16,1024]{3,2,1,0:T(8,128)(2,1)S(1)}, u32[]{:S(2)}, u32[]{:S(2)}) async-start(bf16[16,2,16,1024]{3,2,1,0:T(8,128)(2,1)} %copy.39), calls=%async_computation.6 | async-start | bytes 2097152 | tf_op jit(solution)/shard_map/all_to_all | solution.py:103
  366.1 16.0 %all-to-all-done.3 = bf16[16,2,16,1024]{3,2,1,0:T(8,128)(2,1)S(1)} async-done(((bf16[16,2,16,1024]{3,2,1,0:T(8,128)(2,1)}), bf16[16,2,16,1024]{3,2,1,0:T(8,128)(2,1)S(1)}, u32[]{:S(2)}, u32[]{:S(2)}) %all-to-all-start.3) | async-done | bytes 1048608 | tf_op jit(solution)/shard_map/all_to_all | solution.py:103
  382.1 1.6 convert_multiply_fusion
  383.8 270.5 %conditional.1 = (f32[256,1024]{1,0:T(8,128)}, f32[256,1024]{1,0:T(8,128)}, f32[]{:T(128)}, f32[]{:T(128)}, f32[512,1024]{1,0:T(8,128)}, /*index=5*/f32[512,1024...) conditional(s32[]{:T(128)} %convert_element_type.65, (bf16[16,1280]{1,0:T(8,128)(2,1)S(1)}, ...), branch_computations={%region_10.19_spmd, %region_19.28_spmd} | conditional | flops 553103360 | bytes 31308796 | solution.py:151
  384.6 15.5 %all_to_all.55 = bf16[32,2,256]{2,1,0:T(2,128)(2,1)S(1)} all-to-all(bf16[32,2,256]{2,1,0:T(2,128)(2,1)S(1)} %reshape.190), channel_id=1, replica_groups=mesh['group'=16,'tensor'=32] {'tensor'}, dimensions={0} | all-to-all | bytes 65536 | tf_op jit(solution)/shard_map/cond/branch_1_fun/all_to_all | solution.py:124
  400.2 1.0 fusion.32
  401.4 99.1 %reduce-scatter.6.cloned.1.call-done = f32[16,256]{1,0:T(8,128)} async-done(((f32[512,256]{1,0:T(8,128)}), f32[16,256]{1,0:T(8,128)}) %reduce-scatter.6.cloned.1.call-update) | async-done | bytes 16400 | tf_op jit(solution)/shard_map/cond/branch_1_fun/reduce_scatter | solution.py:127
  500.5 0.8 multiply_reduce_fusion.3
  502.1 48.2 %all_gather.7 = bf16[512,256]{1,0:T(8,128)(2,1)S(1)} all-gather(bf16[16,256]{1,0:T(8,128)(2,1)S(1)} %multiply_convert_fusion.5), channel_id=1, replica_groups=mesh['group'=16,'tensor'=32] {'tensor'}, dimensions={0}, use_global_device_ids=true | all-gather | bytes 270336 | tf_op jit(solution)/shard_map/cond/branch_1_fun/all_gather | solution.py:133
  550.9 46.8 %pmax.19 = f32[512]{0:T(512)S(1)} all-reduce(f32[512]{0:T(512)S(1)} %get-tuple-element.84), channel_id=1, replica_groups=mesh['group'=16,'tensor'=32] {'tensor'}, use_global_device_ids=true, to_apply=%region_25.25 | all-reduce | flops 512 | bytes 4096 | tf_op jit(solution)/shard_map/cond/branch_1_fun/pmax | solution.py:39
  597.7 1.7 exponential_reduce_fusion.1
  599.4 47.4 %psum.37 = f32[512]{0:T(512)} all-reduce(f32[512]{0:T(512)S(1)} %get-tuple-element.80), channel_id=1, replica_groups=mesh['group'=16,'tensor'=32] {'tensor'}, use_global_device_ids=true, to_apply=%region_27.27 | all-reduce | flops 512 | bytes 4096 | tf_op jit(solution)/shard_map/cond/branch_1_fun/psum | solution.py:40
  647.5 1.7 copy.73
  649.7 3.4 convolution_multiply_fusion.1
  653.1 1.1 broadcast.185
  654.2 2.8 multiply_reduce_fusion.4
  657.7 166.4 %psum.43 = f32[]{:T(128)} all-reduce(f32[]{:T(128)S(6)} %neg.5), channel_id=1, replica_groups=mesh['group'=16,'tensor'=32] {'group','tensor'}, use_global_device_ids=true, to_apply=%region_29.0 | all-reduce | flops 1 | bytes 8 | tf_op jit(solution)/shard_map/psum | solution.py:153
  824.8 74.6 %all-reduce.2 = (bf16[256,1024]{1,0:T(8,128)(2,1)}, bf16[256,1024]{1,0:T(8,128)(2,1)}) all-reduce(f32[256,1024]{1,0:T(8,128)} %get-tuple-element.58, f32[256,1024]{1,0:T(8,128)} %get-tuple-element.59), channel_id=1, replica_groups=mesh['group'=16,'tensor'=32] {'group'}, use_global_device_ids=true, to_apply=%region_30.31 | all-reduce | flops 524288 | bytes 3145728 | tf_op jit(solution)/shard_map/psum | solution.py:152
  (59 shorter events, 6.9 us)
Async XLA Ops:
  7.2 186.7 %copy-start = (bf16[256,1024]{1,0:T(8,128)(2,1)S(1)}, bf16[256,1024]{1,0:T(8,128)(2,1)}, u32[]{:S(2)}) copy-start(bf16[256,1024]{1,0:T(8,128)(2,1)} %param.20) | copy-start | bytes 1572868
  10.9 30.2 %all-to-all-start.2 = ((bf16[8,32,128]{2,0,1:T(8,128)(2,1)}), bf16[8,32,128]{2,0,1:T(8,128)(2,1)S(1)}, u32[]{:S(2)}, u32[]{:S(2)}) async-start(bf16[8,32,128]{2,0,1:T(8,128)(2,1)} %fusion.21), calls=%async_computation.4 | async-start | bytes 131072 | tf_op jit(solution)/shard_map/all_to_all | solution.py:74
  27.8 117.2 %reduce-scatter.8.cloned.1.call-start = ((), (), s32[]{:S(2)}) async-start(), calls=%async_computation.9 | async-start | bytes 270336 | tf_op jit(solution)/shard_map/reduce_scatter | solution.py:75
  291.6 90.5 %all-to-all-start.3 = ((bf16[16,2,16,1024]{3,2,1,0:T(8,128)(2,1)}), bf16[16,2,16,1024]{3,2,1,0:T(8,128)(2,1)S(1)}, u32[]{:S(2)}, u32[]{:S(2)}) async-start(bf16[16,2,16,1024]{3,2,1,0:T(8,128)(2,1)} %copy.39), calls=%async_computation.6 | async-start | bytes 2097152 | tf_op jit(solution)/shard_map/all_to_all | solution.py:103
  364.9 18.8 %copy-start.3 = (bf16[256,1024]{1,0:T(8,128)(2,1)S(1)}, bf16[256,1024]{1,0:T(8,128)(2,1)}, u32[]{:S(2)}) copy-start(bf16[256,1024]{1,0:T(8,128)(2,1)} %param.31) | copy-start | bytes 1572868
  364.9 18.8 %copy-start.5 = (bf16[16,1280]{1,0:T(8,128)(2,1)S(1)}, bf16[16,1280]{1,0:T(8,128)(2,1)}, u32[]{:S(2)}) copy-start(bf16[16,1280]{1,0:T(8,128)(2,1)} %param.25) | copy-start | bytes 122884
  364.9 18.8 %copy-start.6 = (bf16[16,1024]{1,0:T(8,128)(2,1)S(1)}, bf16[16,1024]{1,0:T(8,128)(2,1)}, u32[]{:S(2)}) copy-start(bf16[16,1024]{1,0:T(8,128)(2,1)} %param.24) | copy-start | bytes 98308
  364.9 18.8 %copy-start.7 = (bf16[40,256]{1,0:T(8,128)(2,1)S(1)}, bf16[40,256]{1,0:T(8,128)(2,1)}, u32[]{:S(2)}) copy-start(bf16[40,256]{1,0:T(8,128)(2,1)} %param.29) | copy-start | bytes 61444
  364.9 18.8 %copy-start.8 = (bf16[32,256]{1,0:T(8,128)(2,1)S(1)}, bf16[32,256]{1,0:T(8,128)(2,1)}, u32[]{:S(2)}) copy-start(bf16[32,256]{1,0:T(8,128)(2,1)} %param.28) | copy-start | bytes 49156
  365.0 18.8 %copy-start.9 = (f32[1280]{0:T(1024)S(1)}, f32[1280]{0:T(1024)}, u32[]{:S(2)}) copy-start(f32[1280]{0:T(1024)} %param.27) | copy-start | bytes 15364
  365.0 18.8 %copy-start.10 = (f32[1024]{0:T(1024)S(1)}, f32[1024]{0:T(1024)}, u32[]{:S(2)}) copy-start(f32[1024]{0:T(1024)} %param.26) | copy-start | bytes 12292
  383.8 166.6 %copy-start.4 = (bf16[256,1024]{1,0:T(8,128)(2,1)S(1)}, bf16[256,1024]{1,0:T(8,128)(2,1)}, u32[]{:S(2)}) copy-start(bf16[256,1024]{1,0:T(8,128)(2,1)} %get-tuple-element.75) | copy-start | bytes 1572868 | tf_op jit(solution)/shard_map/cond
  383.8 116.7 %reduce-scatter.6.cloned.1.call-start = ((), (), s32[]{:S(2)}) async-start(), calls=%async_computation.8 | async-start | bytes 540672 | tf_op jit(solution)/shard_map/cond/branch_1_fun/reduce_scatter | solution.py:127
  647.5 2.2 copy-start.2
Sparse Core Ops, SparseCore 0:
  42.9 102.1 reduce-scatter.7
  401.4 99.0 reduce-scatter.5
where the time goes:
time: 913 us; the launch traced here: 907 us
  blocking collectives  540 us (59%)
  waiting for transfers between devices  228 us (25%)
  starting transfers between devices  90.4 us (10%)
  between operations  17.3 us (2%)
  other arithmetic  16 us (2%)
    psum x1, blocking collectives, shards(): loss_sum = lax.psum(cross_sum, ('group', 'tensor'))  166 us
    reduce_scatter x1, waiting for transfers between devices, shards(): lax.psum_scatter(jnp.dot(teacher_cols, teacher_proj, preferred_element_ty...  102 us
    reduce_scatter x1, waiting for transfers between devices, large_side(): lax.psum_scatter(jnp.dot(large_cols, proj_large, preferred_element_type=j...  99.1 us
    psum x2, blocking collectives, spread_stats(): lax.psum(jnp.sum(jnp.exp(values - row_top[:, None]), axis=-1), 'tensor')  94.8 us
    pmax x2, blocking collectives, spread_stats(): row_top = lax.pmax(local_top, 'tensor')  93.4 us
    psum x1, blocking collectives, shards(): grad_large, grad_huge = lax.psum((grad_large, grad_huge), 'group')  74.6 us
    all_to_all x1, starting transfers between devices, shards(): lax.all_to_all(packed, 'group', split_axis=0, concat_axis=0, tiled=True)  73.3 us
    all_gather x1, blocking collectives, large_side(): units = lax.all_gather(unit_rows(large_mid), 'tensor', axis=0, tiled=True)  48.2 us
  transfers between devices with their start and end apart: 4, of which 4 were waited for; matrix products, arithmetic and copies ran while one was open for 0% of the time, Pallas kernels for 0%

commit v1 on v0

v1 whole, which is shorter than its diff:
```python
import jax
import jax.numpy as jnp
from jax import lax
from jax.sharding import PartitionSpec as P

PATCH = 16
CG = 16
NEAR = 4


TEACHER_TEMP = 0.07
STUDENT_TEMP = 0.1
EPSILON = 1e-06


def layer_norm(values, gains):
    widened = values.astype(jnp.float32)
    row_mean = jnp.mean(widened, axis=-1, keepdims=True)
    centred = widened - row_mean
    spread = jnp.mean(centred * centred, axis=-1, keepdims=True)
    return (centred * lax.rsqrt(spread + EPSILON) * gains).astype(jnp.bfloat16)


def unit_rows(middle):
    return (middle * lax.rsqrt(jnp.mean(middle * middle, axis=-1, keepdims=True) + EPSILON)).astype(
        jnp.bfloat16
    )


def gather_copies(values, axis):
    copies = jnp.broadcast_to(values[None], (lax.axis_size(axis), *values.shape))
    return lax.all_to_all(copies, axis, split_axis=0, concat_axis=0, tiled=True)


def shards(
    teacher_feat,
    teacher_gain,
    teacher_proj,
    teacher_proto,
    center,
    routes,
    large_groups,
    feat_large,
    feat_huge,
    gain_large,
    gain_huge,
    proj_large,
    proj_huge,
    proto_large,
    proto_huge,
):
    groups = lax.axis_size("group")
    tensors = lax.axis_size("tensor")
    own_group = lax.axis_index("group")
    own_tensor = lax.axis_index("tensor")
    protos = teacher_proto.shape[1]
    width = teacher_proto.shape[0]
    slots_per = tensors // groups
    far = tensors // NEAR
    own_near = own_tensor % NEAR
    far_groups = [[near + NEAR * other for other in range(far)] for near in range(NEAR)]

    weights = jnp.concatenate([teacher_proj, proj_large, proj_huge], axis=0)
    held = [weights] + [
        lax.ppermute(weights, "tensor", [(t, t ^ step) for t in range(tensors)])
        for step in range(1, NEAR)
    ]
    held = jnp.stack(held)
    ordered = [
        lax.dynamic_index_in_dim(held, own_near ^ place, 0, keepdims=False) for place in range(NEAR)
    ]
    first, second = teacher_proj.shape[0], proj_large.shape[0]
    teacher_w = jnp.concatenate([block[:first] for block in ordered], axis=0)
    large_w = jnp.concatenate([block[first : first + second] for block in ordered], axis=0)
    huge_w = jnp.concatenate([block[first + second :] for block in ordered], axis=0)

    is_large = own_group < large_groups[0]
    wide = feat_huge.shape[1]
    padded_large = jnp.pad(feat_large, ((0, 0), (0, wide - feat_large.shape[1])))
    student_feat = jnp.where(is_large, padded_large, feat_huge)
    swap = [
        ((j * groups + s) * slots_per + k, (s * groups + j) * slots_per + k)
        for j in range(groups)
        for s in range(groups)
        for k in range(slots_per)
    ]
    student_feat = lax.ppermute(student_feat, ("group", "tensor"), swap)
    teacher_normed = layer_norm(teacher_feat, teacher_gain)
    row_large = own_tensor // slots_per < large_groups[0]
    slim = feat_large.shape[1]
    normed_large = layer_norm(student_feat[:, :slim], gain_large).reshape(-1, far, slim // far)
    normed_large = jnp.pad(normed_large, ((0, 0), (0, 0), (0, (wide - slim) // far)))
    normed_huge = layer_norm(student_feat, gain_huge).reshape(-1, far, wide // far)
    student_normed = jnp.where(row_large, normed_large, normed_huge)

    teacher_cols = lax.all_to_all(
        teacher_normed.reshape(-1, far, teacher_normed.shape[1] // far).transpose(1, 0, 2),
        "tensor",
        split_axis=0,
        concat_axis=0,
        tiled=True,
        axis_index_groups=far_groups,
    )
    student_cols = lax.all_to_all(
        student_normed.transpose(1, 0, 2),
        "tensor",
        split_axis=0,
        concat_axis=0,
        tiled=True,
        axis_index_groups=far_groups,
    )
    far_large = (
        (jnp.arange(far, dtype=jnp.int32) * NEAR + own_near) // slots_per < large_groups[0]
    )[:, None, None]
    zero = jnp.zeros((), jnp.bfloat16)
    part_teacher = jnp.einsum(
        "crf,fb->crb", teacher_cols, teacher_w, preferred_element_type=jnp.float32
    )
    part_student = jnp.einsum(
        "crf,fb->crb",
        jnp.where(far_large, student_cols[:, :, : large_w.shape[0]], zero),
        large_w,
        preferred_element_type=jnp.float32,
    ) + jnp.einsum(
        "crf,fb->crb",
        jnp.where(far_large, zero, student_cols),
        huge_w,
        preferred_element_type=jnp.float32,
    )
    parts = lax.all_to_all(
        jnp.concatenate([part_teacher, part_student], axis=1),
        "tensor",
        split_axis=0,
        concat_axis=0,
        tiled=True,
        axis_index_groups=far_groups,
    )
    units = gather_copies(unit_rows(jnp.sum(parts, axis=0)), "tensor")
    teacher_rows = teacher_feat.shape[0]
    teacher_units = units[:, :teacher_rows].reshape(-1, width)
    slot_units = units[:, teacher_rows:].reshape(-1, width)

    target_group = lax.dynamic_index_in_dim(
        routes[:, 0].reshape(-1, CG), own_group, 0, keepdims=False
    )
    earlier = jnp.arange(CG)[:, None] > jnp.arange(CG)[None, :]
    matching = target_group[:, None] == target_group[None, :]
    slot_rank = jnp.sum((matching & earlier).astype(jnp.int32), axis=1)
    crop_slot = target_group * slots_per + slot_rank
    row_slot = (crop_slot[:, None] * PATCH + jnp.arange(PATCH, dtype=jnp.int32)[None, :]).reshape(
        -1
    )
    crop_large = jnp.repeat(target_group < large_groups[0], PATCH)[:, None]
    chosen = (row_slot[:, None] == jnp.arange(slot_units.shape[0])[None, :]).astype(jnp.bfloat16)
    student_units = jnp.dot(chosen, slot_units, preferred_element_type=jnp.float32).astype(
        jnp.bfloat16
    )
    both_units = jnp.concatenate(
        [jnp.where(crop_large, student_units, zero), jnp.where(crop_large, zero, student_units)],
        axis=1,
    )
    both_protos = jnp.concatenate([proto_large, proto_huge], axis=0)
    shifted = (
        jnp.dot(teacher_units, teacher_proto, preferred_element_type=jnp.float32) - center[None, :]
    ) / TEACHER_TEMP
    scores = jnp.dot(both_units, both_protos, preferred_element_type=jnp.float32) / STUDENT_TEMP

    teacher_top = jnp.max(shifted, axis=1)
    teacher_exp = jnp.exp(shifted - teacher_top[:, None])
    student_top = jnp.max(scores, axis=1)
    student_exp = jnp.exp(scores - student_top[:, None])
    stats = jnp.stack(
        [
            teacher_top,
            jnp.sum(teacher_exp, axis=1),
            jnp.sum(teacher_exp * scores, axis=1),
            student_top,
            jnp.sum(student_exp, axis=1),
        ]
    )
    stats = gather_copies(stats, "tensor")
    top_t = jnp.max(stats[:, 0], axis=0)
    scale_t = jnp.exp(stats[:, 0] - top_t[None, :])
    total_t = jnp.sum(stats[:, 1] * scale_t, axis=0)
    crossed = jnp.sum(stats[:, 2] * scale_t, axis=0)
    top_s = jnp.max(stats[:, 3], axis=0)
    total_s = jnp.sum(stats[:, 4] * jnp.exp(stats[:, 3] - top_s[None, :]), axis=0)
    group_loss = jnp.sum(top_s + jnp.log(total_s) - crossed / total_t)
    target = (jnp.exp(shifted - top_t[:, None]) / total_t[:, None]).astype(jnp.bfloat16)
    student_prob = jnp.exp(scores - top_s[:, None]) / total_s[:, None]
    deltas = ((student_prob - target.astype(jnp.float32)) / STUDENT_TEMP).astype(jnp.bfloat16)
    grads = lax.dot_general(
        both_units, deltas, (((0,), (0,)), ((), ())), preferred_element_type=jnp.float32
    )

    high = group_loss.astype(jnp.bfloat16)
    rest = group_loss - high.astype(jnp.float32)
    middle = rest.astype(jnp.bfloat16)
    low = (rest - middle.astype(jnp.float32)).astype(jnp.bfloat16)
    lane = jnp.arange(128)
    note = jnp.where(lane == 0, high, jnp.where(lane == 1, middle, jnp.where(lane == 2, low, zero)))
    grad_rows = grads.shape[0] // groups
    sent = jnp.concatenate(
        [
            grads.astype(jnp.bfloat16).reshape(groups, grad_rows, protos),
            jnp.broadcast_to(note, (groups, grad_rows, 128)),
        ],
        axis=2,
    )
    taken = lax.all_to_all(sent, "group", split_axis=0, concat_axis=0, tiled=True)
    loss = (
        jnp.sum(taken[:, 0, protos : protos + 3].astype(jnp.float32)) / (routes.shape[0] * PATCH)
    ).reshape(1)
    summed = jnp.sum(taken[:, :, :protos].astype(jnp.float32), axis=0) / PATCH
    whole = gather_copies(summed.astype(jnp.bfloat16), "group").reshape(-1, protos)
    return (loss, whole[:width], whole[width:])


def solution(mesh):
    placed = (
        P(("group", "tensor"), None),
        P(),
        P("tensor", None),
        P(None, "tensor"),
        P("tensor"),
        P(),
        P(),
        P(("group", "tensor"), None),
        P(("group", "tensor"), None),
        P(),
        P(),
        P("tensor", None),
        P("tensor", None),
        P(None, "tensor"),
        P(None, "tensor"),
    )
    return jax.shard_map(
        shards,
        mesh=mesh,
        in_specs=placed,
        out_specs=(P(), P(None, "tensor"), P(None, "tensor")),
        check_vma=False,
    )
```

time: 913 us -> 205 us (0.22)
  blocking collectives: 540 us -> 69.9 us
  waiting for transfers between devices: 228 us -> 57.6 us
  starting transfers between devices: 90.4 us -> 51.6 us
  between operations: 17.3 us -> 4.74 us
    psum x4 -> x0, blocking collectives: 336 us -> none  [the longest x1 166 us: shards(): loss_sum = lax.psum(cross_sum, ('group', 'tensor'))]
    reduce_scatter x2 -> x0, waiting for transfers between devices: 201 us -> none  [the longest x1 102 us: shards(): lax.psum_scatter(jnp.dot(teacher_cols, teacher_proj, preferred_element_ty...]
    all_gather x2 -> x0, blocking collectives: 95.4 us -> none  [the longest x1 48.2 us: large_side(): units = lax.all_gather(unit_rows(large_mid), 'tensor', axis=0, tiled=True)]
    pmax x2 -> x0, blocking collectives: 93.4 us -> none  [spread_stats(): row_top = lax.pmax(local_top, 'tensor')]
    all_to_all x2 -> x4, starting transfers between devices: 90.3 us -> 33.1 us  [the longest x1 19.6 us: shards(): lax.all_to_all(student_normed.transpose(1, 0, 2), 'tensor', split_axis=0,...]
    all_to_all x1 -> x3, blocking collectives: 15.5 us -> 69.9 us  [the longest x1 30.2 us: shards(): lax.all_to_all(sent, 'group', split_axis=0, concat_axis=0, tiled=True)]
    all_to_all x2 -> x4, waiting for transfers between devices: 26.8 us -> 57.6 us  [the longest x2 33.3 us: gather_copies(): return lax.all_to_all(copies, axis, split_axis=0, concat_axis=0, tiled=True)]
    ppermute x0 -> x4, starting transfers between devices: none -> 18.5 us  [the longest x3 11.2 us: shards(): lax.ppermute(weights, 'tensor', [(t, t ^ step) for t in range(tensors)])]
  transfers between devices with their start and end apart: 4 -> 8, of which waited for: 4 -> 4; matrix products, arithmetic and copies ran while one was open for 0% -> 5% of each run, Pallas kernels for 0% -> 0%
where the time goes in v1:
time: 205 us; the launch traced here: 204 us
  blocking collectives  69.9 us (34%)
  waiting for transfers between devices  57.6 us (28%)
  starting transfers between devices  51.6 us (25%)
  other arithmetic  10.9 us (5%)
  local copies, waits for them, and re-layouts  6.61 us (3%)
  between operations  4.74 us (2%)
  matrix products  2.68 us (1%)
    all_to_all x2, waiting for transfers between devices, gather_copies(): return lax.all_to_all(copies, axis, split_axis=0, concat_axis=0, tiled=True)  33.3 us
    all_to_all x1, blocking collectives, shards(): lax.all_to_all(sent, 'group', split_axis=0, concat_axis=0, tiled=True)  30.2 us
    all_to_all x1, blocking collectives, gather_copies(): return lax.all_to_all(copies, axis, split_axis=0, concat_axis=0, tiled=True)  24.3 us
    all_to_all x1, starting transfers between devices, shards(): lax.all_to_all(student_normed.transpose(1, 0, 2), 'tensor', split_axis=0,...  19.6 us
    all_to_all x1, blocking collectives, shards(): lax.all_to_all(jnp.concatenate([part_teacher, part_student], axis=1), 'te...  15.4 us
    all_to_all x1, waiting for transfers between devices, shards(): lax.all_to_all(student_normed.transpose(1, 0, 2), 'tensor', split_axis=0,...  12.3 us
    all_to_all x1, waiting for transfers between devices, shards(): lax.all_to_all(teacher_normed.reshape(-1, far, teacher_normed.shape[1] //...  11.9 us
    ppermute x3, starting transfers between devices, shards(): lax.ppermute(weights, 'tensor', [(t, t ^ step) for t in range(tensors)])  11.2 us
  transfers between devices with their start and end apart: 8, of which 4 were waited for; matrix products, arithmetic and copies ran while one was open for 5% of the time, Pallas kernels for 0%

profile of v1, /device:TPU:1, one launch (start us, length us, event | category | flops | bytes accessed | tf_op | source)
XLA Modules:
  0.0 204.0 jit_solution(815117829640556147)
XLA Ops:
  0.6 0.9 constant_dynamic-update-slice_fusion.2
  1.5 0.7 constant_dynamic-update-slice_fusion.1
  2.3 0.7 constant_dynamic-update-slice_fusion
  3.0 7.1 %collective-permute-start.2 = (bf16[200,256]{1,0:T(8,128)(2,1)S(1)}, bf16[200,256]{1,0:T(8,128)(2,1)S(1)}, u32[]{:S(2)}, u32[]{:S(2)}) collective-permute-start(bf16[200,256]{1,0:T(8,128)(2,1)S(1)} %constant_dynamic-update-slice_fusion), channel_id=1, source_target_pairs={{0,3},{1,2},{2,1},{3,0},{4,7},{5,6},{6,5},{7,4},{8,11},{9,10},{10,... | collective-permute-start | bytes 307208 | tf_op jit(solution)/shard_map/ppermute | solution.py:65
  10.1 1.9 collective-permute-start.1
  12.0 2.2 %collective-permute-start = (bf16[200,256]{1,0:T(8,128)(2,1)S(1)}, bf16[200,256]{1,0:T(8,128)(2,1)S(1)}, u32[]{:S(2)}, u32[]{:S(2)}) collective-permute-start(bf16[200,256]{1,0:T(8,128)(2,1)S(1)} %constant_dynamic-update-slice_fusion), channel_id=1, source_target_pairs={{0,1},{1,0},{2,3},{3,2},{4,5},{5,4},{6,7},{7,6},{8,9},{9,8},{10,11... | collective-permute-start | bytes 307208 | tf_op jit(solution)/shard_map/ppermute | solution.py:65
  14.9 0.8 pad_select_fusion
  15.6 7.3 %collective-permute-start.3 = (bf16[16,1280]{1,0:T(8,128)(2,1)S(1)}, bf16[16,1280]{1,0:T(8,128)(2,1)S(1)}, u32[]{:S(2)}, u32[]{:S(2)}) collective-permute-start(bf16[16,1280]{1,0:T(8,128)(2,1)S(1)} %pad_select_fusion), channel_id=1, source_target_pairs={{0,0},{1,1},{2,32},{3,33},{4,64},{5,65},{6,96},{7,97},{8,128},{9,1... | collective-permute-start | bytes 122888 | tf_op jit(solution)/shard_map/ppermute | solution.py:87
  23.0 1.0 convert_reduce_fusion.1
  24.0 1.1 fusion.15
  25.0 1.6 fusion.17
  27.3 0.8 fusion.22
  28.3 0.8 copy_bitcast_fusion
  29.0 0.7 fusion.41
  29.7 19.6 %all-to-all-start.1 = ((bf16[8,16,160]{2,1,0:T(8,128)(2,1)}), bf16[8,16,160]{2,1,0:T(8,128)(2,1)S(1)}, u32[]{:S(2)}, u32[]{:S(2)}) async-start(bf16[8,16,160]{2,1,0:T(8,128)(2,1)} %fusion.41), calls=%async_computation.1 | async-start | bytes 131072 | tf_op jit(solution)/shard_map/all_to_all | solution.py:104
  49.5 12.3 %all-to-all-done.1 = bf16[8,16,160]{2,1,0:T(8,128)(2,1)S(1)} async-done(((bf16[8,16,160]{2,1,0:T(8,128)(2,1)}), bf16[8,16,160]{2,1,0:T(8,128)(2,1)S(1)}, u32[]{:S(2)}, u32[]{:S(2)}) %all-to-all-start.1) | async-done | bytes 40992 | tf_op jit(solution)/shard_map/all_to_all | solution.py:104
  61.8 3.4 %all-to-all-start = ((bf16[8,8,512]{2,1,0:T(8,128)(2,1)}), bf16[8,8,512]{2,1,0:T(8,128)(2,1)S(1)}, u32[]{:S(2)}, u32[]{:S(2)}) async-start(bf16[8,8,512]{2,1,0:T(8,128)(2,1)} %bitcast.3), calls=%async_computation | async-start | bytes 131072 | tf_op jit(solution)/shard_map/all_to_all | solution.py:96
  65.6 11.9 %all-to-all-done = bf16[8,8,512]{2,1,0:T(8,128)(2,1)S(1)} async-done(((bf16[8,8,512]{2,1,0:T(8,128)(2,1)}), bf16[8,8,512]{2,1,0:T(8,128)(2,1)S(1)}, u32[]{:S(2)}, u32[]{:S(2)}) %all-to-all-start) | async-done | bytes 65568 | tf_op jit(solution)/shard_map/all_to_all | solution.py:96
  77.7 15.4 %all_to_all.35 = f32[8,24,256]{2,1,0:T(8,128)S(1)} all-to-all(f32[8,24,256]{2,1,0:T(8,128)S(1)} %pad_maximum_fusion.3), channel_id=1, replica_groups={{0,4,8,12,16,20,24,28},{1,5,9,13,17,21,25,29},{2,6,10,14,18,22,26,30},{..., dimensions={0} | all-to-all | bytes 393216 | tf_op jit(solution)/shard_map/all_to_all | solution.py:130
  93.3 0.8 broadcast_in_dim.78
  94.1 6.0 %all-to-all-start.3 = ((bf16[32,24,256]{2,1,0:T(8,128)(2,1)}), bf16[32,24,256]{2,1,0:T(8,128)(2,1)S(1)}, u32[]{:S(2)}, u32[]{:S(2)}) async-start(bf16[32,24,256]{2,1,0:T(8,128)(2,1)} %broadcast_in_dim.78), calls=%async_computation.3 | async-start | bytes 786432 | tf_op jit(solution)/shard_map/all_to_all | solution.py:32
  100.7 0.7 reduce.6
  102.0 17.3 %all-to-all-done.3 = bf16[32,24,256]{2,1,0:T(8,128)(2,1)S(1)} async-done(((bf16[32,24,256]{2,1,0:T(8,128)(2,1)}), bf16[32,24,256]{2,1,0:T(8,128)(2,1)S(1)}, u32[]{:S(2)}, u32[]{:S(2)}) %all-to-all-start.3) | async-done | bytes 393248 | tf_op jit(solution)/shard_map/all_to_all | solution.py:32
  121.4 24.3 %all_to_all.36 = f32[32,5,256]{2,1,0:T(8,128)S(1)} all-to-all(f32[32,5,256]{2,1,0:T(8,128)S(1)} %broadcast_in_dim.121), channel_id=1, replica_groups=mesh['group'=16,'tensor'=32] {'tensor'}, dimensions={0} | all-to-all | bytes 327680 | tf_op jit(solution)/shard_map/all_to_all | solution.py:32
  145.9 0.8 convolution_convert_fusion
  146.7 0.6 subtract_reduce_fusion
  148.9 30.2 %all_to_all.37 = bf16[16,32,1152]{2,1,0:T(8,128)(2,1)S(1)} all-to-all(bf16[16,32,1152]{2,1,0:T(8,128)(2,1)S(1)} %pad_maximum_fusion), channel_id=1, replica_groups=mesh['group'=16,'tensor'=32] {'group'}, dimensions={0} | all-to-all | bytes 2359296 | tf_op jit(solution)/shard_map/all_to_all | solution.py:210
  179.3 1.1 broadcast_in_dim.127
  180.4 4.1 %all-to-all-start.6 = ((bf16[16,32,1024]{2,1,0:T(8,128)(2,1)}), bf16[16,32,1024]{2,1,0:T(8,128)(2,1)S(1)}, u32[]{:S(2)}, u32[]{:S(2)}) async-start(bf16[16,32,1024]{2,1,0:T(8,128)(2,1)} %broadcast_in_dim.127), calls=%async_computation.6 | async-start | bytes 2097152 | tf_op jit(solution)/shard_map/all_to_all | solution.py:32
  184.5 0.6 fusion.57
  185.8 16.0 %all-to-all-done.6 = bf16[16,32,1024]{2,1,0:T(8,128)(2,1)S(1)} async-done(((bf16[16,32,1024]{2,1,0:T(8,128)(2,1)}), bf16[16,32,1024]{2,1,0:T(8,128)(2,1)S(1)}, u32[]{:S(2)}, u32[]{:S(2)}) %all-to-all-start.6) | async-done | bytes 1048608 | tf_op jit(solution)/shard_map/all_to_all | solution.py:32
  201.8 1.1 fusion.70
  (65 shorter events, 5.6 us)
Async XLA Ops:
  0.6 119.6 %copy-start = (bf16[256,1024]{1,0:T(8,128)(2,1)S(1)}, bf16[256,1024]{1,0:T(8,128)(2,1)}, u32[]{:S(2)}) copy-start(bf16[256,1024]{1,0:T(8,128)(2,1)} %param.18) | copy-start | bytes 1572868
  3.0 46.3 %collective-permute-start.2 = (bf16[200,256]{1,0:T(8,128)(2,1)S(1)}, bf16[200,256]{1,0:T(8,128)(2,1)S(1)}, u32[]{:S(2)}, u32[]{:S(2)}) collective-permute-start(bf16[200,256]{1,0:T(8,128)(2,1)S(1)} %constant_dynamic-update-slice_fusion), channel_id=1, source_target_pairs={{0,3},{1,2},{2,1},{3,0},{4,7},{5,6},{6,5},{7,4},{8,11},{9,10},{10,... | collective-permute-start | bytes 307208 | tf_op jit(solution)/shard_map/ppermute | solution.py:65
  10.1 39.2 %collective-permute-start.1 = (bf16[200,256]{1,0:T(8,128)(2,1)S(1)}, bf16[200,256]{1,0:T(8,128)(2,1)S(1)}, u32[]{:S(2)}, u32[]{:S(2)}) collective-permute-start(bf16[200,256]{1,0:T(8,128)(2,1)S(1)} %constant_dynamic-update-slice_fusion), channel_id=1, source_target_pairs={{0,2},{1,3},{2,0},{3,1},{4,6},{5,7},{6,4},{7,5},{8,10},{9,11},{10,... | collective-permute-start | bytes 307208 | tf_op jit(solution)/shard_map/ppermute | solution.py:65
  12.0 37.3 %collective-permute-start = (bf16[200,256]{1,0:T(8,128)(2,1)S(1)}, bf16[200,256]{1,0:T(8,128)(2,1)S(1)}, u32[]{:S(2)}, u32[]{:S(2)}) collective-permute-start(bf16[200,256]{1,0:T(8,128)(2,1)S(1)} %constant_dynamic-update-slice_fusion), channel_id=1, source_target_pairs={{0,1},{1,0},{2,3},{3,2},{4,5},{5,4},{6,7},{7,6},{8,9},{9,8},{10,11... | collective-permute-start | bytes 307208 | tf_op jit(solution)/shard_map/ppermute | solution.py:65
  15.6 11.0 %collective-permute-start.3 = (bf16[16,1280]{1,0:T(8,128)(2,1)S(1)}, bf16[16,1280]{1,0:T(8,128)(2,1)S(1)}, u32[]{:S(2)}, u32[]{:S(2)}) collective-permute-start(bf16[16,1280]{1,0:T(8,128)(2,1)S(1)} %pad_select_fusion), channel_id=1, source_target_pairs={{0,0},{1,1},{2,32},{3,33},{4,64},{5,65},{6,96},{7,97},{8,128},{9,1... | collective-permute-start | bytes 122888 | tf_op jit(solution)/shard_map/ppermute | solution.py:87
  29.7 32.1 %all-to-all-start.1 = ((bf16[8,16,160]{2,1,0:T(8,128)(2,1)}), bf16[8,16,160]{2,1,0:T(8,128)(2,1)S(1)}, u32[]{:S(2)}, u32[]{:S(2)}) async-start(bf16[8,16,160]{2,1,0:T(8,128)(2,1)} %fusion.41), calls=%async_computation.1 | async-start | bytes 131072 | tf_op jit(solution)/shard_map/all_to_all | solution.py:104
  61.8 15.7 %all-to-all-start = ((bf16[8,8,512]{2,1,0:T(8,128)(2,1)}), bf16[8,8,512]{2,1,0:T(8,128)(2,1)S(1)}, u32[]{:S(2)}, u32[]{:S(2)}) async-start(bf16[8,8,512]{2,1,0:T(8,128)(2,1)} %bitcast.3), calls=%async_computation | async-start | bytes 131072 | tf_op jit(solution)/shard_map/all_to_all | solution.py:96
  77.7 23.0 %copy-start.4 = (s32[256,1]{0,1:T(1,128)S(1)}, s32[256,1]{0,1:T(1,128)}, u32[]{:S(2)}) copy-start(s32[256,1]{0,1:T(1,128)} %param.20) | copy-start | bytes 3076
  93.3 26.3 %copy-start.5 = (bf16[256,1024]{1,0:T(8,128)(2,1)S(1)}, bf16[256,1024]{1,0:T(8,128)(2,1)}, u32[]{:S(2)}) copy-start(bf16[256,1024]{1,0:T(8,128)(2,1)} %param.29) | copy-start | bytes 1572868
  93.3 26.3 %copy-start.6 = (bf16[256,1024]{1,0:T(8,128)(2,1)S(1)}, bf16[256,1024]{1,0:T(8,128)(2,1)}, u32[]{:S(2)}) copy-start(bf16[256,1024]{1,0:T(8,128)(2,1)} %param.28) | copy-start | bytes 1572868
  94.1 25.1 %all-to-all-start.3 = ((bf16[32,24,256]{2,1,0:T(8,128)(2,1)}), bf16[32,24,256]{2,1,0:T(8,128)(2,1)S(1)}, u32[]{:S(2)}, u32[]{:S(2)}) async-start(bf16[32,24,256]{2,1,0:T(8,128)(2,1)} %broadcast_in_dim.78), calls=%async_computation.3 | async-start | bytes 786432 | tf_op jit(solution)/shard_map/all_to_all | solution.py:32
  119.7 0.7 copy-start.3
  120.4 1.0 copy-start.1
  121.4 24.5 %copy-start.2 = (f32[256,1024]{1,0:T(8,128)S(1)}, f32[256,1024]{1,0:T(8,128)}, u32[]{:S(2)}) copy-start(f32[256,1024]{1,0:T(8,128)} %copy-done.1) | copy-start | bytes 3145732
  180.4 21.4 %all-to-all-start.6 = ((bf16[16,32,1024]{2,1,0:T(8,128)(2,1)}), bf16[16,32,1024]{2,1,0:T(8,128)(2,1)S(1)}, u32[]{:S(2)}, u32[]{:S(2)}) async-start(bf16[16,32,1024]{2,1,0:T(8,128)(2,1)} %broadcast_in_dim.127), calls=%async_computation.6 | async-start | bytes 2097152 | tf_op jit(solution)/shard_map/all_to_all | solution.py:32

commit v2 on v1

--- a/solution.py
+++ b/solution.py
@@ -30,6 +30,27 @@
 def gather_copies(values, axis):
     copies = jnp.broadcast_to(values[None], (lax.axis_size(axis), *values.shape))
     return lax.all_to_all(copies, axis, split_axis=0, concat_axis=0, tiled=True)
+
+
+def log_total(logs):
+    top = jnp.max(logs, axis=0)
+    return top + jnp.log(jnp.sum(jnp.exp(logs - top[None, :]), axis=0))
+
+
+def parts_of(value):
+    high = lax.reduce_precision(value, 8, 7)
+    middle = lax.reduce_precision(value - high, 8, 7)
+    low = lax.reduce_precision(value - high - middle, 8, 7)
+    lane = jnp.arange(128)
+    zero = jnp.zeros((), jnp.float32)
+    parts = jnp.where(lane == 0, high, jnp.where(lane == 1, middle, jnp.where(lane == 2, low, zero)))
+    return parts.astype(jnp.bfloat16)[None, :]
+
+
+def partial_grad(units, deltas):
+    return lax.dot_general(
+        units, deltas, (((0,), (0,)), ((), ())), preferred_element_type=jnp.float32
+    )
 
 
 def shards(
@@ -60,24 +81,11 @@
     own_near = own_tensor % NEAR
     far_groups = [[near + NEAR * other for other in range(far)] for near in range(NEAR)]
 
-    weights = jnp.concatenate([teacher_proj, proj_large, proj_huge], axis=0)
-    held = [weights] + [
-        lax.ppermute(weights, "tensor", [(t, t ^ step) for t in range(tensors)])
-        for step in range(1, NEAR)
-    ]
-    held = jnp.stack(held)
-    ordered = [
-        lax.dynamic_index_in_dim(held, own_near ^ place, 0, keepdims=False) for place in range(NEAR)
-    ]
-    first, second = teacher_proj.shape[0], proj_large.shape[0]
-    teacher_w = jnp.concatenate([block[:first] for block in ordered], axis=0)
-    large_w = jnp.concatenate([block[first : first + second] for block in ordered], axis=0)
-    huge_w = jnp.concatenate([block[first + second :] for block in ordered], axis=0)
-
     is_large = own_group < large_groups[0]
     wide = feat_huge.shape[1]
     padded_large = jnp.pad(feat_large, ((0, 0), (0, wide - feat_large.shape[1])))
     student_feat = jnp.where(is_large, padded_large, feat_huge)
+    student_feat, teacher_proj = lax.optimization_barrier((student_feat, teacher_proj))
     swap = [
         ((j * groups + s) * slots_per + k, (s * groups + j) * slots_per + k)
         for j in range(groups)
@@ -93,21 +101,42 @@
     normed_huge = layer_norm(student_feat, gain_huge).reshape(-1, far, wide // far)
     student_normed = jnp.where(row_large, normed_large, normed_huge)
 
-    teacher_cols = lax.all_to_all(
-        teacher_normed.reshape(-1, far, teacher_normed.shape[1] // far).transpose(1, 0, 2),
+    weights = jnp.concatenate([teacher_proj, proj_large, proj_huge], axis=0)
+    held = [weights] + [
+        lax.ppermute(weights, "tensor", [(t, t ^ step) for t in range(tensors)])
+        for step in range(1, NEAR)
+    ]
+    held = jnp.stack(held)
+    ordered = [
+        lax.dynamic_index_in_dim(held, own_near ^ place, 0, keepdims=False) for place in range(NEAR)
+    ]
+    first, second = teacher_proj.shape[0], proj_large.shape[0]
+    teacher_w = jnp.concatenate([block[:first] for block in ordered], axis=0)
+    large_w = jnp.concatenate([block[first : first + second] for block in ordered], axis=0)
+    huge_w = jnp.concatenate([block[first + second :] for block in ordered], axis=0)
+
+    teacher_rows = teacher_feat.shape[0]
+    piece = teacher_feat.shape[1] // far
+    slot_pad = piece // 2 - wide // far
+    teacher_sent = teacher_normed.reshape(teacher_rows, far, piece).transpose(1, 0, 2)
+    student_sent = jnp.pad(student_normed, ((0, 0), (0, 0), (0, slot_pad))).transpose(1, 0, 2)
+    half = student_sent.shape[1] // 2
+    student_sent = jnp.concatenate([student_sent[:, :half], student_sent[:, half:]], axis=2)
+    cols = lax.all_to_all(
+        jnp.concatenate([teacher_sent, student_sent], axis=1),
         "tensor",
         split_axis=0,
         concat_axis=0,
         tiled=True,
         axis_index_groups=far_groups,
     )
-    student_cols = lax.all_to_all(
-        student_normed.transpose(1, 0, 2),
-        "tensor",
-        split_axis=0,
-        concat_axis=0,
-        tiled=True,
-        axis_index_groups=far_groups,
+    teacher_cols = cols[:, :teacher_rows]
+    student_cols = jnp.concatenate(
+        [
+            cols[:, teacher_rows:, : wide // far],
+            cols[:, teacher_rows:, piece // 2 : piece // 2 + wide // far],
+        ],
+        axis=1,
     )
     far_large = (
         (jnp.arange(far, dtype=jnp.int32) * NEAR + own_near) // slots_per < large_groups[0]
@@ -136,7 +165,6 @@
         axis_index_groups=far_groups,
     )
     units = gather_copies(unit_rows(jnp.sum(parts, axis=0)), "tensor")
-    teacher_rows = teacher_feat.shape[0]
     teacher_units = units[:, :teacher_rows].reshape(-1, width)
     slot_units = units[:, teacher_rows:].reshape(-1, width)
 
@@ -167,53 +195,68 @@
 
     teacher_top = jnp.max(shifted, axis=1)
     teacher_exp = jnp.exp(shifted - teacher_top[:, None])
+    teacher_sum = jnp.sum(teacher_exp, axis=1)
     student_top = jnp.max(scores, axis=1)
-    student_exp = jnp.exp(scores - student_top[:, None])
+    student_sum = jnp.sum(jnp.exp(scores - student_top[:, None]), axis=1)
     stats = jnp.stack(
         [
-            teacher_top,
-            jnp.sum(teacher_exp, axis=1),
-            jnp.sum(teacher_exp * scores, axis=1),
-            student_top,
-            jnp.sum(student_exp, axis=1),
+            teacher_top + jnp.log(teacher_sum),
+            jnp.sum(teacher_exp * scores, axis=1) / teacher_sum,
+            student_top + jnp.log(student_sum),
         ]
     )
-    stats = gather_copies(stats, "tensor")
-    top_t = jnp.max(stats[:, 0], axis=0)
-    scale_t = jnp.exp(stats[:, 0] - top_t[None, :])
-    total_t = jnp.sum(stats[:, 1] * scale_t, axis=0)
-    crossed = jnp.sum(stats[:, 2] * scale_t, axis=0)
-    top_s = jnp.max(stats[:, 3], axis=0)
-    total_s = jnp.sum(stats[:, 4] * jnp.exp(stats[:, 3] - top_s[None, :]), axis=0)
-    group_loss = jnp.sum(top_s + jnp.log(total_s) - crossed / total_t)
-    target = (jnp.exp(shifted - top_t[:, None]) / total_t[:, None]).astype(jnp.bfloat16)
-    student_prob = jnp.exp(scores - top_s[:, None]) / total_s[:, None]
-    deltas = ((student_prob - target.astype(jnp.float32)) / STUDENT_TEMP).astype(jnp.bfloat16)
-    grads = lax.dot_general(
-        both_units, deltas, (((0,), (0,)), ((), ())), preferred_element_type=jnp.float32
-    )
-
-    high = group_loss.astype(jnp.bfloat16)
-    rest = group_loss - high.astype(jnp.float32)
-    middle = rest.astype(jnp.bfloat16)
-    low = (rest - middle.astype(jnp.float32)).astype(jnp.bfloat16)
-    lane = jnp.arange(128)
-    note = jnp.where(lane == 0, high, jnp.where(lane == 1, middle, jnp.where(lane == 2, low, zero)))
-    grad_rows = grads.shape[0] // groups
+    stats = gather_copies(stats.reshape(-1, 128), "tensor").reshape(tensors, 3, -1)
+    log_t = log_total(stats[:, 0])
+    crossed = jnp.sum(stats[:, 1] * jnp.exp(stats[:, 0] - log_t[None, :]), axis=0)
+    log_s = log_total(stats[:, 2])
+    group_loss = jnp.sum(log_s - crossed)
+    target = lax.reduce_precision(jnp.exp(shifted - log_t[:, None]), 8, 7)
+    student_prob = jnp.exp(scores - log_s[:, None])
+    deltas = ((student_prob - target) / STUDENT_TEMP).astype(jnp.bfloat16)
+
+    own_core = own_group % 2
+    kept_rows = crop_large == (own_core == 0)
+    gives = partial_grad(jnp.where(kept_rows, zero, student_units), deltas)
+    keeps = partial_grad(jnp.where(kept_rows, student_units, zero), deltas)
+    pairs = [(g, g ^ 1) for g in range(groups)]
+    got = lax.ppermute(
+        jnp.concatenate(
+            [gives.astype(jnp.bfloat16), jnp.broadcast_to(parts_of(group_loss), (width, 128))],
+            axis=1,
+        ),
+        "group",
+        pairs,
+    )
+    chip_grad = keeps + got[:, :protos].astype(jnp.float32)
+    chip_loss = group_loss + jnp.sum(got[0, protos:].astype(jnp.float32))
+    chips = groups // 2
+    grad_rows = width // chips
     sent = jnp.concatenate(
-        [
-            grads.astype(jnp.bfloat16).reshape(groups, grad_rows, protos),
-            jnp.broadcast_to(note, (groups, grad_rows, 128)),
-        ],
-        axis=2,
-    )
-    taken = lax.all_to_all(sent, "group", split_axis=0, concat_axis=0, tiled=True)
+        [chip_grad.astype(jnp.bfloat16), jnp.broadcast_to(parts_of(chip_loss), (width, 128))],
+        axis=1,
+    ).reshape(chips, grad_rows, protos + 128)
+    same_core = [[core + 2 * chip for chip in range(chips)] for core in range(2)]
+    taken = lax.all_to_all(
+        sent, "group", split_axis=0, concat_axis=0, tiled=True, axis_index_groups=same_core
+    )
     loss = (
-        jnp.sum(taken[:, 0, protos : protos + 3].astype(jnp.float32)) / (routes.shape[0] * PATCH)
+        jnp.sum(taken[:, 0, protos:].astype(jnp.float32)) / (routes.shape[0] * PATCH)
     ).reshape(1)
     summed = jnp.sum(taken[:, :, :protos].astype(jnp.float32), axis=0) / PATCH
-    whole = gather_copies(summed.astype(jnp.bfloat16), "group").reshape(-1, protos)
-    return (loss, whole[:width], whole[width:])
+    mine = lax.all_to_all(
+        jnp.broadcast_to(summed.astype(jnp.bfloat16)[None], (chips, grad_rows, protos)),
+        "group",
+        split_axis=0,
+        concat_axis=0,
+        tiled=True,
+        axis_index_groups=same_core,
+    ).reshape(width, protos)
+    other = lax.ppermute(mine, "group", pairs)
+    return (
+        loss,
+        jnp.where(own_core == 0, mine, other),
+        jnp.where(own_core == 0, other, mine),
+    )
 
 
 def solution(mesh):

time: 205 us -> 195 us (0.951)
  blocking collectives: 69.9 us -> 44.1 us
  starting transfers between devices: 51.6 us -> 63.4 us
  waiting for transfers between devices: 57.6 us -> 50.4 us
  between operations: 4.74 us -> 11.9 us
  other arithmetic: 10.9 us -> 15.5 us
    all_to_all x2, blocking collectives: 54.5 us -> 27.5 us  [the longest x1 15 us: shards(): lax.all_to_all(sent, 'group', split_axis=0, concat_axis=0, tiled=True, ax...]
    all_to_all x2 -> x1, waiting for transfers between devices: 24.3 us -> 12.8 us  [shards(): lax.all_to_all(jnp.concatenate([teacher_sent, student_sent], axis=1), 'te...]
    ppermute x0 -> x2, starting transfers between devices: none -> 11.2 us  [the longest x1 6.5 us: shards(): lax.ppermute(jnp.concatenate([gives.astype(jnp.bfloat16), jnp.broadcast_t...]
    convert_element_type x1 -> x4, other arithmetic: 0.01 us -> 4.33 us  [the longest x2 3.93 us: parts_of(): return parts.astype(jnp.bfloat16)[None, :]]
    all_to_all x2, starting transfers between devices: 10.1 us -> 13.4 us  [gather_copies(): return lax.all_to_all(copies, axis, split_axis=0, concat_axis=0, tiled=True)]
    all_to_all x2 -> x1, starting transfers between devices: 22.9 us -> 20.2 us  [shards(): lax.all_to_all(jnp.concatenate([teacher_sent, student_sent], axis=1), 'te...]
    all_to_all x2, waiting for transfers between devices: 33.3 us -> 35.8 us  [gather_copies(): return lax.all_to_all(copies, axis, split_axis=0, concat_axis=0, tiled=True)]
  transfers between devices with their start and end apart: 8 -> 9, of which waited for: 4 -> 5; matrix products, arithmetic and copies ran while one was open for 5% -> 4% of each run, Pallas kernels for 0% -> 0%
where the time goes in v2:
time: 195 us; the launch traced here: 194 us
  starting transfers between devices  63.4 us (33%)
  waiting for transfers between devices  50.4 us (26%)
  blocking collectives  44.1 us (23%)
  other arithmetic  15.5 us (8%)
  between operations  11.9 us (6%)
  local copies, waits for them, and re-layouts  4.99 us (3%)
  matrix products  3.55 us (2%)
    all_to_all x2, waiting for transfers between devices, gather_copies(): return lax.all_to_all(copies, axis, split_axis=0, concat_axis=0, tiled=True)  35.8 us
    all_to_all x1, starting transfers between devices, shards(): lax.all_to_all(jnp.concatenate([teacher_sent, student_sent], axis=1), 'te...  20.2 us
    all_to_all x1, blocking collectives, shards(): lax.all_to_all(jnp.concatenate([part_teacher, part_student], axis=1), 'te...  16.6 us
    all_to_all x1, blocking collectives, shards(): lax.all_to_all(sent, 'group', split_axis=0, concat_axis=0, tiled=True, ax...  15 us
    all_to_all x2, starting transfers between devices, gather_copies(): return lax.all_to_all(copies, axis, split_axis=0, concat_axis=0, tiled=True)  13.4 us
    all_to_all x1, waiting for transfers between devices, shards(): lax.all_to_all(jnp.concatenate([teacher_sent, student_sent], axis=1), 'te...  12.8 us
    all_to_all x1, blocking collectives, shards(): lax.all_to_all(jnp.broadcast_to(summed.astype(jnp.bfloat16)[None], (chips...  12.5 us
    ppermute x3, starting transfers between devices, shards(): lax.ppermute(weights, 'tensor', [(t, t ^ step) for t in range(tensors)])  11.2 us
  transfers between devices with their start and end apart: 9, of which 5 were waited for; matrix products, arithmetic and copies ran while one was open for 4% of the time, Pallas kernels for 0%

profile of v2, /device:TPU:1, one launch (start us, length us, event | category | flops | bytes accessed | tf_op | source)
XLA Modules:
  0.0 193.9 jit_solution(18088862874051994906)
XLA Ops:
  1.4 0.8 pad_select_fusion
  2.2 0.8 constant_dynamic-update-slice_fusion.2
  3.0 0.7 constant_dynamic-update-slice_fusion.1
  3.7 0.7 constant_dynamic-update-slice_fusion
  4.5 7.1 %collective-permute-start.3 = (bf16[200,256]{1,0:T(8,128)(2,1)S(1)}, bf16[200,256]{1,0:T(8,128)(2,1)S(1)}, u32[]{:S(2)}, u32[]{:S(2)}) collective-permute-start(bf16[200,256]{1,0:T(8,128)(2,1)S(1)} %constant_dynamic-update-slice_fusion), channel_id=1, source_target_pairs={{0,3},{1,2},{2,1},{3,0},{4,7},{5,6},{6,5},{7,4},{8,11},{9,10},{10,... | collective-permute-start | bytes 307208 | tf_op jit(solution)/shard_map/ppermute | solution.py:106
  11.5 1.9 collective-permute-start.2
  13.5 2.2 %collective-permute-start.1 = (bf16[200,256]{1,0:T(8,128)(2,1)S(1)}, bf16[200,256]{1,0:T(8,128)(2,1)S(1)}, u32[]{:S(2)}, u32[]{:S(2)}) collective-permute-start(bf16[200,256]{1,0:T(8,128)(2,1)S(1)} %constant_dynamic-update-slice_fusion), channel_id=1, source_target_pairs={{0,1},{1,0},{2,3},{3,2},{4,5},{5,4},{6,7},{7,6},{8,9},{9,8},{10,11... | collective-permute-start | bytes 307208 | tf_op jit(solution)/shard_map/ppermute | solution.py:106
  15.7 7.3 %collective-permute-start = (bf16[16,1280]{1,0:T(8,128)(2,1)S(1)}, bf16[16,1280]{1,0:T(8,128)(2,1)S(1)}, u32[]{:S(2)}, u32[]{:S(2)}) collective-permute-start(bf16[16,1280]{1,0:T(8,128)(2,1)S(1)} %pad_select_fusion), channel_id=1, source_target_pairs={{0,0},{1,1},{2,32},{3,33},{4,64},{5,65},{6,96},{7,97},{8,128},{9,1... | collective-permute-start | bytes 122888 | tf_op jit(solution)/shard_map/ppermute | solution.py:95
  23.0 1.0 convert_reduce_fusion.1
  24.0 1.1 fusion.18
  25.1 0.9 fusion.20
  26.7 0.8 fusion.32
  27.8 0.7 maximum_maximum_fusion
  28.5 20.2 %all-to-all-start = ((bf16[8,16,512]{2,1,0:T(8,128)(2,1)}), bf16[8,16,512]{2,1,0:T(8,128)(2,1)S(1)}, u32[]{:S(2)}, u32[]{:S(2)}) async-start(bf16[8,16,512]{2,1,0:T(8,128)(2,1)} %maximum_maximum_fusion), calls=%async_computation | async-start | bytes 262144 | tf_op jit(solution)/shard_map/all_to_all | solution.py:125
  48.9 12.8 %all-to-all-done = bf16[8,16,512]{2,1,0:T(8,128)(2,1)S(1)} async-done(((bf16[8,16,512]{2,1,0:T(8,128)(2,1)}), bf16[8,16,512]{2,1,0:T(8,128)(2,1)S(1)}, u32[]{:S(2)}, u32[]{:S(2)}) %all-to-all-start) | async-done | bytes 131104 | tf_op jit(solution)/shard_map/all_to_all | solution.py:125
  62.3 16.6 %all_to_all.30 = f32[8,24,256]{2,1,0:T(8,128)S(1)} all-to-all(f32[8,24,256]{2,1,0:T(8,128)S(1)} %pad_maximum_fusion.3), channel_id=1, replica_groups={{0,4,8,12,16,20,24,28},{1,5,9,13,17,21,25,29},{2,6,10,14,18,22,26,30},{..., dimensions={0} | all-to-all | bytes 393216 | tf_op jit(solution)/shard_map/all_to_all | solution.py:159
  79.2 0.8 broadcast_in_dim.145
  80.0 8.0 %all-to-all-start.2 = ((bf16[32,24,256]{2,1,0:T(8,128)(2,1)}), bf16[32,24,256]{2,1,0:T(8,128)(2,1)S(1)}, u32[]{:S(2)}, u32[]{:S(2)}) async-start(bf16[32,24,256]{2,1,0:T(8,128)(2,1)} %broadcast_in_dim.145), calls=%async_computation.2 | async-start | bytes 786432 | tf_op jit(solution)/shard_map/all_to_all | solution.py:32
  88.5 0.7 reduce.7
  89.8 21.4 %all-to-all-done.2 = bf16[32,24,256]{2,1,0:T(8,128)(2,1)S(1)} async-done(((bf16[32,24,256]{2,1,0:T(8,128)(2,1)}), bf16[32,24,256]{2,1,0:T(8,128)(2,1)S(1)}, u32[]{:S(2)}, u32[]{:S(2)}) %all-to-all-start.2) | async-done | bytes 393248 | tf_op jit(solution)/shard_map/all_to_all | solution.py:32
  111.6 1.6 fusion.85
  114.2 0.7 broadcast_in_dim.149
  114.9 5.4 %all-to-all-start.3 = ((f32[32,6,128]{2,1,0:T(8,128)}), f32[32,6,128]{2,1,0:T(8,128)S(1)}, u32[]{:S(2)}, u32[]{:S(2)}) async-start(f32[32,6,128]{2,1,0:T(8,128)} %broadcast_in_dim.149), calls=%async_computation.3 | async-start | bytes 262144 | tf_op jit(solution)/shard_map/all_to_all | solution.py:32
  120.3 14.4 %all-to-all-done.3 = f32[32,6,128]{2,1,0:T(8,128)S(1)} async-done(((f32[32,6,128]{2,1,0:T(8,128)}), f32[32,6,128]{2,1,0:T(8,128)S(1)}, u32[]{:S(2)}, u32[]{:S(2)}) %all-to-all-start.3) | async-done | bytes 98336 | tf_op jit(solution)/shard_map/all_to_all | solution.py:32
  139.7 2.0 %fusion.69 = bf16[128]{0:T(256)(128)(2,1)S(1)} fusion(bf16[]{:T(256)} %reduce_precision.24, f32[]{:T(128)} %reduce_precision.23, f32[]{:T(128)} %reduce_precision.22), kind=kLoop, calls=%fused_computation.147 | loop fusion | flops 768 | bytes 266 | tf_op jit(solution)/shard_map/convert_element_type | solution.py:47
  142.6 6.5 %collective-permute-start.4 = (bf16[256,1152]{1,0:T(8,128)(2,1)S(1)}, bf16[256,1152]{1,0:T(8,128)(2,1)S(1)}, u32[]{:S(2)}, u32[]{:S(2)}) collective-permute-start(bf16[256,1152]{1,0:T(8,128)(2,1)S(1)} %pad_maximum_fusion), channel_id=1, source_target_pairs={{0,32},{32,0},{64,96},{96,64},{128,160},{160,128},{192,224},{224,1... | collective-permute-start | bytes 1769480 | tf_op jit(solution)/shard_map/ppermute | solution.py:222
  149.1 1.6 collective-permute-done.4
  155.4 1.9 %fusion.70 = bf16[128]{0:T(256)(128)(2,1)S(1)} fusion(bf16[]{:T(256)} %reduce_precision.27, f32[]{:T(128)} %reduce_precision.26, f32[]{:T(128)} %reduce_precision.25), kind=kLoop, calls=%fused_computation.148 | loop fusion | flops 768 | bytes 266 | tf_op jit(solution)/shard_map/convert_element_type | solution.py:47
  157.8 15.0 %all_to_all.31 = bf16[8,32,1152]{2,1,0:T(8,128)(2,1)S(1)} all-to-all(bf16[8,32,1152]{2,1,0:T(8,128)(2,1)S(1)} %bitcast.90), channel_id=1, replica_groups={{0,64,128,192,256,320,384,448},{32,96,160,224,288,352,416,480},{1,65,12..., dimensions={0} | all-to-all | bytes 1179648 | tf_op jit(solution)/shard_map/all_to_all | solution.py:239
  172.9 12.5 %all_to_all.32 = bf16[8,32,1024]{2,1,0:T(8,128)(2,1)S(1)} all-to-all(bf16[8,32,1024]{2,1,0:T(8,128)(2,1)S(1)} %broadcast_in_dim.159), channel_id=1, replica_groups={{0,64,128,192,256,320,384,448},{32,96,160,224,288,352,416,480},{1,65,12..., dimensions={0} | all-to-all | bytes 1048576 | tf_op jit(solution)/shard_map/all_to_all | solution.py:246
  185.4 4.7 %collective-permute-start.5 = (bf16[256,1024]{1,0:T(8,128)(2,1)S(1)}, bf16[256,1024]{1,0:T(8,128)(2,1)S(1)}, u32[]{:S(2)}, u32[]{:S(2)}) collective-permute-start(bf16[256,1024]{1,0:T(8,128)(2,1)S(1)} %bitcast.91), channel_id=1, source_target_pairs={{0,32},{32,0},{64,96},{96,64},{128,160},{160,128},{192,224},{224,1... | collective-permute-start | bytes 1572872 | tf_op jit(solution)/shard_map/ppermute | solution.py:254
  191.7 1.1 broadcast_select_fusion
  (80 shorter events, 8.1 us)
Async XLA Ops:
  0.6 112.6 %copy-start = (bf16[256,1024]{1,0:T(8,128)(2,1)S(1)}, bf16[256,1024]{1,0:T(8,128)(2,1)}, u32[]{:S(2)}) copy-start(bf16[256,1024]{1,0:T(8,128)(2,1)} %param.18) | copy-start | bytes 1572868
  0.6 27.0 %copy-start.2 = (f32[1024]{0:T(1024)S(1)}, f32[1024]{0:T(1024)}, u32[]{:S(2)}) copy-start(f32[1024]{0:T(1024)} %param.24) | copy-start | bytes 12292
  4.5 44.3 %collective-permute-start.3 = (bf16[200,256]{1,0:T(8,128)(2,1)S(1)}, bf16[200,256]{1,0:T(8,128)(2,1)S(1)}, u32[]{:S(2)}, u32[]{:S(2)}) collective-permute-start(bf16[200,256]{1,0:T(8,128)(2,1)S(1)} %constant_dynamic-update-slice_fusion), channel_id=1, source_target_pairs={{0,3},{1,2},{2,1},{3,0},{4,7},{5,6},{6,5},{7,4},{8,11},{9,10},{10,... | collective-permute-start | bytes 307208 | tf_op jit(solution)/shard_map/ppermute | solution.py:106
  11.5 37.2 %collective-permute-start.2 = (bf16[200,256]{1,0:T(8,128)(2,1)S(1)}, bf16[200,256]{1,0:T(8,128)(2,1)S(1)}, u32[]{:S(2)}, u32[]{:S(2)}) collective-permute-start(bf16[200,256]{1,0:T(8,128)(2,1)S(1)} %constant_dynamic-update-slice_fusion), channel_id=1, source_target_pairs={{0,2},{1,3},{2,0},{3,1},{4,6},{5,7},{6,4},{7,5},{8,10},{9,11},{10,... | collective-permute-start | bytes 307208 | tf_op jit(solution)/shard_map/ppermute | solution.py:106
  13.5 35.3 %collective-permute-start.1 = (bf16[200,256]{1,0:T(8,128)(2,1)S(1)}, bf16[200,256]{1,0:T(8,128)(2,1)S(1)}, u32[]{:S(2)}, u32[]{:S(2)}) collective-permute-start(bf16[200,256]{1,0:T(8,128)(2,1)S(1)} %constant_dynamic-update-slice_fusion), channel_id=1, source_target_pairs={{0,1},{1,0},{2,3},{3,2},{4,5},{5,4},{6,7},{7,6},{8,9},{9,8},{10,11... | collective-permute-start | bytes 307208 | tf_op jit(solution)/shard_map/ppermute | solution.py:106
  15.7 10.4 %collective-permute-start = (bf16[16,1280]{1,0:T(8,128)(2,1)S(1)}, bf16[16,1280]{1,0:T(8,128)(2,1)S(1)}, u32[]{:S(2)}, u32[]{:S(2)}) collective-permute-start(bf16[16,1280]{1,0:T(8,128)(2,1)S(1)} %pad_select_fusion), channel_id=1, source_target_pairs={{0,0},{1,1},{2,32},{3,33},{4,64},{5,65},{6,96},{7,97},{8,128},{9,1... | collective-permute-start | bytes 122888 | tf_op jit(solution)/shard_map/ppermute | solution.py:95
  28.5 33.2 %all-to-all-start = ((bf16[8,16,512]{2,1,0:T(8,128)(2,1)}), bf16[8,16,512]{2,1,0:T(8,128)(2,1)S(1)}, u32[]{:S(2)}, u32[]{:S(2)}) async-start(bf16[8,16,512]{2,1,0:T(8,128)(2,1)} %maximum_maximum_fusion), calls=%async_computation | async-start | bytes 262144 | tf_op jit(solution)/shard_map/all_to_all | solution.py:125
  62.3 26.2 %copy-start.3 = (s32[256,1]{0,1:T(1,128)S(1)}, s32[256,1]{0,1:T(1,128)}, u32[]{:S(2)}) copy-start(s32[256,1]{0,1:T(1,128)} %param.20) | copy-start | bytes 3076
  80.0 31.6 %copy-start.4 = (bf16[256,1024]{1,0:T(8,128)(2,1)S(1)}, bf16[256,1024]{1,0:T(8,128)(2,1)}, u32[]{:S(2)}) copy-start(bf16[256,1024]{1,0:T(8,128)(2,1)} %param.29) | copy-start | bytes 1572868
  80.0 31.2 %all-to-all-start.2 = ((bf16[32,24,256]{2,1,0:T(8,128)(2,1)}), bf16[32,24,256]{2,1,0:T(8,128)(2,1)S(1)}, u32[]{:S(2)}, u32[]{:S(2)}) async-start(bf16[32,24,256]{2,1,0:T(8,128)(2,1)} %broadcast_in_dim.145), calls=%async_computation.2 | async-start | bytes 786432 | tf_op jit(solution)/shard_map/all_to_all | solution.py:32
  111.6 1.6 copy-start.1
  114.9 19.8 %all-to-all-start.3 = ((f32[32,6,128]{2,1,0:T(8,128)}), f32[32,6,128]{2,1,0:T(8,128)S(1)}, u32[]{:S(2)}, u32[]{:S(2)}) async-start(f32[32,6,128]{2,1,0:T(8,128)} %broadcast_in_dim.149), calls=%async_computation.3 | async-start | bytes 262144 | tf_op jit(solution)/shard_map/all_to_all | solution.py:32
  142.6 8.1 %collective-permute-start.4 = (bf16[256,1152]{1,0:T(8,128)(2,1)S(1)}, bf16[256,1152]{1,0:T(8,128)(2,1)S(1)}, u32[]{:S(2)}, u32[]{:S(2)}) collective-permute-start(bf16[256,1152]{1,0:T(8,128)(2,1)S(1)} %pad_maximum_fusion), channel_id=1, source_target_pairs={{0,32},{32,0},{64,96},{96,64},{128,160},{160,128},{192,224},{224,1... | collective-permute-start | bytes 1769480 | tf_op jit(solution)/shard_map/ppermute | solution.py:222
  185.4 6.3 %collective-permute-start.5 = (bf16[256,1024]{1,0:T(8,128)(2,1)S(1)}, bf16[256,1024]{1,0:T(8,128)(2,1)S(1)}, u32[]{:S(2)}, u32[]{:S(2)}) collective-permute-start(bf16[256,1024]{1,0:T(8,128)(2,1)S(1)} %bitcast.91), channel_id=1, source_target_pairs={{0,32},{32,0},{64,96},{96,64},{128,160},{160,128},{192,224},{224,1... | collective-permute-start | bytes 1572872 | tf_op jit(solution)/shard_map/ppermute | solution.py:254

commit v3 on v2

--- a/solution.py
+++ b/solution.py
@@ -37,14 +37,21 @@
     return top + jnp.log(jnp.sum(jnp.exp(logs - top[None, :]), axis=0))
 
 
-def parts_of(value):
-    high = lax.reduce_precision(value, 8, 7)
-    middle = lax.reduce_precision(value - high, 8, 7)
-    low = lax.reduce_precision(value - high - middle, 8, 7)
-    lane = jnp.arange(128)
-    zero = jnp.zeros((), jnp.float32)
-    parts = jnp.where(lane == 0, high, jnp.where(lane == 1, middle, jnp.where(lane == 2, low, zero)))
-    return parts.astype(jnp.bfloat16)[None, :]
+def parts_of(values):
+    high = lax.reduce_precision(values, 8, 7)
+    middle = lax.reduce_precision(values - high, 8, 7)
+    low = lax.reduce_precision(values - high - middle, 8, 7)
+    return jnp.stack([high, middle, low]).astype(jnp.bfloat16)
+
+
+def crop_rows(routes, group, large, slots_per):
+    target_group = lax.dynamic_index_in_dim(routes[:, 0].reshape(-1, CG), group, 0, keepdims=False)
+    earlier = jnp.arange(CG)[:, None] > jnp.arange(CG)[None, :]
+    matching = target_group[:, None] == target_group[None, :]
+    slot_rank = jnp.sum((matching & earlier).astype(jnp.int32), axis=1)
+    first_row = (target_group * slots_per + slot_rank) * PATCH
+    row_slot = (first_row[:, None] + jnp.arange(PATCH, dtype=jnp.int32)[None, :]).reshape(-1)
+    return (row_slot, jnp.repeat(target_group < large, PATCH)[:, None])
 
 
 def partial_grad(units, deltas):
@@ -85,7 +92,6 @@
     wide = feat_huge.shape[1]
     padded_large = jnp.pad(feat_large, ((0, 0), (0, wide - feat_large.shape[1])))
     student_feat = jnp.where(is_large, padded_large, feat_huge)
-    student_feat, teacher_proj = lax.optimization_barrier((student_feat, teacher_proj))
     swap = [
         ((j * groups + s) * slots_per + k, (s * groups + j) * slots_per + k)
         for j in range(groups)
@@ -94,6 +100,7 @@
     ]
     student_feat = lax.ppermute(student_feat, ("group", "tensor"), swap)
     teacher_normed = layer_norm(teacher_feat, teacher_gain)
+    teacher_normed, teacher_proj = lax.optimization_barrier((teacher_normed, teacher_proj))
     row_large = own_tensor // slots_per < large_groups[0]
     slim = feat_large.shape[1]
     normed_large = layer_norm(student_feat[:, :slim], gain_large).reshape(-1, far, slim // far)
@@ -106,15 +113,6 @@
         lax.ppermute(weights, "tensor", [(t, t ^ step) for t in range(tensors)])
         for step in range(1, NEAR)
     ]
-    held = jnp.stack(held)
-    ordered = [
-        lax.dynamic_index_in_dim(held, own_near ^ place, 0, keepdims=False) for place in range(NEAR)
-    ]
-    first, second = teacher_proj.shape[0], proj_large.shape[0]
-    teacher_w = jnp.concatenate([block[:first] for block in ordered], axis=0)
-    large_w = jnp.concatenate([block[first : first + second] for block in ordered], axis=0)
-    huge_w = jnp.concatenate([block[first + second :] for block in ordered], axis=0)
-
     teacher_rows = teacher_feat.shape[0]
     piece = teacher_feat.shape[1] // far
     slot_pad = piece // 2 - wide // far
@@ -130,6 +128,15 @@
         tiled=True,
         axis_index_groups=far_groups,
     )
+    cols, held = lax.optimization_barrier((cols, held))
+    held = jnp.stack(held)
+    ordered = [
+        lax.dynamic_index_in_dim(held, own_near ^ place, 0, keepdims=False) for place in range(NEAR)
+    ]
+    first, second = teacher_proj.shape[0], proj_large.shape[0]
+    teacher_w = jnp.concatenate([block[:first] for block in ordered], axis=0)
+    large_w = jnp.concatenate([block[first : first + second] for block in ordered], axis=0)
+    huge_w = jnp.concatenate([block[first + second :] for block in ordered], axis=0)
     teacher_cols = cols[:, :teacher_rows]
     student_cols = jnp.concatenate(
         [
@@ -156,6 +163,15 @@
         huge_w,
         preferred_element_type=jnp.float32,
     )
+    own_core = own_group % 2
+    row_slot, crop_large = crop_rows(routes, own_group, large_groups[0], slots_per)
+    _, other_large = crop_rows(routes, own_group ^ 1, large_groups[0], slots_per)
+    chosen = (
+        row_slot[:, None] == jnp.arange(tensors * PATCH, dtype=jnp.int32)[None, :]
+    ).astype(jnp.bfloat16)
+    kept_rows = crop_large == (own_core == 0)
+    other_rows = other_large == (own_core == 0)
+
     parts = lax.all_to_all(
         jnp.concatenate([part_teacher, part_student], axis=1),
         "tensor",
@@ -164,22 +180,14 @@
         tiled=True,
         axis_index_groups=far_groups,
     )
-    units = gather_copies(unit_rows(jnp.sum(parts, axis=0)), "tensor")
+    units = unit_rows(jnp.sum(parts, axis=0))
+    units, chosen, crop_large, kept_rows, other_rows = lax.optimization_barrier(
+        (units, chosen, crop_large, kept_rows, other_rows)
+    )
+    units = gather_copies(units, "tensor")
     teacher_units = units[:, :teacher_rows].reshape(-1, width)
     slot_units = units[:, teacher_rows:].reshape(-1, width)
 
-    target_group = lax.dynamic_index_in_dim(
-        routes[:, 0].reshape(-1, CG), own_group, 0, keepdims=False
-    )
-    earlier = jnp.arange(CG)[:, None] > jnp.arange(CG)[None, :]
-    matching = target_group[:, None] == target_group[None, :]
-    slot_rank = jnp.sum((matching & earlier).astype(jnp.int32), axis=1)
-    crop_slot = target_group * slots_per + slot_rank
-    row_slot = (crop_slot[:, None] * PATCH + jnp.arange(PATCH, dtype=jnp.int32)[None, :]).reshape(
-        -1
-    )
-    crop_large = jnp.repeat(target_group < large_groups[0], PATCH)[:, None]
-    chosen = (row_slot[:, None] == jnp.arange(slot_units.shape[0])[None, :]).astype(jnp.bfloat16)
     student_units = jnp.dot(chosen, slot_units, preferred_element_type=jnp.float32).astype(
         jnp.bfloat16
     )
@@ -209,38 +217,39 @@
     log_t = log_total(stats[:, 0])
     crossed = jnp.sum(stats[:, 1] * jnp.exp(stats[:, 0] - log_t[None, :]), axis=0)
     log_s = log_total(stats[:, 2])
-    group_loss = jnp.sum(log_s - crossed)
+    group_loss = jnp.sum((log_s - crossed).reshape(-1, 128), axis=0)
     target = lax.reduce_precision(jnp.exp(shifted - log_t[:, None]), 8, 7)
     student_prob = jnp.exp(scores - log_s[:, None])
     deltas = ((student_prob - target) / STUDENT_TEMP).astype(jnp.bfloat16)
 
-    own_core = own_group % 2
-    kept_rows = crop_large == (own_core == 0)
-    gives = partial_grad(jnp.where(kept_rows, zero, student_units), deltas)
-    keeps = partial_grad(jnp.where(kept_rows, student_units, zero), deltas)
     pairs = [(g, g ^ 1) for g in range(groups)]
+    rows = deltas.shape[0]
+    note = jnp.pad(parts_of(group_loss), ((0, PATCH - 3), (0, protos + width - 128)))
     got = lax.ppermute(
-        jnp.concatenate(
-            [gives.astype(jnp.bfloat16), jnp.broadcast_to(parts_of(group_loss), (width, 128))],
-            axis=1,
-        ),
+        jnp.concatenate([jnp.concatenate([deltas, student_units], axis=1), note], axis=0),
         "group",
         pairs,
     )
-    chip_grad = keeps + got[:, :protos].astype(jnp.float32)
-    chip_loss = group_loss + jnp.sum(got[0, protos:].astype(jnp.float32))
+    chip_grad = partial_grad(jnp.where(kept_rows, student_units, zero), deltas) + partial_grad(
+        jnp.where(other_rows, got[:rows, protos:], zero), got[:rows, :protos]
+    )
+    chip_loss = group_loss + jnp.sum(got[rows : rows + 3, :128].astype(jnp.float32), axis=0)
     chips = groups // 2
     grad_rows = width // chips
+    note = jnp.pad(parts_of(chip_loss), ((0, grad_rows - 3), (0, 0)))
     sent = jnp.concatenate(
-        [chip_grad.astype(jnp.bfloat16), jnp.broadcast_to(parts_of(chip_loss), (width, 128))],
-        axis=1,
-    ).reshape(chips, grad_rows, protos + 128)
+        [
+            chip_grad.astype(jnp.bfloat16).reshape(chips, grad_rows, protos),
+            jnp.broadcast_to(note[None], (chips, grad_rows, 128)),
+        ],
+        axis=2,
+    )
     same_core = [[core + 2 * chip for chip in range(chips)] for core in range(2)]
     taken = lax.all_to_all(
         sent, "group", split_axis=0, concat_axis=0, tiled=True, axis_index_groups=same_core
     )
     loss = (
-        jnp.sum(taken[:, 0, protos:].astype(jnp.float32)) / (routes.shape[0] * PATCH)
+        jnp.sum(taken[:, :3, protos:].astype(jnp.float32)) / (routes.shape[0] * PATCH)
     ).reshape(1)
     summed = jnp.sum(taken[:, :, :protos].astype(jnp.float32), axis=0) / PATCH
     mine = lax.all_to_all(

time: 195 us -> 185 us (0.949)
  waiting for transfers between devices: 50.4 us -> 65.3 us
  blocking collectives: 44.1 us -> 29.3 us
  between operations: 11.9 us -> 3.59 us
  other arithmetic: 15.5 us -> 13.3 us
    all_to_all x1 -> x0, blocking collectives: 16.6 us -> none  [shards(): lax.all_to_all(jnp.concatenate([part_teacher, part_student], axis=1), 'te...]
    all_to_all x0 -> x1, waiting for transfers between devices: none -> 12.4 us  [shards(): lax.all_to_all(jnp.concatenate([part_teacher, part_student], axis=1), 'te...]
    all_to_all x1, starting transfers between devices: 20.2 us -> 13.9 us  [shards(): lax.all_to_all(jnp.concatenate([teacher_sent, student_sent], axis=1), 'te...]
    all_to_all x0 -> x1, starting transfers between devices: none -> 4.48 us  [shards(): lax.all_to_all(jnp.concatenate([part_teacher, part_student], axis=1), 'te...]
    all_to_all x2, starting transfers between devices: 13.4 us -> 17.6 us  [gather_copies(): return lax.all_to_all(copies, axis, split_axis=0, concat_axis=0, tiled=True)]
    convert_element_type x2 -> x1, other arithmetic: 3.93 us -> 0.11 us  [shards(): chosen = (row_slot[:, None] == jnp.arange(tensors * PATCH, dtype=jnp.int3...]
    all_to_all x2, waiting for transfers between devices: 35.8 us -> 38.6 us  [gather_copies(): return lax.all_to_all(copies, axis, split_axis=0, concat_axis=0, tiled=True)]
  transfers between devices with their start and end apart: 9 -> 10, of which waited for: 5 -> 6; matrix products, arithmetic and copies ran while one was open for 4% -> 7% of each run, Pallas kernels for 0% -> 0%
where the time goes in v3:
time: 185 us; the launch traced here: 184 us
  waiting for transfers between devices  65.3 us (35%)
  starting transfers between devices  61.5 us (33%)
  blocking collectives  29.3 us (16%)
  other arithmetic  13.3 us (7%)
  local copies, waits for them, and re-layouts  6.25 us (3%)
  matrix products  4.5 us (2%)
  between operations  3.59 us (2%)
    all_to_all x2, waiting for transfers between devices, gather_copies(): return lax.all_to_all(copies, axis, split_axis=0, concat_axis=0, tiled=True)  38.6 us
    all_to_all x2, starting transfers between devices, gather_copies(): return lax.all_to_all(copies, axis, split_axis=0, concat_axis=0, tiled=True)  17.6 us
    all_to_all x1, blocking collectives, shards(): lax.all_to_all(sent, 'group', split_axis=0, concat_axis=0, tiled=True, ax...  16.8 us
    all_to_all x1, starting transfers between devices, shards(): lax.all_to_all(jnp.concatenate([teacher_sent, student_sent], axis=1), 'te...  13.9 us
    all_to_all x1, blocking collectives, shards(): lax.all_to_all(jnp.broadcast_to(summed.astype(jnp.bfloat16)[None], (chips...  12.5 us
    all_to_all x1, waiting for transfers between devices, shards(): lax.all_to_all(jnp.concatenate([part_teacher, part_student], axis=1), 'te...  12.4 us
    all_to_all x1, waiting for transfers between devices, shards(): lax.all_to_all(jnp.concatenate([teacher_sent, student_sent], axis=1), 'te...  12.4 us
    ppermute x3, starting transfers between devices, shards(): lax.ppermute(weights, 'tensor', [(t, t ^ step) for t in range(tensors)])  9.44 us
  transfers between devices with their start and end apart: 10, of which 6 were waited for; matrix products, arithmetic and copies ran while one was open for 7% of the time, Pallas kernels for 0%

profile of v3, /device:TPU:1, one launch (start us, length us, event | category | flops | bytes accessed | tf_op | source)
XLA Modules:
  0.0 183.6 jit_solution(6421294002362742382)
XLA Ops:
  1.4 0.8 pad_select_fusion
  2.1 6.3 %collective-permute-start = (bf16[16,1280]{1,0:T(8,128)(2,1)S(1)}, bf16[16,1280]{1,0:T(8,128)(2,1)S(1)}, u32[]{:S(2)}, u32[]{:S(2)}) collective-permute-start(bf16[16,1280]{1,0:T(8,128)(2,1)S(1)} %pad_select_fusion), channel_id=1, source_target_pairs={{0,0},{1,1},{2,32},{3,33},{4,64},{5,65},{6,96},{7,97},{8,128},{9,1... | collective-permute-start | bytes 122888 | tf_op jit(solution)/shard_map/ppermute | solution.py:101
  8.4 1.0 convert_reduce_fusion.1
  9.4 1.1 fusion.20
  10.5 0.9 fusion.22
  11.4 0.8 constant_dynamic-update-slice_fusion.2
  12.3 0.7 constant_dynamic-update-slice_fusion.1
  13.0 0.7 constant_dynamic-update-slice_fusion
  13.7 3.5 %collective-permute-start.1 = (bf16[200,256]{1,0:T(8,128)(2,1)S(1)}, bf16[200,256]{1,0:T(8,128)(2,1)S(1)}, u32[]{:S(2)}, u32[]{:S(2)}) collective-permute-start(bf16[200,256]{1,0:T(8,128)(2,1)S(1)} %constant_dynamic-update-slice_fusion), channel_id=1, source_target_pairs={{0,1},{1,0},{2,3},{3,2},{4,5},{5,4},{6,7},{7,6},{8,9},{9,8},{10,11... | collective-permute-start | bytes 307208 | tf_op jit(solution)/shard_map/ppermute | solution.py:113
  17.3 1.9 %collective-permute-start.2 = (bf16[200,256]{1,0:T(8,128)(2,1)S(1)}, bf16[200,256]{1,0:T(8,128)(2,1)S(1)}, u32[]{:S(2)}, u32[]{:S(2)}) collective-permute-start(bf16[200,256]{1,0:T(8,128)(2,1)S(1)} %constant_dynamic-update-slice_fusion), channel_id=1, source_target_pairs={{0,2},{1,3},{2,0},{3,1},{4,6},{5,7},{6,4},{7,5},{8,10},{9,11},{10,... | collective-permute-start | bytes 307208 | tf_op jit(solution)/shard_map/ppermute | solution.py:113
  19.2 4.0 %collective-permute-start.3 = (bf16[200,256]{1,0:T(8,128)(2,1)S(1)}, bf16[200,256]{1,0:T(8,128)(2,1)S(1)}, u32[]{:S(2)}, u32[]{:S(2)}) collective-permute-start(bf16[200,256]{1,0:T(8,128)(2,1)S(1)} %constant_dynamic-update-slice_fusion), channel_id=1, source_target_pairs={{0,3},{1,2},{2,1},{3,0},{4,7},{5,6},{6,5},{7,4},{8,11},{9,10},{10,... | collective-permute-start | bytes 307208 | tf_op jit(solution)/shard_map/ppermute | solution.py:113
  23.7 1.3 reduce.8
  25.8 0.8 fusion.32
  26.7 0.8 copy_bitcast_fusion
  28.2 13.9 %all-to-all-start = ((bf16[8,16,512]{2,1,0:T(8,128)(2,1)}), bf16[8,16,512]{2,1,0:T(8,128)(2,1)S(1)}, u32[]{:S(2)}, u32[]{:S(2)}) async-start(bf16[8,16,512]{2,1,0:T(8,128)(2,1)} %maximum_maximum_fusion), calls=%async_computation | async-start | bytes 262144 | tf_op jit(solution)/shard_map/all_to_all | solution.py:123
  42.4 12.4 %all-to-all-done = bf16[8,16,512]{2,1,0:T(8,128)(2,1)S(1)} async-done(((bf16[8,16,512]{2,1,0:T(8,128)(2,1)}), bf16[8,16,512]{2,1,0:T(8,128)(2,1)S(1)}, u32[]{:S(2)}, u32[]{:S(2)}) %all-to-all-start) | async-done | bytes 131104 | tf_op jit(solution)/shard_map/all_to_all | solution.py:123
  56.3 4.5 %all-to-all-start.1 = ((f32[8,24,256]{2,1,0:T(8,128)}), f32[8,24,256]{2,1,0:T(8,128)S(1)}, u32[]{:S(2)}, u32[]{:S(2)}) async-start(f32[8,24,256]{2,1,0:T(8,128)} %pad_maximum_fusion.3), calls=%async_computation.1 | async-start | bytes 393216 | tf_op jit(solution)/shard_map/all_to_all | solution.py:175
  61.4 12.4 %all-to-all-done.1 = f32[8,24,256]{2,1,0:T(8,128)S(1)} async-done(((f32[8,24,256]{2,1,0:T(8,128)}), f32[8,24,256]{2,1,0:T(8,128)S(1)}, u32[]{:S(2)}, u32[]{:S(2)}) %all-to-all-start.1) | async-done | bytes 196640 | tf_op jit(solution)/shard_map/all_to_all | solution.py:175
  74.1 0.8 broadcast_in_dim.127
  74.9 10.8 %all-to-all-start.2 = ((bf16[32,24,256]{2,1,0:T(8,128)(2,1)}), bf16[32,24,256]{2,1,0:T(8,128)(2,1)S(1)}, u32[]{:S(2)}, u32[]{:S(2)}) async-start(bf16[32,24,256]{2,1,0:T(8,128)(2,1)} %broadcast_in_dim.127), calls=%async_computation.2 | async-start | bytes 786432 | tf_op jit(solution)/shard_map/all_to_all | solution.py:32
  85.7 24.1 %all-to-all-done.2 = bf16[32,24,256]{2,1,0:T(8,128)(2,1)S(1)} async-done(((bf16[32,24,256]{2,1,0:T(8,128)(2,1)}), bf16[32,24,256]{2,1,0:T(8,128)(2,1)S(1)}, u32[]{:S(2)}, u32[]{:S(2)}) %all-to-all-start.2) | async-done | bytes 393248 | tf_op jit(solution)/shard_map/all_to_all | solution.py:32
  110.1 1.6 fusion.99
  113.4 6.8 %all-to-all-start.3 = ((f32[32,6,128]{2,1,0:T(8,128)}), f32[32,6,128]{2,1,0:T(8,128)S(1)}, u32[]{:S(2)}, u32[]{:S(2)}) async-start(f32[32,6,128]{2,1,0:T(8,128)} %broadcast_in_dim.132), calls=%async_computation.3 | async-start | bytes 262144 | tf_op jit(solution)/shard_map/all_to_all | solution.py:32
  120.3 14.5 %all-to-all-done.3 = f32[32,6,128]{2,1,0:T(8,128)S(1)} async-done(((f32[32,6,128]{2,1,0:T(8,128)}), f32[32,6,128]{2,1,0:T(8,128)S(1)}, u32[]{:S(2)}, u32[]{:S(2)}) %all-to-all-start.3) | async-done | bytes 98336 | tf_op jit(solution)/shard_map/all_to_all | solution.py:32
  135.6 5.1 %collective-permute-start.4 = (bf16[272,1280]{1,0:T(8,128)(2,1)S(1)}, bf16[272,1280]{1,0:T(8,128)(2,1)}, u32[]{:S(2)}, u32[]{:S(2)}) collective-permute-start(bf16[272,1280]{1,0:T(8,128)(2,1)S(1)} %pad_maximum_fusion), channel_id=1, source_target_pairs={{0,32},{32,0},{64,96},{96,64},{128,160},{160,128},{192,224},{224,1... | collective-permute-start | bytes 2088968 | tf_op jit(solution)/shard_map/ppermute | solution.py:228
  141.1 1.5 collective-permute-done.4
  142.6 0.9 slice.175
  144.3 1.3 fusion.1
  145.7 16.8 %all_to_all.30 = bf16[8,32,1152]{2,1,0:T(8,128)(2,1)S(1)} all-to-all(bf16[8,32,1152]{2,1,0:T(8,128)(2,1)S(1)} %pad_maximum_fusion.1), channel_id=1, replica_groups={{0,64,128,192,256,320,384,448},{32,96,160,224,288,352,416,480},{1,65,12..., dimensions={0} | all-to-all | bytes 1179648 | tf_op jit(solution)/shard_map/all_to_all | solution.py:248
  162.7 12.5 %all_to_all.31 = bf16[8,32,1024]{2,1,0:T(8,128)(2,1)S(1)} all-to-all(bf16[8,32,1024]{2,1,0:T(8,128)(2,1)S(1)} %broadcast_in_dim.136), channel_id=1, replica_groups={{0,64,128,192,256,320,384,448},{32,96,160,224,288,352,416,480},{1,65,12..., dimensions={0} | all-to-all | bytes 1048576 | tf_op jit(solution)/shard_map/all_to_all | solution.py:255
  175.1 4.7 %collective-permute-start.5 = (bf16[256,1024]{1,0:T(8,128)(2,1)S(1)}, bf16[256,1024]{1,0:T(8,128)(2,1)S(1)}, u32[]{:S(2)}, u32[]{:S(2)}) collective-permute-start(bf16[256,1024]{1,0:T(8,128)(2,1)S(1)} %bitcast.107), channel_id=1, source_target_pairs={{0,32},{32,0},{64,96},{96,64},{128,160},{160,128},{192,224},{224,1... | collective-permute-start | bytes 1572872 | tf_op jit(solution)/shard_map/ppermute | solution.py:263
  181.4 1.1 broadcast_select_fusion
  (89 shorter events, 9.6 us)
Async XLA Ops:
  0.6 111.1 %copy-start = (bf16[256,1024]{1,0:T(8,128)(2,1)S(1)}, bf16[256,1024]{1,0:T(8,128)(2,1)}, u32[]{:S(2)}) copy-start(bf16[256,1024]{1,0:T(8,128)(2,1)} %param.18) | copy-start | bytes 1572868
  2.1 23.0 %collective-permute-start = (bf16[16,1280]{1,0:T(8,128)(2,1)S(1)}, bf16[16,1280]{1,0:T(8,128)(2,1)S(1)}, u32[]{:S(2)}, u32[]{:S(2)}) collective-permute-start(bf16[16,1280]{1,0:T(8,128)(2,1)S(1)} %pad_select_fusion), channel_id=1, source_target_pairs={{0,0},{1,1},{2,32},{3,33},{4,64},{5,65},{6,96},{7,97},{8,128},{9,1... | collective-permute-start | bytes 122888 | tf_op jit(solution)/shard_map/ppermute | solution.py:101
  13.7 28.7 %collective-permute-start.1 = (bf16[200,256]{1,0:T(8,128)(2,1)S(1)}, bf16[200,256]{1,0:T(8,128)(2,1)S(1)}, u32[]{:S(2)}, u32[]{:S(2)}) collective-permute-start(bf16[200,256]{1,0:T(8,128)(2,1)S(1)} %constant_dynamic-update-slice_fusion), channel_id=1, source_target_pairs={{0,1},{1,0},{2,3},{3,2},{4,5},{5,4},{6,7},{7,6},{8,9},{9,8},{10,11... | collective-permute-start | bytes 307208 | tf_op jit(solution)/shard_map/ppermute | solution.py:113
  17.3 25.1 %collective-permute-start.2 = (bf16[200,256]{1,0:T(8,128)(2,1)S(1)}, bf16[200,256]{1,0:T(8,128)(2,1)S(1)}, u32[]{:S(2)}, u32[]{:S(2)}) collective-permute-start(bf16[200,256]{1,0:T(8,128)(2,1)S(1)} %constant_dynamic-update-slice_fusion), channel_id=1, source_target_pairs={{0,2},{1,3},{2,0},{3,1},{4,6},{5,7},{6,4},{7,5},{8,10},{9,11},{10,... | collective-permute-start | bytes 307208 | tf_op jit(solution)/shard_map/ppermute | solution.py:113
  19.2 23.2 %collective-permute-start.3 = (bf16[200,256]{1,0:T(8,128)(2,1)S(1)}, bf16[200,256]{1,0:T(8,128)(2,1)S(1)}, u32[]{:S(2)}, u32[]{:S(2)}) collective-permute-start(bf16[200,256]{1,0:T(8,128)(2,1)S(1)} %constant_dynamic-update-slice_fusion), channel_id=1, source_target_pairs={{0,3},{1,2},{2,1},{3,0},{4,7},{5,6},{6,5},{7,4},{8,11},{9,10},{10,... | collective-permute-start | bytes 307208 | tf_op jit(solution)/shard_map/ppermute | solution.py:113
  28.2 26.6 %all-to-all-start = ((bf16[8,16,512]{2,1,0:T(8,128)(2,1)}), bf16[8,16,512]{2,1,0:T(8,128)(2,1)S(1)}, u32[]{:S(2)}, u32[]{:S(2)}) async-start(bf16[8,16,512]{2,1,0:T(8,128)(2,1)} %maximum_maximum_fusion), calls=%async_computation | async-start | bytes 262144 | tf_op jit(solution)/shard_map/all_to_all | solution.py:123
  56.3 17.6 %all-to-all-start.1 = ((f32[8,24,256]{2,1,0:T(8,128)}), f32[8,24,256]{2,1,0:T(8,128)S(1)}, u32[]{:S(2)}, u32[]{:S(2)}) async-start(f32[8,24,256]{2,1,0:T(8,128)} %pad_maximum_fusion.3), calls=%async_computation.1 | async-start | bytes 393216 | tf_op jit(solution)/shard_map/all_to_all | solution.py:175
  74.9 35.2 %copy-start.2 = (bf16[256,1024]{1,0:T(8,128)(2,1)S(1)}, bf16[256,1024]{1,0:T(8,128)(2,1)}, u32[]{:S(2)}) copy-start(bf16[256,1024]{1,0:T(8,128)(2,1)} %param.29) | copy-start | bytes 1572868
  74.9 34.9 %all-to-all-start.2 = ((bf16[32,24,256]{2,1,0:T(8,128)(2,1)}), bf16[32,24,256]{2,1,0:T(8,128)(2,1)S(1)}, u32[]{:S(2)}, u32[]{:S(2)}) async-start(bf16[32,24,256]{2,1,0:T(8,128)(2,1)} %broadcast_in_dim.127), calls=%async_computation.2 | async-start | bytes 786432 | tf_op jit(solution)/shard_map/all_to_all | solution.py:32
  110.1 1.6 copy-start.1
  113.4 21.4 %all-to-all-start.3 = ((f32[32,6,128]{2,1,0:T(8,128)}), f32[32,6,128]{2,1,0:T(8,128)S(1)}, u32[]{:S(2)}, u32[]{:S(2)}) async-start(f32[32,6,128]{2,1,0:T(8,128)} %broadcast_in_dim.132), calls=%async_computation.3 | async-start | bytes 262144 | tf_op jit(solution)/shard_map/all_to_all | solution.py:32
  135.6 7.0 %collective-permute-start.4 = (bf16[272,1280]{1,0:T(8,128)(2,1)S(1)}, bf16[272,1280]{1,0:T(8,128)(2,1)}, u32[]{:S(2)}, u32[]{:S(2)}) collective-permute-start(bf16[272,1280]{1,0:T(8,128)(2,1)S(1)} %pad_maximum_fusion), channel_id=1, source_target_pairs={{0,32},{32,0},{64,96},{96,64},{128,160},{160,128},{192,224},{224,1... | collective-permute-start | bytes 2088968 | tf_op jit(solution)/shard_map/ppermute | solution.py:228
  175.1 6.3 %collective-permute-start.5 = (bf16[256,1024]{1,0:T(8,128)(2,1)S(1)}, bf16[256,1024]{1,0:T(8,128)(2,1)S(1)}, u32[]{:S(2)}, u32[]{:S(2)}) collective-permute-start(bf16[256,1024]{1,0:T(8,128)(2,1)S(1)} %bitcast.107), channel_id=1, source_target_pairs={{0,32},{32,0},{64,96},{96,64},{128,160},{160,128},{192,224},{224,1... | collective-permute-start | bytes 1572872 | tf_op jit(solution)/shard_map/ppermute | solution.py:263

commit v4 on v3

--- a/solution.py
+++ b/solution.py
@@ -5,7 +5,7 @@
 
 PATCH = 16
 CG = 16
-NEAR = 4
+FAR = 4
 
 
 TEACHER_TEMP = 0.07
@@ -35,6 +35,12 @@
 def log_total(logs):
     top = jnp.max(logs, axis=0)
     return top + jnp.log(jnp.sum(jnp.exp(logs - top[None, :]), axis=0))
+
+
+def by_near(columns, halves):
+    rows, tensors, wide = columns.shape
+    columns = columns.reshape(rows, halves, FAR, FAR, wide).transpose(1, 3, 0, 2, 4)
+    return columns.reshape(tensors // FAR, rows, FAR * wide)
 
 
 def parts_of(values):
@@ -58,6 +64,11 @@
     return lax.dot_general(
         units, deltas, (((0,), (0,)), ((), ())), preferred_element_type=jnp.float32
     )
+
+
+def alone(values, live, exchange):
+    values, live = lax.optimization_barrier((values, live))
+    return lax.optimization_barrier((exchange(values), live))
 
 
 def shards(
@@ -84,9 +95,20 @@
     protos = teacher_proto.shape[1]
     width = teacher_proto.shape[0]
     slots_per = tensors // groups
-    far = tensors // NEAR
-    own_near = own_tensor % NEAR
-    far_groups = [[near + NEAR * other for other in range(far)] for near in range(NEAR)]
+    near = tensors // FAR
+    halves = tensors // (FAR * FAR)
+    own_far = own_tensor // FAR % FAR
+    own_core = own_group % 2
+    near_groups = [
+        [half * FAR * FAR + place * FAR + low for half in range(halves) for low in range(FAR)]
+        for place in range(FAR)
+    ]
+    far_groups = [
+        [half * FAR * FAR + place * FAR + low for place in range(FAR)]
+        for half in range(halves)
+        for low in range(FAR)
+    ]
+    pairs = [(g, g ^ 1) for g in range(groups)]
 
     is_large = own_group < large_groups[0]
     wide = feat_huge.shape[1]
@@ -100,91 +122,103 @@
     ]
     student_feat = lax.ppermute(student_feat, ("group", "tensor"), swap)
     teacher_normed = layer_norm(teacher_feat, teacher_gain)
-    teacher_normed, teacher_proj = lax.optimization_barrier((teacher_normed, teacher_proj))
     row_large = own_tensor // slots_per < large_groups[0]
     slim = feat_large.shape[1]
-    normed_large = layer_norm(student_feat[:, :slim], gain_large).reshape(-1, far, slim // far)
-    normed_large = jnp.pad(normed_large, ((0, 0), (0, 0), (0, (wide - slim) // far)))
-    normed_huge = layer_norm(student_feat, gain_huge).reshape(-1, far, wide // far)
+    student_rows = student_feat.shape[0]
+    normed_large = layer_norm(student_feat[:, :slim], gain_large)
+    normed_large = by_near(normed_large.reshape(student_rows, tensors, -1), halves)
+    normed_large = jnp.pad(normed_large, ((0, 0), (0, 0), (0, (wide - slim) // near)))
+    normed_huge = layer_norm(student_feat, gain_huge)
+    normed_huge = by_near(normed_huge.reshape(student_rows, tensors, -1), halves)
     student_normed = jnp.where(row_large, normed_large, normed_huge)
 
     weights = jnp.concatenate([teacher_proj, proj_large, proj_huge], axis=0)
-    held = [weights] + [
-        lax.ppermute(weights, "tensor", [(t, t ^ step) for t in range(tensors)])
-        for step in range(1, NEAR)
-    ]
-    teacher_rows = teacher_feat.shape[0]
-    piece = teacher_feat.shape[1] // far
-    slot_pad = piece // 2 - wide // far
-    teacher_sent = teacher_normed.reshape(teacher_rows, far, piece).transpose(1, 0, 2)
-    student_sent = jnp.pad(student_normed, ((0, 0), (0, 0), (0, slot_pad))).transpose(1, 0, 2)
-    half = student_sent.shape[1] // 2
-    student_sent = jnp.concatenate([student_sent[:, :half], student_sent[:, half:]], axis=2)
-    cols = lax.all_to_all(
-        jnp.concatenate([teacher_sent, student_sent], axis=1),
+    half_width = width // 2
+    held = jnp.where(own_core == 0, weights[:, :half_width], weights[:, half_width:])
+    held = lax.all_to_all(
+        jnp.broadcast_to(held[None], (FAR, *held.shape)),
         "tensor",
         split_axis=0,
         concat_axis=0,
         tiled=True,
         axis_index_groups=far_groups,
     )
-    cols, held = lax.optimization_barrier((cols, held))
-    held = jnp.stack(held)
-    ordered = [
-        lax.dynamic_index_in_dim(held, own_near ^ place, 0, keepdims=False) for place in range(NEAR)
-    ]
+    lent = lax.ppermute(held, "group", pairs)
+
+    teacher_rows = teacher_feat.shape[0]
+    piece = teacher_feat.shape[1] // near
+    slot_pad = piece // 2 - wide // near
+    teacher_sent = by_near(teacher_normed.reshape(teacher_rows, tensors, -1), halves)
+    student_sent = jnp.pad(student_normed, ((0, 0), (0, 0), (0, slot_pad)))
+    half = student_rows // 2
+    student_sent = jnp.concatenate([student_sent[:, :half], student_sent[:, half:]], axis=2)
+
+    def to_near(values):
+        return lax.all_to_all(
+            values,
+            "tensor",
+            split_axis=0,
+            concat_axis=0,
+            tiled=True,
+            axis_index_groups=near_groups,
+        )
+
+    row_slot, crop_large = crop_rows(routes, own_group, large_groups[0], slots_per)
+    _, other_large = crop_rows(routes, own_group ^ 1, large_groups[0], slots_per)
+    near_large = jnp.array(near_groups, dtype=jnp.int32)[own_far] // slots_per < large_groups[0]
+    heads = (teacher_proto, center, proto_large, proto_huge)
+    live = (row_slot, crop_large, other_large, near_large, own_core, heads)
+    cols, live = alone(jnp.concatenate([teacher_sent, student_sent], axis=1), live, to_near)
+    cols, held, lent = lax.optimization_barrier((cols, held, lent))
+    row_slot, crop_large, other_large, near_large, own_core, heads = live
+    held = jnp.concatenate(
+        [jnp.where(own_core == 0, held, lent), jnp.where(own_core == 0, lent, held)], axis=2
+    )
     first, second = teacher_proj.shape[0], proj_large.shape[0]
-    teacher_w = jnp.concatenate([block[:first] for block in ordered], axis=0)
-    large_w = jnp.concatenate([block[first : first + second] for block in ordered], axis=0)
-    huge_w = jnp.concatenate([block[first + second :] for block in ordered], axis=0)
+    teacher_w = held[:, :first].reshape(-1, width)
+    large_w = held[:, first : first + second].reshape(-1, width)
+    huge_w = held[:, first + second :].reshape(-1, width)
     teacher_cols = cols[:, :teacher_rows]
     student_cols = jnp.concatenate(
         [
-            cols[:, teacher_rows:, : wide // far],
-            cols[:, teacher_rows:, piece // 2 : piece // 2 + wide // far],
+            cols[:, teacher_rows:, : wide // near],
+            cols[:, teacher_rows:, piece // 2 : piece // 2 + wide // near],
         ],
         axis=1,
     )
-    far_large = (
-        (jnp.arange(far, dtype=jnp.int32) * NEAR + own_near) // slots_per < large_groups[0]
-    )[:, None, None]
+    near_large = near_large[:, None, None]
     zero = jnp.zeros((), jnp.bfloat16)
     part_teacher = jnp.einsum(
         "crf,fb->crb", teacher_cols, teacher_w, preferred_element_type=jnp.float32
     )
     part_student = jnp.einsum(
         "crf,fb->crb",
-        jnp.where(far_large, student_cols[:, :, : large_w.shape[0]], zero),
+        jnp.where(near_large, student_cols[:, :, : large_w.shape[0]], zero),
         large_w,
         preferred_element_type=jnp.float32,
     ) + jnp.einsum(
         "crf,fb->crb",
-        jnp.where(far_large, zero, student_cols),
+        jnp.where(near_large, zero, student_cols),
         huge_w,
         preferred_element_type=jnp.float32,
     )
-    own_core = own_group % 2
-    row_slot, crop_large = crop_rows(routes, own_group, large_groups[0], slots_per)
-    _, other_large = crop_rows(routes, own_group ^ 1, large_groups[0], slots_per)
+    live = (row_slot, crop_large, other_large, own_core, heads)
+    parts, live = alone(jnp.concatenate([part_teacher, part_student], axis=1), live, to_near)
+    units = jnp.broadcast_to(
+        unit_rows(jnp.sum(parts, axis=0))[None], (tensors, parts.shape[1], width)
+    )
+
+    def to_all(values):
+        return lax.all_to_all(values, "tensor", split_axis=0, concat_axis=0, tiled=True)
+
+    units, live = alone(units, live, to_all)
+    row_slot, crop_large, other_large, own_core, heads = live
+    teacher_proto, center, proto_large, proto_huge = heads
     chosen = (
         row_slot[:, None] == jnp.arange(tensors * PATCH, dtype=jnp.int32)[None, :]
     ).astype(jnp.bfloat16)
     kept_rows = crop_large == (own_core == 0)
     other_rows = other_large == (own_core == 0)
-
-    parts = lax.all_to_all(
-        jnp.concatenate([part_teacher, part_student], axis=1),
-        "tensor",
-        split_axis=0,
-        concat_axis=0,
-        tiled=True,
-        axis_index_groups=far_groups,
-    )
-    units = unit_rows(jnp.sum(parts, axis=0))
-    units, chosen, crop_large, kept_rows, other_rows = lax.optimization_barrier(
-        (units, chosen, crop_large, kept_rows, other_rows)
-    )
-    units = gather_copies(units, "tensor")
     teacher_units = units[:, :teacher_rows].reshape(-1, width)
     slot_units = units[:, teacher_rows:].reshape(-1, width)
 
@@ -213,7 +247,11 @@
             student_top + jnp.log(student_sum),
         ]
     )
-    stats = gather_copies(stats.reshape(-1, 128), "tensor").reshape(tensors, 3, -1)
+    stats = jnp.broadcast_to(stats.reshape(1, -1, 128), (tensors, stats.size // 128, 128))
+    live = (shifted, scores, student_units, kept_rows, other_rows, own_core)
+    stats, live = alone(stats, live, to_all)
+    shifted, scores, student_units, kept_rows, other_rows, own_core = live
+    stats = stats.reshape(tensors, 3, -1)
     log_t = log_total(stats[:, 0])
     crossed = jnp.sum(stats[:, 1] * jnp.exp(stats[:, 0] - log_t[None, :]), axis=0)
     log_s = log_total(stats[:, 2])
@@ -222,7 +260,6 @@
     student_prob = jnp.exp(scores - log_s[:, None])
     deltas = ((student_prob - target) / STUDENT_TEMP).astype(jnp.bfloat16)
 
-    pairs = [(g, g ^ 1) for g in range(groups)]
     rows = deltas.shape[0]
     note = jnp.pad(parts_of(group_loss), ((0, PATCH - 3), (0, protos + width - 128)))
     got = lax.ppermute(

time: 185 us -> 163 us (0.88)
  blocking collectives: 29.3 us -> 87.6 us
  waiting for transfers between devices: 65.3 us -> 15.1 us
  starting transfers between devices: 61.5 us -> 39.9 us
  other arithmetic: 13.3 us -> 7.94 us
  matrix products: 4.5 us -> 2.6 us
    all_to_all x0 -> x3, blocking collectives: none -> 55.9 us  [the longest x2 46.5 us: to_all(): lax.all_to_all(values, 'tensor', split_axis=0, concat_axis=0, tiled=True)]
    all_to_all x4 -> x2, waiting for transfers between devices: 63.5 us -> 13.6 us  [the longest x1 8.4 us: shards(): lax.all_to_all(jnp.broadcast_to(held[None], (FAR, *held.shape)), 'tensor'...]
    all_to_all x4 -> x2, starting transfers between devices: 35.9 us -> 20.8 us  [the longest x1 12 us: shards(): lax.all_to_all(jnp.broadcast_to(held[None], (FAR, *held.shape)), 'tensor'...]
    ppermute x3 -> x1, starting transfers between devices: 9.44 us -> 1.91 us  [shards(): lent = lax.ppermute(held, 'group', pairs)]
    all_to_all x1, blocking collectives: 16.8 us -> 19.2 us  [shards(): lax.all_to_all(sent, 'group', split_axis=0, concat_axis=0, tiled=True, ax...]
  transfers between devices with their start and end apart: 10 -> 6, of which waited for: 6 -> 4; matrix products, arithmetic and copies ran while one was open for 7% -> 6% of each run, Pallas kernels for 0% -> 0%
where the time goes in v4:
time: 163 us; the launch traced here: 162 us
  blocking collectives  87.6 us (54%)
  starting transfers between devices  39.9 us (24%)
  waiting for transfers between devices  15.1 us (9%)
  other arithmetic  7.94 us (5%)
  local copies, waits for them, and re-layouts  5.47 us (3%)
  between operations  3.62 us (2%)
  matrix products  2.6 us (2%)
    all_to_all x2, blocking collectives, to_all(): lax.all_to_all(values, 'tensor', split_axis=0, concat_axis=0, tiled=True)  46.5 us
    all_to_all x1, blocking collectives, shards(): lax.all_to_all(sent, 'group', split_axis=0, concat_axis=0, tiled=True, ax...  19.2 us
    all_to_all x1, blocking collectives, shards(): lax.all_to_all(jnp.broadcast_to(summed.astype(jnp.bfloat16)[None], (chips...  12.5 us
    all_to_all x1, starting transfers between devices, shards(): lax.all_to_all(jnp.broadcast_to(held[None], (FAR, *held.shape)), 'tensor'...  12 us
    all_to_all x1, blocking collectives, to_near(): lax.all_to_all(values, 'tensor', split_axis=0, concat_axis=0, tiled=True,...  9.4 us
    all_to_all x1, starting transfers between devices, to_near(): lax.all_to_all(values, 'tensor', split_axis=0, concat_axis=0, tiled=True,...  8.8 us
    all_to_all x1, waiting for transfers between devices, shards(): lax.all_to_all(jnp.broadcast_to(held[None], (FAR, *held.shape)), 'tensor'...  8.4 us
    ppermute x1, starting transfers between devices, shards(): student_feat = lax.ppermute(student_feat, ('group', 'tensor'), swap)  6.29 us
  transfers between devices with their start and end apart: 6, of which 4 were waited for; matrix products, arithmetic and copies ran while one was open for 6% of the time, Pallas kernels for 0%

profile of v4, /device:TPU:1, one launch (start us, length us, event | category | flops | bytes accessed | tf_op | source)
XLA Modules:
  0.0 162.2 jit_solution(927914531595874078)
XLA Ops:
  1.4 0.8 pad_select_fusion.1
  2.2 6.3 %collective-permute-start = (bf16[16,1280]{1,0:T(8,128)(2,1)S(1)}, bf16[16,1280]{1,0:T(8,128)(2,1)S(1)}, u32[]{:S(2)}, u32[]{:S(2)}) collective-permute-start(bf16[16,1280]{1,0:T(8,128)(2,1)S(1)} %pad_select_fusion.1), channel_id=1, source_target_pairs={{0,0},{1,1},{2,32},{3,33},{4,64},{5,65},{6,96},{7,97},{8,128},{9,1... | collective-permute-start | bytes 122888 | tf_op jit(solution)/shard_map/ppermute | solution.py:123
  8.5 0.8 constant_dynamic-update-slice_fusion.2
  9.3 0.7 constant_dynamic-update-slice_fusion.1
  10.1 0.7 constant_dynamic-update-slice_fusion
  10.8 0.7 broadcast_in_dim.128
  11.5 12.0 %all-to-all-start.1 = ((bf16[4,200,128]{2,1,0:T(8,128)(2,1)}), bf16[4,200,128]{2,1,0:T(8,128)(2,1)S(1)}, u32[]{:S(2)}, u32[]{:S(2)}) async-start(bf16[4,200,128]{2,1,0:T(8,128)(2,1)} %broadcast_in_dim.128), calls=%async_computation.1 | async-start | bytes 409600 | tf_op jit(solution)/shard_map/all_to_all | solution.py:138
  23.9 0.5 broadcast.216
  24.4 0.7 reduce.8
  25.6 0.7 fusion.72
  28.4 0.7 maximum_maximum_fusion
  29.1 8.4 %all-to-all-done.1 = bf16[4,200,128]{2,1,0:T(8,128)(2,1)S(1)} async-done(((bf16[4,200,128]{2,1,0:T(8,128)(2,1)}), bf16[4,200,128]{2,1,0:T(8,128)(2,1)S(1)}, u32[]{:S(2)}, u32[]{:S(2)}) %all-to-all-start.1) | async-done | bytes 204832 | tf_op jit(solution)/shard_map/all_to_all | solution.py:138
  37.5 8.8 %all-to-all-start = ((bf16[8,16,512]{2,1,0:T(8,128)(2,1)}), bf16[8,16,512]{2,1,0:T(8,128)(2,1)S(1)}, u32[]{:S(2)}, u32[]{:S(2)}) async-start(bf16[8,16,512]{2,1,0:T(8,128)(2,1)} %maximum_maximum_fusion), calls=%async_computation | async-start | bytes 262144 | tf_op jit(solution)/shard_map/all_to_all | solution.py:157
  46.3 1.9 %collective-permute-start.1 = (bf16[4,200,128]{2,1,0:T(8,128)(2,1)S(1)}, bf16[4,200,128]{2,1,0:T(8,128)(2,1)S(1)}, u32[]{:S(2)}, u32[]{:S(2)}) collective-permute-start(bf16[4,200,128]{2,1,0:T(8,128)(2,1)S(1)} %all-to-all-done.1), channel_id=1, source_target_pairs={{0,32},{32,0},{64,96},{96,64},{128,160},{160,128},{192,224},{224,1... | collective-permute-start | bytes 614408 | tf_op jit(solution)/shard_map/ppermute | solution.py:146
  48.2 5.2 %all-to-all-done = bf16[8,16,512]{2,1,0:T(8,128)(2,1)S(1)} async-done(((bf16[8,16,512]{2,1,0:T(8,128)(2,1)}), bf16[8,16,512]{2,1,0:T(8,128)(2,1)S(1)}, u32[]{:S(2)}, u32[]{:S(2)}) %all-to-all-start) | async-done | bytes 131104 | tf_op jit(solution)/shard_map/all_to_all | solution.py:157
  54.1 9.4 %all_to_all.35 = f32[8,24,256]{2,1,0:T(8,128)S(1)} all-to-all(f32[8,24,256]{2,1,0:T(8,128)S(1)} %pad_maximum_fusion.2), channel_id=1, replica_groups={{0,1,2,3,16,17,18,19},{4,5,6,7,20,21,22,23},{8,9,10,11,24,25,26,27},{12..., dimensions={0} | all-to-all | bytes 393216 | tf_op jit(solution)/shard_map/all_to_all | solution.py:157
  63.8 26.9 %all_to_all.36 = bf16[32,24,256]{2,1,0:T(8,128)(2,1)S(1)} all-to-all(bf16[32,24,256]{2,1,0:T(8,128)(2,1)S(1)} %broadcast_in_dim.133), channel_id=1, replica_groups=mesh['group'=16,'tensor'=32] {'tensor'}, dimensions={0} | all-to-all | bytes 786432 | tf_op jit(solution)/shard_map/all_to_all | solution.py:212
  90.8 0.4 fusion.83
  91.5 0.3 copy-done.7
  91.9 0.5 fusion.82
  92.5 0.6 fusion.5
  93.1 19.6 %all_to_all.37 = f32[32,6,128]{2,1,0:T(8,128)S(1)} all-to-all(f32[32,6,128]{2,1,0:T(8,128)S(1)} %broadcast_in_dim.138), channel_id=1, replica_groups=mesh['group'=16,'tensor'=32] {'tensor'}, dimensions={0} | all-to-all | bytes 196608 | tf_op jit(solution)/shard_map/all_to_all | solution.py:212
  113.0 0.4 multiply_convert_fusion
  113.5 6.2 %collective-permute-start.2 = (bf16[272,1280]{1,0:T(8,128)(2,1)S(1)}, bf16[272,1280]{1,0:T(8,128)(2,1)S(1)}, u32[]{:S(2)}, u32[]{:S(2)}) collective-permute-start(bf16[272,1280]{1,0:T(8,128)(2,1)S(1)} %pad_maximum_fusion), channel_id=1, source_target_pairs={{0,32},{32,0},{64,96},{96,64},{128,160},{160,128},{192,224},{224,1... | collective-permute-start | bytes 2088968 | tf_op jit(solution)/shard_map/ppermute | solution.py:265
  119.7 0.4 fusion.18
  120.1 1.3 collective-permute-done.2
  121.5 0.4 fusion.1
  121.9 19.2 %all_to_all.38 = bf16[8,32,1152]{2,1,0:T(8,128)(2,1)S(1)} all-to-all(bf16[8,32,1152]{2,1,0:T(8,128)(2,1)S(1)} %pad_maximum_fusion.1), channel_id=1, replica_groups={{0,64,128,192,256,320,384,448},{32,96,160,224,288,352,416,480},{1,65,12..., dimensions={0} | all-to-all | bytes 1179648 | tf_op jit(solution)/shard_map/all_to_all | solution.py:285
  141.3 12.5 %all_to_all.39 = bf16[8,32,1024]{2,1,0:T(8,128)(2,1)S(1)} all-to-all(bf16[8,32,1024]{2,1,0:T(8,128)(2,1)S(1)} %broadcast_in_dim.144), channel_id=1, replica_groups={{0,64,128,192,256,320,384,448},{32,96,160,224,288,352,416,480},{1,65,12..., dimensions={0} | all-to-all | bytes 1048576 | tf_op jit(solution)/shard_map/all_to_all | solution.py:292
  153.8 4.7 %collective-permute-start.3 = (bf16[256,1024]{1,0:T(8,128)(2,1)S(1)}, bf16[256,1024]{1,0:T(8,128)(2,1)S(1)}, u32[]{:S(2)}, u32[]{:S(2)}) collective-permute-start(bf16[256,1024]{1,0:T(8,128)(2,1)S(1)} %bitcast.87), channel_id=1, source_target_pairs={{0,32},{32,0},{64,96},{96,64},{128,160},{160,128},{192,224},{224,1... | collective-permute-start | bytes 1572872 | tf_op jit(solution)/shard_map/ppermute | solution.py:300
  158.5 0.6 convert_reduce_fusion.4
  160.0 1.1 broadcast_select_fusion
  (99 shorter events, 5.2 us)
Async XLA Ops:
  0.6 90.1 %copy-start = (bf16[256,1024]{1,0:T(8,128)(2,1)S(1)}, bf16[256,1024]{1,0:T(8,128)(2,1)}, u32[]{:S(2)}) copy-start(bf16[256,1024]{1,0:T(8,128)(2,1)} %param.19) | copy-start | bytes 1572868
  0.6 22.9 %copy-start.1 = (bf16[8,4096]{1,0:T(8,128)(2,1)S(1)}, bf16[8,4096]{1,0:T(8,128)(2,1)}, u32[]{:S(2)}) copy-start(bf16[8,4096]{1,0:T(8,128)(2,1)} %param.16) | copy-start | bytes 196612
  0.7 23.8 %copy-start.6 = (s32[256,1]{0,1:T(1,128)S(1)}, s32[256,1]{0,1:T(1,128)}, u32[]{:S(2)}) copy-start(s32[256,1]{0,1:T(1,128)} %param.21) | copy-start | bytes 3076
  0.7 24.8 %copy-start.2 = (f32[4096]{0:T(1024)S(1)}, f32[4096]{0:T(1024)}, u32[]{:S(2)}) copy-start(f32[4096]{0:T(1024)} %param.17) | copy-start | bytes 49156
  0.7 26.7 %copy-start.3 = (f32[1280]{0:T(1024)S(1)}, f32[1280]{0:T(1024)}, u32[]{:S(2)}) copy-start(f32[1280]{0:T(1024)} %param.26) | copy-start | bytes 15364
  2.2 24.6 %collective-permute-start = (bf16[16,1280]{1,0:T(8,128)(2,1)S(1)}, bf16[16,1280]{1,0:T(8,128)(2,1)S(1)}, u32[]{:S(2)}, u32[]{:S(2)}) collective-permute-start(bf16[16,1280]{1,0:T(8,128)(2,1)S(1)} %pad_select_fusion.1), channel_id=1, source_target_pairs={{0,0},{1,1},{2,32},{3,33},{4,64},{5,65},{6,96},{7,97},{8,128},{9,1... | collective-permute-start | bytes 122888 | tf_op jit(solution)/shard_map/ppermute | solution.py:123
  10.8 17.1 %copy-start.5 = (f32[1024]{0:T(1024)S(1)}, f32[1024]{0:T(1024)}, u32[]{:S(2)}) copy-start(f32[1024]{0:T(1024)} %param.25) | copy-start | bytes 12292
  11.5 26.0 %all-to-all-start.1 = ((bf16[4,200,128]{2,1,0:T(8,128)(2,1)}), bf16[4,200,128]{2,1,0:T(8,128)(2,1)S(1)}, u32[]{:S(2)}, u32[]{:S(2)}) async-start(bf16[4,200,128]{2,1,0:T(8,128)(2,1)} %broadcast_in_dim.128), calls=%async_computation.1 | async-start | bytes 409600 | tf_op jit(solution)/shard_map/all_to_all | solution.py:138
  37.5 15.9 %all-to-all-start = ((bf16[8,16,512]{2,1,0:T(8,128)(2,1)}), bf16[8,16,512]{2,1,0:T(8,128)(2,1)S(1)}, u32[]{:S(2)}, u32[]{:S(2)}) async-start(bf16[8,16,512]{2,1,0:T(8,128)(2,1)} %maximum_maximum_fusion), calls=%async_computation | async-start | bytes 262144 | tf_op jit(solution)/shard_map/all_to_all | solution.py:157
  46.3 7.1 %collective-permute-start.1 = (bf16[4,200,128]{2,1,0:T(8,128)(2,1)S(1)}, bf16[4,200,128]{2,1,0:T(8,128)(2,1)S(1)}, u32[]{:S(2)}, u32[]{:S(2)}) collective-permute-start(bf16[4,200,128]{2,1,0:T(8,128)(2,1)S(1)} %all-to-all-done.1), channel_id=1, source_target_pairs={{0,32},{32,0},{64,96},{96,64},{128,160},{160,128},{192,224},{224,1... | collective-permute-start | bytes 614408 | tf_op jit(solution)/shard_map/ppermute | solution.py:146
  63.5 27.2 %copy-start.4 = (f32[1024]{0:T(1024)S(1)}, f32[1024]{0:T(1024)}, u32[]{:S(2)}) copy-start(f32[1024]{0:T(1024)} %param.20) | copy-start | bytes 12292
  90.7 1.0 copy-start.7
  90.7 1.2 copy-start.8
  113.5 7.9 %collective-permute-start.2 = (bf16[272,1280]{1,0:T(8,128)(2,1)S(1)}, bf16[272,1280]{1,0:T(8,128)(2,1)S(1)}, u32[]{:S(2)}, u32[]{:S(2)}) collective-permute-start(bf16[272,1280]{1,0:T(8,128)(2,1)S(1)} %pad_maximum_fusion), channel_id=1, source_target_pairs={{0,32},{32,0},{64,96},{96,64},{128,160},{160,128},{192,224},{224,1... | collective-permute-start | bytes 2088968 | tf_op jit(solution)/shard_map/ppermute | solution.py:265
  153.8 6.3 %collective-permute-start.3 = (bf16[256,1024]{1,0:T(8,128)(2,1)S(1)}, bf16[256,1024]{1,0:T(8,128)(2,1)S(1)}, u32[]{:S(2)}, u32[]{:S(2)}) collective-permute-start(bf16[256,1024]{1,0:T(8,128)(2,1)S(1)} %bitcast.87), channel_id=1, source_target_pairs={{0,32},{32,0},{64,96},{96,64},{128,160},{160,128},{192,224},{224,1... | collective-permute-start | bytes 1572872 | tf_op jit(solution)/shard_map/ppermute | solution.py:300

commit v5 on v4

--- a/solution.py
+++ b/solution.py
@@ -1,6 +1,8 @@
 import jax
 import jax.numpy as jnp
 from jax import lax
+from jax.experimental import pallas as pl
+from jax.experimental.pallas import tpu as pltpu
 from jax.sharding import PartitionSpec as P
 
 PATCH = 16
@@ -50,12 +52,16 @@
     return jnp.stack([high, middle, low]).astype(jnp.bfloat16)
 
 
-def crop_rows(routes, group, large, slots_per):
+def crop_rows(routes, group, large, places):
     target_group = lax.dynamic_index_in_dim(routes[:, 0].reshape(-1, CG), group, 0, keepdims=False)
     earlier = jnp.arange(CG)[:, None] > jnp.arange(CG)[None, :]
     matching = target_group[:, None] == target_group[None, :]
     slot_rank = jnp.sum((matching & earlier).astype(jnp.int32), axis=1)
-    first_row = (target_group * slots_per + slot_rank) * PATCH
+    slots = places.shape[1]
+    own_places = lax.dynamic_index_in_dim(places, group, 0, keepdims=False)
+    crop_slot = target_group * (slots // places.shape[0]) + slot_rank
+    named = crop_slot[:, None] == jnp.arange(slots, dtype=jnp.int32)[None, :]
+    first_row = jnp.sum(jnp.where(named, own_places[None, :], 0), axis=1) * PATCH
     row_slot = (first_row[:, None] + jnp.arange(PATCH, dtype=jnp.int32)[None, :]).reshape(-1)
     return (row_slot, jnp.repeat(target_group < large, PATCH)[:, None])
 
@@ -69,6 +75,97 @@
 def alone(values, live, exchange):
     values, live = lax.optimization_barrier((values, live))
     return lax.optimization_barrier((exchange(values), live))
+
+
+def around(first, second, count):
+    return min((first - second) % count, (second - first) % count)
+
+
+def hops(first_group, first_tensor, second_group, second_tensor):
+    first_x = first_group // 8 * 2 + first_tensor // 16
+    second_x = second_group // 8 * 2 + second_tensor // 16
+    return (
+        around(first_x, second_x, 4)
+        + around(first_group // 2, second_group // 2, 4)
+        + around(first_tensor, second_tensor, 16)
+    )
+
+
+def best_places(costs):
+    count = len(costs)
+    rows, cols, match = [0] * (count + 1), [0] * (count + 1), [0] * (count + 1)
+    for row in range(1, count + 1):
+        match[0], col = row, 0
+        least, back, used = [1 << 60] * (count + 1), [0] * (count + 1), [False] * (count + 1)
+        while match[col]:
+            used[col] = True
+            current, step, following = match[col], 1 << 60, 0
+            for other in range(1, count + 1):
+                if not used[other]:
+                    left = costs[current - 1][other - 1] - rows[current] - cols[other]
+                    if left < least[other]:
+                        least[other], back[other] = left, col
+                    if least[other] < step:
+                        step, following = least[other], other
+            for other in range(count + 1):
+                if used[other]:
+                    rows[match[other]] += step
+                    cols[other] -= step
+                else:
+                    least[other] -= step
+            col = following
+        while col:
+            match[col] = match[back[col]]
+            col = back[col]
+    places = [0] * count
+    for col in range(1, count + 1):
+        places[match[col] - 1] = col - 1
+    return places
+
+
+def slot_places(groups, tensors):
+    slots_per = tensors // groups
+    return [
+        best_places(
+            [
+                [hops(slot // slots_per, s * slots_per + slot % slots_per, s, t) ** 6 for t in range(tensors)]
+                for slot in range(tensors)
+            ]
+        )
+        for s in range(groups)
+    ]
+
+
+def prepare_kernel(flags, teacher_w, large_w, huge_w, large_x, huge_x, weights, student):
+    half = weights.shape[2]
+    first, second, third = teacher_w.shape[0], large_w.shape[0], huge_w.shape[0]
+    low_core = flags[0] == 0
+    spare = weights.shape[1] - first - second - third
+    end = jnp.concatenate([huge_w[...], jnp.zeros((spare, 2 * half), huge_w.dtype)], axis=0)
+    for start, rows in ((0, teacher_w[...]), (first, large_w[...]), (first + second, end)):
+        kept = jnp.where(low_core, rows[:, :half], rows[:, half:])
+        for place in range(FAR):
+            weights[place, start : start + rows.shape[0], :] = kept
+    slim = large_x.shape[1]
+    is_large = flags[1] != 0
+    student[:, :slim] = jnp.where(is_large, large_x[...], huge_x[:, :slim])
+    student[:, slim:] = jnp.where(is_large, jnp.zeros_like(huge_x[:, slim:]), huge_x[:, slim:])
+
+
+def prepare(own_core, is_large, teacher_w, large_w, huge_w, large_x, huge_x):
+    rows = teacher_w.shape[0] + large_w.shape[0] + huge_w.shape[0]
+    rows += -rows % 16
+    flags = jnp.stack([own_core.astype(jnp.int32), is_large.astype(jnp.int32)])
+    whole = pl.BlockSpec(memory_space=pltpu.VMEM)
+    return pl.pallas_call(
+        prepare_kernel,
+        out_shape=(
+            jax.ShapeDtypeStruct((FAR, rows, teacher_w.shape[1] // 2), jnp.bfloat16),
+            jax.ShapeDtypeStruct(huge_x.shape, jnp.bfloat16),
+        ),
+        in_specs=[pl.BlockSpec(memory_space=pltpu.SMEM)] + [whole] * 5,
+        out_specs=(whole, whole),
+    )(flags, teacher_w, large_w, huge_w, large_x, huge_x)
 
 
 def shards(
@@ -112,17 +209,23 @@
 
     is_large = own_group < large_groups[0]
     wide = feat_huge.shape[1]
-    padded_large = jnp.pad(feat_large, ((0, 0), (0, wide - feat_large.shape[1])))
-    student_feat = jnp.where(is_large, padded_large, feat_huge)
+    weights, student_feat = prepare(
+        own_core, is_large, teacher_proj, proj_large, proj_huge, feat_large, feat_huge
+    )
+    places = slot_places(groups, tensors)
+    owners = [[row.index(place) for place in range(tensors)] for row in places]
     swap = [
-        ((j * groups + s) * slots_per + k, (s * groups + j) * slots_per + k)
+        (j * tensors + s * slots_per + k, s * tensors + places[s][j * slots_per + k])
         for j in range(groups)
         for s in range(groups)
         for k in range(slots_per)
     ]
     student_feat = lax.ppermute(student_feat, ("group", "tensor"), swap)
     teacher_normed = layer_norm(teacher_feat, teacher_gain)
-    row_large = own_tensor // slots_per < large_groups[0]
+    places, owners = jnp.array(places, jnp.int32), jnp.array(owners, jnp.int32)
+    own_owners = lax.dynamic_index_in_dim(owners, own_group, 0, keepdims=False)
+    large_places = own_owners // slots_per < large_groups[0]
+    row_large = lax.dynamic_index_in_dim(large_places, own_tensor, 0, keepdims=False)
     slim = feat_large.shape[1]
     student_rows = student_feat.shape[0]
     normed_large = layer_norm(student_feat[:, :slim], gain_large)
@@ -132,11 +235,8 @@
     normed_huge = by_near(normed_huge.reshape(student_rows, tensors, -1), halves)
     student_normed = jnp.where(row_large, normed_large, normed_huge)
 
-    weights = jnp.concatenate([teacher_proj, proj_large, proj_huge], axis=0)
-    half_width = width // 2
-    held = jnp.where(own_core == 0, weights[:, :half_width], weights[:, half_width:])
     held = lax.all_to_all(
-        jnp.broadcast_to(held[None], (FAR, *held.shape)),
+        weights,
         "tensor",
         split_axis=0,
         concat_axis=0,
@@ -163,9 +263,11 @@
             axis_index_groups=near_groups,
         )
 
-    row_slot, crop_large = crop_rows(routes, own_group, large_groups[0], slots_per)
-    _, other_large = crop_rows(routes, own_group ^ 1, large_groups[0], slots_per)
-    near_large = jnp.array(near_groups, dtype=jnp.int32)[own_far] // slots_per < large_groups[0]
+    row_slot, crop_large = crop_rows(routes, own_group, large_groups[0], places)
+    _, other_large = crop_rows(routes, own_group ^ 1, large_groups[0], places)
+    near_large = lax.dynamic_index_in_dim(
+        large_places.reshape(halves, FAR, FAR), own_far, 1, keepdims=False
+    ).reshape(-1)
     heads = (teacher_proto, center, proto_large, proto_huge)
     live = (row_slot, crop_large, other_large, near_large, own_core, heads)
     cols, live = alone(jnp.concatenate([teacher_sent, student_sent], axis=1), live, to_near)
@@ -177,7 +279,7 @@
     first, second = teacher_proj.shape[0], proj_large.shape[0]
     teacher_w = held[:, :first].reshape(-1, width)
     large_w = held[:, first : first + second].reshape(-1, width)
-    huge_w = held[:, first + second :].reshape(-1, width)
+    huge_w = held[:, first + second : first + second + proj_huge.shape[0]].reshape(-1, width)
     teacher_cols = cols[:, :teacher_rows]
     student_cols = jnp.concatenate(
         [
@@ -204,14 +306,24 @@
     )
     live = (row_slot, crop_large, other_large, own_core, heads)
     parts, live = alone(jnp.concatenate([part_teacher, part_student], axis=1), live, to_near)
-    units = jnp.broadcast_to(
-        unit_rows(jnp.sum(parts, axis=0))[None], (tensors, parts.shape[1], width)
-    )
-
-    def to_all(values):
+    units = unit_rows(jnp.sum(parts, axis=0))
+    ring = tensors // halves
+    rings = [[half * ring + place for place in range(ring)] for half in range(halves)]
+    across = [[place, place + ring] for place in range(ring)]
+
+    def to_ring(values):
+        return lax.all_to_all(
+            values, "tensor", split_axis=0, concat_axis=0, tiled=True, axis_index_groups=rings
+        )
+
+    def to_tensor(values):
         return lax.all_to_all(values, "tensor", split_axis=0, concat_axis=0, tiled=True)
 
-    units, live = alone(units, live, to_all)
+    def to_half(values):
+        return lax.all_gather(values, "tensor", axis=0, tiled=True, axis_index_groups=across)
+
+    units, live = alone(jnp.broadcast_to(units[None], (ring, *units.shape)), live, to_ring)
+    units, live = alone(units, live, to_half)
     row_slot, crop_large, other_large, own_core, heads = live
     teacher_proto, center, proto_large, proto_huge = heads
     chosen = (
@@ -249,7 +361,7 @@
     )
     stats = jnp.broadcast_to(stats.reshape(1, -1, 128), (tensors, stats.size // 128, 128))
     live = (shifted, scores, student_units, kept_rows, other_rows, own_core)
-    stats, live = alone(stats, live, to_all)
+    stats, live = alone(stats, live, to_tensor)
     shifted, scores, student_units, kept_rows, other_rows, own_core = live
     stats = stats.reshape(tensors, 3, -1)
     log_t = log_total(stats[:, 0])

time: 163 us -> 161 us (0.988)
  waiting for transfers between devices: 15.1 us -> 4.7 us
  starting transfers between devices: 39.9 us -> 46.9 us
  other arithmetic: 7.94 us -> 11.7 us
  blocking collectives: 87.6 us -> 84.3 us
    all_to_all x1, waiting for transfers between devices: 8.4 us -> 0.01 us  [shards(): lax.all_to_all(weights, 'tensor', split_axis=0, concat_axis=0, tiled=True...]
    all_to_all x2, blocking collectives: 46.5 us -> 39.4 us  [the longest x1 21.4 us: to_tensor(): lax.all_to_all(values, 'tensor', split_axis=0, concat_axis=0, tiled=True)]
    ppermute x1, starting transfers between devices: 6.29 us -> 12.3 us  [shards(): student_feat = lax.ppermute(student_feat, ('group', 'tensor'), swap)]
    all_gather x0 -> x1, blocking collectives: none -> 5.18 us  [to_half(): lax.all_gather(values, 'tensor', axis=0, tiled=True, axis_index_groups=ac...]
    all_to_all x1, starting transfers between devices: 8.8 us -> 3.64 us  [to_near(): lax.all_to_all(values, 'tensor', split_axis=0, concat_axis=0, tiled=True,...]
    all_to_all x1, starting transfers between devices: 12 us -> 15.6 us  [shards(): lax.all_to_all(weights, 'tensor', split_axis=0, concat_axis=0, tiled=True...]
    all_to_all x1, blocking collectives: 19.2 us -> 16.9 us  [shards(): lax.all_to_all(sent, 'group', split_axis=0, concat_axis=0, tiled=True, ax...]
    all_to_all x1, waiting for transfers between devices: 5.18 us -> 3.14 us  [to_near(): lax.all_to_all(values, 'tensor', split_axis=0, concat_axis=0, tiled=True,...]
  transfers between devices with their start and end apart: 6 -> 6, of which waited for: 4 -> 3; matrix products, arithmetic and copies ran while one was open for 6% -> 8% of each run, Pallas kernels for 0% -> 0%
where the time goes in v5:
time: 161 us; the launch traced here: 160 us
  blocking collectives  84.3 us (52%)
  starting transfers between devices  46.9 us (29%)
  other arithmetic  11.7 us (7%)
  waiting for transfers between devices  4.7 us (3%)
  local copies, waits for them, and re-layouts  4.6 us (3%)
  between operations  3.6 us (2%)
  matrix products  2.59 us (2%)
  Pallas kernels  1.61 us (1%)
    all_to_all x1, blocking collectives, to_tensor(): lax.all_to_all(values, 'tensor', split_axis=0, concat_axis=0, tiled=True)  21.4 us
    all_to_all x1, blocking collectives, to_ring(): lax.all_to_all(values, 'tensor', split_axis=0, concat_axis=0, tiled=True,...  18 us
    all_to_all x1, blocking collectives, shards(): lax.all_to_all(sent, 'group', split_axis=0, concat_axis=0, tiled=True, ax...  16.9 us
    all_to_all x1, starting transfers between devices, shards(): lax.all_to_all(weights, 'tensor', split_axis=0, concat_axis=0, tiled=True...  15.6 us
    all_to_all x1, blocking collectives, shards(): lax.all_to_all(jnp.broadcast_to(summed.astype(jnp.bfloat16)[None], (chips...  12.5 us
    ppermute x1, starting transfers between devices, shards(): student_feat = lax.ppermute(student_feat, ('group', 'tensor'), swap)  12.3 us
    all_to_all x1, blocking collectives, to_near(): lax.all_to_all(values, 'tensor', split_axis=0, concat_axis=0, tiled=True,...  10.4 us
    ppermute x1, starting transfers between devices, shards(): lax.ppermute(jnp.concatenate([jnp.concatenate([deltas, student_units], ax...  7.33 us
  transfers between devices with their start and end apart: 6, of which 3 were waited for; matrix products, arithmetic and copies ran while one was open for 8% of the time, Pallas kernels for 0%

profile of v5, /device:TPU:1, one launch (start us, length us, event | category | flops | bytes accessed | tf_op | source)
XLA Modules:
  0.0 160.1 jit_solution(7156050831599408604)
XLA Ops:
  1.4 0.6 pad_add_fusion.flags
  2.0 1.6 %shard_map.184 = (bf16[4,208,128]{2,1,0:T(8,128)(2,1)}, bf16[16,1280]{1,0:T(8,128)(2,1)}) custom-call(s32[2]{0:T(128)} %pad_add_fusion.flags, bf16[128,256]{1,0:T(8,128)(2,1)} %teacher_w.1, bf16[32,256]{1,0:T(8,128)(2,1)} %large_w.1, bf16[40,256]{1,0:T(8,128)(2,1)} %huge_w.1, bf16[16,1024]{1,0:T(8,128)(2,1)} %large_x.1, bf16[16,1280]{1,0:T(8,128)(2,1)} %huge_x.1), custom_call_target="tpu_custom_call" | custom-call | tf_op jit(solution)/shard_map/pallas_call | solution.py:160
  3.6 15.6 %all-to-all-start.1 = ((bf16[4,208,128]{2,1,0:T(8,128)(2,1)}), bf16[4,208,128]{2,1,0:T(8,128)(2,1)S(1)}, u32[]{:S(2)}, u32[]{:S(2)}) async-start(bf16[4,208,128]{2,1,0:T(8,128)(2,1)} %get-tuple-element.99), calls=%async_computation.1 | async-start | bytes 425984 | tf_op jit(solution)/shard_map/all_to_all | solution.py:238
  19.2 12.3 %collective-permute-start = (bf16[16,1280]{1,0:T(8,128)(2,1)}, bf16[16,1280]{1,0:T(8,128)(2,1)S(1)}, u32[]{:S(2)}, u32[]{:S(2)}) collective-permute-start(bf16[16,1280]{1,0:T(8,128)(2,1)} %get-tuple-element.87), channel_id=1, source_target_pairs={{0,9},{1,8},{2,43},{3,42},{4,64},{5,74},{6,98},{7,108},{8,136},{9,... | collective-permute-start | bytes 122888 | tf_op jit(solution)/shard_map/ppermute | solution.py:223
  31.5 0.7 fusion.75
  32.3 0.7 fusion.73
  33.0 0.7 fusion.74
  33.8 1.0 convert_reduce_fusion.1
  34.7 1.1 fusion.14
  35.8 0.5 broadcast.235
  36.3 1.3 reduce.14
  38.1 0.9 fusion.16
  39.7 0.6 dynamic_slice.23
  41.9 0.7 pad_select_fusion
  42.6 0.7 maximum_maximum_fusion
  43.3 3.6 %all-to-all-start = ((bf16[8,16,512]{2,1,0:T(8,128)(2,1)}), bf16[8,16,512]{2,1,0:T(8,128)(2,1)S(1)}, u32[]{:S(2)}, u32[]{:S(2)}) async-start(bf16[8,16,512]{2,1,0:T(8,128)(2,1)} %maximum_maximum_fusion), calls=%async_computation | async-start | bytes 262144 | tf_op jit(solution)/shard_map/all_to_all | solution.py:257
  46.9 3.2 %collective-permute-start.1 = (bf16[4,208,128]{2,1,0:T(8,128)(2,1)S(1)}, bf16[4,208,128]{2,1,0:T(8,128)(2,1)S(1)}, u32[]{:S(2)}, u32[]{:S(2)}) collective-permute-start(bf16[4,208,128]{2,1,0:T(8,128)(2,1)S(1)} %all-to-all-done.1), channel_id=1, source_target_pairs={{0,32},{32,0},{64,96},{96,64},{128,160},{160,128},{192,224},{224,1... | collective-permute-start | bytes 638984 | tf_op jit(solution)/shard_map/ppermute | solution.py:246
  50.1 3.1 %all-to-all-done = bf16[8,16,512]{2,1,0:T(8,128)(2,1)S(1)} async-done(((bf16[8,16,512]{2,1,0:T(8,128)(2,1)}), bf16[8,16,512]{2,1,0:T(8,128)(2,1)S(1)}, u32[]{:S(2)}, u32[]{:S(2)}) %all-to-all-start) | async-done | bytes 131104 | tf_op jit(solution)/shard_map/all_to_all | solution.py:257
  54.0 10.4 %all_to_all.35 = f32[8,24,256]{2,1,0:T(8,128)S(1)} all-to-all(f32[8,24,256]{2,1,0:T(8,128)S(1)} %pad_maximum_fusion.2), channel_id=1, replica_groups={{0,1,2,3,16,17,18,19},{4,5,6,7,20,21,22,23},{8,9,10,11,24,25,26,27},{12..., dimensions={0} | all-to-all | bytes 393216 | tf_op jit(solution)/shard_map/all_to_all | solution.py:257
  64.7 18.0 %all_to_all.36 = bf16[16,24,256]{2,1,0:T(8,128)(2,1)S(1)} all-to-all(bf16[16,24,256]{2,1,0:T(8,128)(2,1)S(1)} %broadcast_in_dim.146), channel_id=1, replica_groups={{0,1,2,3,4,5,6,7,8,9,10,11,12,13,14,15},{16,17,18,19,20,21,22,23,24,25,..., dimensions={0} | all-to-all | bytes 393216 | tf_op jit(solution)/shard_map/all_to_all | solution.py:315
  82.6 5.2 %all_gather.3 = bf16[32,24,256]{2,1,0:T(8,128)(2,1)S(1)} all-gather(bf16[16,24,256]{2,1,0:T(8,128)(2,1)S(1)} %all_to_all.36), channel_id=1, replica_groups={{0,16},{1,17},{2,18},{3,19},{4,20},{5,21},{6,22},{7,23},{8,24},{9,25},{..., dimensions={0}, use_global_device_ids=true | all-gather | bytes 589824 | tf_op jit(solution)/shard_map/all_gather | solution.py:323
  89.1 0.5 fusion.85
  89.6 0.6 fusion.5
  90.2 21.4 %all_to_all.37 = f32[32,6,128]{2,1,0:T(8,128)S(1)} all-to-all(f32[32,6,128]{2,1,0:T(8,128)S(1)} %broadcast_in_dim.151), channel_id=1, replica_groups=mesh['group'=16,'tensor'=32] {'tensor'}, dimensions={0} | all-to-all | bytes 196608 | tf_op jit(solution)/shard_map/all_to_all | solution.py:320
  112.4 7.3 %collective-permute-start.2 = (bf16[272,1280]{1,0:T(8,128)(2,1)S(1)}, bf16[272,1280]{1,0:T(8,128)(2,1)S(1)}, u32[]{:S(2)}, u32[]{:S(2)}) collective-permute-start(bf16[272,1280]{1,0:T(8,128)(2,1)S(1)} %pad_maximum_fusion), channel_id=1, source_target_pairs={{0,32},{32,0},{64,96},{96,64},{128,160},{160,128},{192,224},{224,1... | collective-permute-start | bytes 2088968 | tf_op jit(solution)/shard_map/ppermute | solution.py:377
  120.2 1.3 collective-permute-done.2
  121.6 0.4 fusion.1
  122.0 16.9 %all_to_all.38 = bf16[8,32,1152]{2,1,0:T(8,128)(2,1)S(1)} all-to-all(bf16[8,32,1152]{2,1,0:T(8,128)(2,1)S(1)} %pad_maximum_fusion.1), channel_id=1, replica_groups={{0,64,128,192,256,320,384,448},{32,96,160,224,288,352,416,480},{1,65,12..., dimensions={0} | all-to-all | bytes 1179648 | tf_op jit(solution)/shard_map/all_to_all | solution.py:397
  139.1 12.5 %all_to_all.39 = bf16[8,32,1024]{2,1,0:T(8,128)(2,1)S(1)} all-to-all(bf16[8,32,1024]{2,1,0:T(8,128)(2,1)S(1)} %broadcast_in_dim.157), channel_id=1, replica_groups={{0,64,128,192,256,320,384,448},{32,96,160,224,288,352,416,480},{1,65,12..., dimensions={0} | all-to-all | bytes 1048576 | tf_op jit(solution)/shard_map/all_to_all | solution.py:404
  151.6 4.7 %collective-permute-start.3 = (bf16[256,1024]{1,0:T(8,128)(2,1)S(1)}, bf16[256,1024]{1,0:T(8,128)(2,1)S(1)}, u32[]{:S(2)}, u32[]{:S(2)}) collective-permute-start(bf16[256,1024]{1,0:T(8,128)(2,1)S(1)} %bitcast.92), channel_id=1, source_target_pairs={{0,32},{32,0},{64,96},{96,64},{128,160},{160,128},{192,224},{224,1... | collective-permute-start | bytes 1572872 | tf_op jit(solution)/shard_map/ppermute | solution.py:412
  156.3 0.6 convert_reduce_fusion.4
  157.9 1.1 broadcast_select_fusion
  (100 shorter events, 6.7 us)
Async XLA Ops:
  0.6 87.2 %copy-start = (bf16[256,1024]{1,0:T(8,128)(2,1)S(1)}, bf16[256,1024]{1,0:T(8,128)(2,1)}, u32[]{:S(2)}) copy-start(bf16[256,1024]{1,0:T(8,128)(2,1)} %param.20) | copy-start | bytes 1572868
  0.6 40.3 %copy-start.1 = (f32[1280]{0:T(1024)S(1)}, f32[1280]{0:T(1024)}, u32[]{:S(2)}) copy-start(f32[1280]{0:T(1024)} %param.27) | copy-start | bytes 15364
  1.4 40.1 %copy-start.3 = (f32[1024]{0:T(1024)S(1)}, f32[1024]{0:T(1024)}, u32[]{:S(2)}) copy-start(f32[1024]{0:T(1024)} %param.26) | copy-start | bytes 12292
  3.6 39.7 %all-to-all-start.1 = ((bf16[4,208,128]{2,1,0:T(8,128)(2,1)}), bf16[4,208,128]{2,1,0:T(8,128)(2,1)S(1)}, u32[]{:S(2)}, u32[]{:S(2)}) async-start(bf16[4,208,128]{2,1,0:T(8,128)(2,1)} %get-tuple-element.99), calls=%async_computation.1 | async-start | bytes 425984 | tf_op jit(solution)/shard_map/all_to_all | solution.py:238
  19.2 21.1 %collective-permute-start = (bf16[16,1280]{1,0:T(8,128)(2,1)}, bf16[16,1280]{1,0:T(8,128)(2,1)S(1)}, u32[]{:S(2)}, u32[]{:S(2)}) collective-permute-start(bf16[16,1280]{1,0:T(8,128)(2,1)} %get-tuple-element.87), channel_id=1, source_target_pairs={{0,9},{1,8},{2,43},{3,42},{4,64},{5,74},{6,98},{7,108},{8,136},{9,... | collective-permute-start | bytes 122888 | tf_op jit(solution)/shard_map/ppermute | solution.py:223
  43.3 10.0 %all-to-all-start = ((bf16[8,16,512]{2,1,0:T(8,128)(2,1)}), bf16[8,16,512]{2,1,0:T(8,128)(2,1)S(1)}, u32[]{:S(2)}, u32[]{:S(2)}) async-start(bf16[8,16,512]{2,1,0:T(8,128)(2,1)} %maximum_maximum_fusion), calls=%async_computation | async-start | bytes 262144 | tf_op jit(solution)/shard_map/all_to_all | solution.py:257
  46.9 6.4 %collective-permute-start.1 = (bf16[4,208,128]{2,1,0:T(8,128)(2,1)S(1)}, bf16[4,208,128]{2,1,0:T(8,128)(2,1)S(1)}, u32[]{:S(2)}, u32[]{:S(2)}) collective-permute-start(bf16[4,208,128]{2,1,0:T(8,128)(2,1)S(1)} %all-to-all-done.1), channel_id=1, source_target_pairs={{0,32},{32,0},{64,96},{96,64},{128,160},{160,128},{192,224},{224,1... | collective-permute-start | bytes 638984 | tf_op jit(solution)/shard_map/ppermute | solution.py:246
  64.4 23.4 %copy-start.2 = (f32[1024]{0:T(1024)S(1)}, f32[1024]{0:T(1024)}, u32[]{:S(2)}) copy-start(f32[1024]{0:T(1024)} %param.21) | copy-start | bytes 12292
  87.9 1.0 copy-start.4
  87.9 1.2 copy-start.5
  112.4 9.1 %collective-permute-start.2 = (bf16[272,1280]{1,0:T(8,128)(2,1)S(1)}, bf16[272,1280]{1,0:T(8,128)(2,1)S(1)}, u32[]{:S(2)}, u32[]{:S(2)}) collective-permute-start(bf16[272,1280]{1,0:T(8,128)(2,1)S(1)} %pad_maximum_fusion), channel_id=1, source_target_pairs={{0,32},{32,0},{64,96},{96,64},{128,160},{160,128},{192,224},{224,1... | collective-permute-start | bytes 2088968 | tf_op jit(solution)/shard_map/ppermute | solution.py:377
  151.6 6.3 %collective-permute-start.3 = (bf16[256,1024]{1,0:T(8,128)(2,1)S(1)}, bf16[256,1024]{1,0:T(8,128)(2,1)S(1)}, u32[]{:S(2)}, u32[]{:S(2)}) collective-permute-start(bf16[256,1024]{1,0:T(8,128)(2,1)S(1)} %bitcast.92), channel_id=1, source_target_pairs={{0,32},{32,0},{64,96},{96,64},{128,160},{160,128},{192,224},{224,1... | collective-permute-start | bytes 1572872 | tf_op jit(solution)/shard_map/ppermute | solution.py:412

commit v6 on v5

--- a/solution.py
+++ b/solution.py
@@ -15,14 +15,6 @@
 EPSILON = 1e-06
 
 
-def layer_norm(values, gains):
-    widened = values.astype(jnp.float32)
-    row_mean = jnp.mean(widened, axis=-1, keepdims=True)
-    centred = widened - row_mean
-    spread = jnp.mean(centred * centred, axis=-1, keepdims=True)
-    return (centred * lax.rsqrt(spread + EPSILON) * gains).astype(jnp.bfloat16)
-
-
 def unit_rows(middle):
     return (middle * lax.rsqrt(jnp.mean(middle * middle, axis=-1, keepdims=True) + EPSILON)).astype(
         jnp.bfloat16
@@ -37,12 +29,6 @@
 def log_total(logs):
     top = jnp.max(logs, axis=0)
     return top + jnp.log(jnp.sum(jnp.exp(logs - top[None, :]), axis=0))
-
-
-def by_near(columns, halves):
-    rows, tensors, wide = columns.shape
-    columns = columns.reshape(rows, halves, FAR, FAR, wide).transpose(1, 3, 0, 2, 4)
-    return columns.reshape(tensors // FAR, rows, FAR * wide)
 
 
 def parts_of(values):
@@ -136,36 +122,89 @@
     ]
 
 
-def prepare_kernel(flags, teacher_w, large_w, huge_w, large_x, huge_x, weights, student):
+def normed_rows(values, gains):
+    row_mean = jnp.mean(values, axis=-1, keepdims=True)
+    centred = values - row_mean
+    spread = jnp.mean(centred * centred, axis=-1, keepdims=True)
+    return centred * lax.rsqrt(spread + EPSILON) * gains
+
+
+def near_columns(values, tensors, dest):
+    wide = values.shape[1] // tensors
+    half, low = dest // FAR, dest % FAR
+    places = [(half * FAR + place) * FAR + low for place in range(FAR)]
+    return [values[:, place * wide : (place + 1) * wide] for place in places]
+
+
+def prepare_kernel(
+    teacher_w, large_w, huge_w, teacher_x, gain, weights, sent
+):
+    own_group = lax.axis_index("group")
     half = weights.shape[2]
     first, second, third = teacher_w.shape[0], large_w.shape[0], huge_w.shape[0]
-    low_core = flags[0] == 0
+    low_core = lax.rem(own_group, 2) == 0
     spare = weights.shape[1] - first - second - third
     end = jnp.concatenate([huge_w[...], jnp.zeros((spare, 2 * half), huge_w.dtype)], axis=0)
     for start, rows in ((0, teacher_w[...]), (first, large_w[...]), (first + second, end)):
         kept = jnp.where(low_core, rows[:, :half], rows[:, half:])
         for place in range(FAR):
             weights[place, start : start + rows.shape[0], :] = kept
-    slim = large_x.shape[1]
-    is_large = flags[1] != 0
-    student[:, :slim] = jnp.where(is_large, large_x[...], huge_x[:, :slim])
-    student[:, slim:] = jnp.where(is_large, jnp.zeros_like(huge_x[:, slim:]), huge_x[:, slim:])
-
-
-def prepare(own_core, is_large, teacher_w, large_w, huge_w, large_x, huge_x):
+    normed = normed_rows(teacher_x[...].astype(jnp.float32), gain[...]).astype(jnp.bfloat16)
+    tensors = sent.shape[0] * FAR
+    for dest in range(sent.shape[0]):
+        sent[dest] = jnp.concatenate(near_columns(normed, tensors, dest), axis=1)
+
+
+def prepare(teacher_w, large_w, huge_w, teacher_x, gain, near):
     rows = teacher_w.shape[0] + large_w.shape[0] + huge_w.shape[0]
     rows += -rows % 16
-    flags = jnp.stack([own_core.astype(jnp.int32), is_large.astype(jnp.int32)])
     whole = pl.BlockSpec(memory_space=pltpu.VMEM)
     return pl.pallas_call(
         prepare_kernel,
         out_shape=(
             jax.ShapeDtypeStruct((FAR, rows, teacher_w.shape[1] // 2), jnp.bfloat16),
-            jax.ShapeDtypeStruct(huge_x.shape, jnp.bfloat16),
+            jax.ShapeDtypeStruct((near, teacher_x.shape[0], teacher_x.shape[1] // near), jnp.bfloat16),
         ),
-        in_specs=[pl.BlockSpec(memory_space=pltpu.SMEM)] + [whole] * 5,
+        in_specs=[whole] * 5,
         out_specs=(whole, whole),
-    )(flags, teacher_w, large_w, huge_w, large_x, huge_x)
+    )(teacher_w, large_w, huge_w, teacher_x, gain.reshape(1, -1))
+
+
+def student_kernel(large_groups, owners, student, gain_large, gain_huge, teacher, sent):
+    own_group, own_tensor = lax.axis_index("group"), lax.axis_index("tensor")
+    groups, tensors = owners.shape
+    is_large = owners[own_group, own_tensor] // (tensors // groups) < large_groups[0]
+    rows = teacher.shape[1]
+
+    def send(normed):
+        for dest in range(sent.shape[0]):
+            columns = near_columns(normed, tensors, dest)
+            filled = FAR * columns[0].shape[1]
+            columns.append(jnp.zeros((2 * rows, sent.shape[2] // 2 - filled), jnp.float32))
+            block = jnp.concatenate(columns, axis=1)
+            block = jnp.concatenate([block[:rows], block[rows:]], axis=1)
+            block = jnp.concatenate([teacher[dest].astype(jnp.float32), block], axis=0)
+            sent[dest] = block.astype(jnp.bfloat16)
+
+    @pl.when(is_large)
+    def _():
+        send(normed_rows(student[:, : gain_large.shape[1]].astype(jnp.float32), gain_large[...]))
+
+    @pl.when(jnp.logical_not(is_large))
+    def _():
+        send(normed_rows(student[...].astype(jnp.float32), gain_huge[...]))
+
+
+def student_columns(large_groups, owners, student, gain_large, gain_huge, teacher):
+    near, rows, wide = teacher.shape
+    whole = pl.BlockSpec(memory_space=pltpu.VMEM)
+    scalars = pl.BlockSpec(memory_space=pltpu.SMEM)
+    return pl.pallas_call(
+        student_kernel,
+        out_shape=jax.ShapeDtypeStruct((near, 2 * rows, wide), jnp.bfloat16),
+        in_specs=[scalars, scalars] + [whole] * 4,
+        out_specs=whole,
+    )(large_groups, owners, student, gain_large.reshape(1, -1), gain_huge.reshape(1, -1), teacher)
 
 
 def shards(
@@ -207,10 +246,10 @@
     ]
     pairs = [(g, g ^ 1) for g in range(groups)]
 
-    is_large = own_group < large_groups[0]
-    wide = feat_huge.shape[1]
-    weights, student_feat = prepare(
-        own_core, is_large, teacher_proj, proj_large, proj_huge, feat_large, feat_huge
+    padded_large = jnp.pad(feat_large, ((0, 0), (0, feat_huge.shape[1] - feat_large.shape[1])))
+    student_feat = jnp.where(own_group < large_groups[0], padded_large, feat_huge)
+    weights, teacher_sent = prepare(
+        teacher_proj, proj_large, proj_huge, teacher_feat, teacher_gain, near
     )
     places = slot_places(groups, tensors)
     owners = [[row.index(place) for place in range(tensors)] for row in places]
@@ -221,19 +260,9 @@
         for k in range(slots_per)
     ]
     student_feat = lax.ppermute(student_feat, ("group", "tensor"), swap)
-    teacher_normed = layer_norm(teacher_feat, teacher_gain)
     places, owners = jnp.array(places, jnp.int32), jnp.array(owners, jnp.int32)
     own_owners = lax.dynamic_index_in_dim(owners, own_group, 0, keepdims=False)
     large_places = own_owners // slots_per < large_groups[0]
-    row_large = lax.dynamic_index_in_dim(large_places, own_tensor, 0, keepdims=False)
-    slim = feat_large.shape[1]
-    student_rows = student_feat.shape[0]
-    normed_large = layer_norm(student_feat[:, :slim], gain_large)
-    normed_large = by_near(normed_large.reshape(student_rows, tensors, -1), halves)
-    normed_large = jnp.pad(normed_large, ((0, 0), (0, 0), (0, (wide - slim) // near)))
-    normed_huge = layer_norm(student_feat, gain_huge)
-    normed_huge = by_near(normed_huge.reshape(student_rows, tensors, -1), halves)
-    student_normed = jnp.where(row_large, normed_large, normed_huge)
 
     held = lax.all_to_all(
         weights,
@@ -245,13 +274,11 @@
     )
     lent = lax.ppermute(held, "group", pairs)
 
-    teacher_rows = teacher_feat.shape[0]
+    teacher_rows, wide = teacher_feat.shape[0], feat_huge.shape[1]
     piece = teacher_feat.shape[1] // near
-    slot_pad = piece // 2 - wide // near
-    teacher_sent = by_near(teacher_normed.reshape(teacher_rows, tensors, -1), halves)
-    student_sent = jnp.pad(student_normed, ((0, 0), (0, 0), (0, slot_pad)))
-    half = student_rows // 2
-    student_sent = jnp.concatenate([student_sent[:, :half], student_sent[:, half:]], axis=2)
+    sent = student_columns(
+        large_groups, owners, student_feat, gain_large, gain_huge, teacher_sent
+    )
 
     def to_near(values):
         return lax.all_to_all(
@@ -270,7 +297,7 @@
     ).reshape(-1)
     heads = (teacher_proto, center, proto_large, proto_huge)
     live = (row_slot, crop_large, other_large, near_large, own_core, heads)
-    cols, live = alone(jnp.concatenate([teacher_sent, student_sent], axis=1), live, to_near)
+    cols, live = alone(sent, live, to_near)
     cols, held, lent = lax.optimization_barrier((cols, held, lent))
     row_slot, crop_large, other_large, near_large, own_core, heads = live
     held = jnp.concatenate(

time: 161 us -> 157 us (0.975)
  other arithmetic: 11.7 us -> 6.17 us
  blocking collectives: 84.3 us -> 80.5 us
  waiting for transfers between devices: 4.7 us -> 8.14 us
  Pallas kernels: 1.61 us -> 3.64 us
    all_to_all x1, starting transfers between devices: 15.6 us -> 4.62 us  [shards(): lax.all_to_all(weights, 'tensor', split_axis=0, concat_axis=0, tiled=True...]
    all_to_all x1, starting transfers between devices: 3.64 us -> 9.9 us  [to_near(): lax.all_to_all(values, 'tensor', split_axis=0, concat_axis=0, tiled=True,...]
    all_to_all x1, waiting for transfers between devices: 0.01 us -> 4.44 us  [shards(): lax.all_to_all(weights, 'tensor', split_axis=0, concat_axis=0, tiled=True...]
    ppermute x1, starting transfers between devices: 12.3 us -> 15.9 us  [shards(): student_feat = lax.ppermute(student_feat, ('group', 'tensor'), swap)]
    reduce_sum x6 -> x0, other arithmetic: 2.67 us -> none  [the longest x3 1.44 us: layer_norm(): spread = jnp.mean(centred * centred, axis=-1, keepdims=True)]
    all_to_all x1, blocking collectives: 18 us -> 15.4 us  [to_ring(): lax.all_to_all(values, 'tensor', split_axis=0, concat_axis=0, tiled=True,...]
    all_to_all x1, blocking collectives: 16.9 us -> 14.7 us  [shards(): lax.all_to_all(sent, 'group', split_axis=0, concat_axis=0, tiled=True, ax...]
    pallas_call x0 -> x1, Pallas kernels: none -> 1.88 us  [student_columns(): pl.pallas_call(student_kernel, out_shape=jax.ShapeDtypeStruct((near, 2 *...]
  transfers between devices with their start and end apart: 6 -> 6, of which waited for: 3 -> 4; matrix products, arithmetic and copies ran while one was open for 8% -> 4% of each run, Pallas kernels for 0% -> 2%
where the time goes in v6:
time: 157 us; the launch traced here: 156 us
  blocking collectives  80.5 us (51%)
  starting transfers between devices  46.8 us (30%)
  waiting for transfers between devices  8.14 us (5%)
  other arithmetic  6.17 us (4%)
  local copies, waits for them, and re-layouts  5.17 us (3%)
  Pallas kernels  3.64 us (2%)
  between operations  3.47 us (2%)
  matrix products  2.59 us (2%)
    all_to_all x1, blocking collectives, to_tensor(): lax.all_to_all(values, 'tensor', split_axis=0, concat_axis=0, tiled=True)  21.4 us
    ppermute x1, starting transfers between devices, shards(): student_feat = lax.ppermute(student_feat, ('group', 'tensor'), swap)  15.9 us
    all_to_all x1, blocking collectives, to_ring(): lax.all_to_all(values, 'tensor', split_axis=0, concat_axis=0, tiled=True,...  15.4 us
    all_to_all x1, blocking collectives, shards(): lax.all_to_all(sent, 'group', split_axis=0, concat_axis=0, tiled=True, ax...  14.7 us
    all_to_all x1, blocking collectives, shards(): lax.all_to_all(jnp.broadcast_to(summed.astype(jnp.bfloat16)[None], (chips...  12.5 us
    all_to_all x1, blocking collectives, to_near(): lax.all_to_all(values, 'tensor', split_axis=0, concat_axis=0, tiled=True,...  11.4 us
    all_to_all x1, starting transfers between devices, to_near(): lax.all_to_all(values, 'tensor', split_axis=0, concat_axis=0, tiled=True,...  9.9 us
    ppermute x1, starting transfers between devices, shards(): lax.ppermute(jnp.concatenate([jnp.concatenate([deltas, student_units], ax...  7.33 us
  transfers between devices with their start and end apart: 6, of which 4 were waited for; matrix products, arithmetic and copies ran while one was open for 4% of the time, Pallas kernels for 2%

profile of v6, /device:TPU:1, one launch (start us, length us, event | category | flops | bytes accessed | tf_op | source)
XLA Modules:
  0.0 156.5 jit_solution(17705055898255270222)
XLA Ops:
  1.4 0.8 pad_select_fusion
  2.1 15.9 %collective-permute-start = (bf16[16,1280]{1,0:T(8,128)(2,1)S(1)}, bf16[16,1280]{1,0:T(8,128)(2,1)S(1)}, u32[]{:S(2)}, u32[]{:S(2)}) collective-permute-start(bf16[16,1280]{1,0:T(8,128)(2,1)S(1)} %pad_select_fusion), channel_id=1, source_target_pairs={{0,9},{1,8},{2,43},{3,42},{4,64},{5,74},{6,98},{7,108},{8,136},{9,... | collective-permute-start | bytes 122888 | tf_op jit(solution)/shard_map/ppermute | solution.py:262
  18.1 1.8 %shard_map.184 = (bf16[4,208,128]{2,1,0:T(8,128)(2,1)}, bf16[8,8,512]{2,1,0:T(8,128)(2,1)}) custom-call(bf16[128,256]{1,0:T(8,128)(2,1)} %teacher_w.1, bf16[32,256]{1,0:T(8,128)(2,1)} %large_w.1, bf16[40,256]{1,0:T(8,128)(2,1)} %huge_w.1, bf16[8,4096]{1,0:T(8,128)(2,1)} %teacher_x.1, f32[1,4096]{1,0:T(1,128)} %bitcast.80), custom_call_target="tpu_custom_call" | custom-call | tf_op jit(solution)/shard_map/pallas_call | solution.py:162
  19.8 4.6 %all-to-all-start.1 = ((bf16[4,208,128]{2,1,0:T(8,128)(2,1)}), bf16[4,208,128]{2,1,0:T(8,128)(2,1)S(1)}, u32[]{:S(2)}, u32[]{:S(2)}) async-start(bf16[4,208,128]{2,1,0:T(8,128)(2,1)} %get-tuple-element.99), calls=%async_computation.1 | async-start | bytes 425984 | tf_op jit(solution)/shard_map/all_to_all | solution.py:267
  24.5 0.7 fusion.58
  25.2 0.7 fusion.59
  26.0 0.5 broadcast.142
  26.5 1.3 reduce.14
  28.4 1.3 reshape.244.gain_huge
  30.3 0.6 copy-done.1
  30.9 1.9 %shard_map.185 = bf16[8,16,512]{2,1,0:T(8,128)(2,1)} custom-call(s32[1]{0:T(128)} %copy.40.large_groups, s32[16,32]{1,0:T(8,128)} %constant.104.clone.owners, bf16[16,1280]{1,0:T(8,128)(2,1)} %copy-done.1, f32[1,1024]{1,0:T(1,128)} %bitcast.81, f32[1,1280]{1,0:T(1,128)} %reshape.244.gain_huge, bf16[8,8,512]{2,1,0:T(8,128)(2,1)} %get-tuple-element.87.teacher), custom_call_target="tpu_custom_call" | custom-call | tf_op jit(solution)/shard_map/pallas_call | solution.py:202
  32.8 4.4 %all-to-all-done.1 = bf16[4,208,128]{2,1,0:T(8,128)(2,1)S(1)} async-done(((bf16[4,208,128]{2,1,0:T(8,128)(2,1)}), bf16[4,208,128]{2,1,0:T(8,128)(2,1)S(1)}, u32[]{:S(2)}, u32[]{:S(2)}) %all-to-all-start.1) | async-done | bytes 213024 | tf_op jit(solution)/shard_map/all_to_all | solution.py:267
  37.2 9.9 %all-to-all-start = ((bf16[8,16,512]{2,1,0:T(8,128)(2,1)}), bf16[8,16,512]{2,1,0:T(8,128)(2,1)S(1)}, u32[]{:S(2)}, u32[]{:S(2)}) async-start(bf16[8,16,512]{2,1,0:T(8,128)(2,1)} %shard_map.185), calls=%async_computation | async-start | bytes 262144 | tf_op jit(solution)/shard_map/all_to_all | solution.py:284
  47.1 4.2 %collective-permute-start.1 = (bf16[4,208,128]{2,1,0:T(8,128)(2,1)S(1)}, bf16[4,208,128]{2,1,0:T(8,128)(2,1)S(1)}, u32[]{:S(2)}, u32[]{:S(2)}) collective-permute-start(bf16[4,208,128]{2,1,0:T(8,128)(2,1)S(1)} %all-to-all-done.1), channel_id=1, source_target_pairs={{0,32},{32,0},{64,96},{96,64},{128,160},{160,128},{192,224},{224,1... | collective-permute-start | bytes 638984 | tf_op jit(solution)/shard_map/ppermute | solution.py:275
  51.3 2.1 %all-to-all-done = bf16[8,16,512]{2,1,0:T(8,128)(2,1)S(1)} async-done(((bf16[8,16,512]{2,1,0:T(8,128)(2,1)}), bf16[8,16,512]{2,1,0:T(8,128)(2,1)S(1)}, u32[]{:S(2)}, u32[]{:S(2)}) %all-to-all-start) | async-done | bytes 131104 | tf_op jit(solution)/shard_map/all_to_all | solution.py:284
  54.2 11.4 %all_to_all.35 = f32[8,24,256]{2,1,0:T(8,128)S(1)} all-to-all(f32[8,24,256]{2,1,0:T(8,128)S(1)} %pad_maximum_fusion.2), channel_id=1, replica_groups={{0,1,2,3,16,17,18,19},{4,5,6,7,20,21,22,23},{8,9,10,11,24,25,26,27},{12..., dimensions={0} | all-to-all | bytes 393216 | tf_op jit(solution)/shard_map/all_to_all | solution.py:284
  65.9 15.4 %all_to_all.36 = bf16[16,24,256]{2,1,0:T(8,128)(2,1)S(1)} all-to-all(bf16[16,24,256]{2,1,0:T(8,128)(2,1)S(1)} %broadcast_in_dim.137), channel_id=1, replica_groups={{0,1,2,3,4,5,6,7,8,9,10,11,12,13,14,15},{16,17,18,19,20,21,22,23,24,25,..., dimensions={0} | all-to-all | bytes 393216 | tf_op jit(solution)/shard_map/all_to_all | solution.py:342
  81.3 5.2 %all_gather.3 = bf16[32,24,256]{2,1,0:T(8,128)(2,1)S(1)} all-gather(bf16[16,24,256]{2,1,0:T(8,128)(2,1)S(1)} %all_to_all.36), channel_id=1, replica_groups={{0,16},{1,17},{2,18},{3,19},{4,20},{5,21},{6,22},{7,23},{8,24},{9,25},{..., dimensions={0}, use_global_device_ids=true | all-gather | bytes 589824 | tf_op jit(solution)/shard_map/all_gather | solution.py:350
  86.6 0.4 fusion.70
  87.7 0.5 fusion.69
  88.3 0.6 fusion.5
  88.9 21.4 %all_to_all.37 = f32[32,6,128]{2,1,0:T(8,128)S(1)} all-to-all(f32[32,6,128]{2,1,0:T(8,128)S(1)} %broadcast_in_dim.142), channel_id=1, replica_groups=mesh['group'=16,'tensor'=32] {'tensor'}, dimensions={0} | all-to-all | bytes 196608 | tf_op jit(solution)/shard_map/all_to_all | solution.py:347
  110.6 0.4 multiply_convert_fusion
  111.1 7.3 %collective-permute-start.2 = (bf16[272,1280]{1,0:T(8,128)(2,1)S(1)}, bf16[272,1280]{1,0:T(8,128)(2,1)S(1)}, u32[]{:S(2)}, u32[]{:S(2)}) collective-permute-start(bf16[272,1280]{1,0:T(8,128)(2,1)S(1)} %pad_maximum_fusion), channel_id=1, source_target_pairs={{0,32},{32,0},{64,96},{96,64},{128,160},{160,128},{192,224},{224,1... | collective-permute-start | bytes 2088968 | tf_op jit(solution)/shard_map/ppermute | solution.py:404
  118.4 0.4 fusion.13
  118.9 1.3 collective-permute-done.2
  120.2 0.4 fusion.1
  120.7 14.7 %all_to_all.38 = bf16[8,32,1152]{2,1,0:T(8,128)(2,1)S(1)} all-to-all(bf16[8,32,1152]{2,1,0:T(8,128)(2,1)S(1)} %pad_maximum_fusion.1), channel_id=1, replica_groups={{0,64,128,192,256,320,384,448},{32,96,160,224,288,352,416,480},{1,65,12..., dimensions={0} | all-to-all | bytes 1179648 | tf_op jit(solution)/shard_map/all_to_all | solution.py:424
  135.5 12.5 %all_to_all.39 = bf16[8,32,1024]{2,1,0:T(8,128)(2,1)S(1)} all-to-all(bf16[8,32,1024]{2,1,0:T(8,128)(2,1)S(1)} %broadcast_in_dim.148), channel_id=1, replica_groups={{0,64,128,192,256,320,384,448},{32,96,160,224,288,352,416,480},{1,65,12..., dimensions={0} | all-to-all | bytes 1048576 | tf_op jit(solution)/shard_map/all_to_all | solution.py:431
  148.0 4.7 %collective-permute-start.3 = (bf16[256,1024]{1,0:T(8,128)(2,1)S(1)}, bf16[256,1024]{1,0:T(8,128)(2,1)S(1)}, u32[]{:S(2)}, u32[]{:S(2)}) collective-permute-start(bf16[256,1024]{1,0:T(8,128)(2,1)S(1)} %bitcast.74), channel_id=1, source_target_pairs={{0,32},{32,0},{64,96},{96,64},{128,160},{160,128},{192,224},{224,1... | collective-permute-start | bytes 1572872 | tf_op jit(solution)/shard_map/ppermute | solution.py:439
  152.8 0.6 convert_reduce_fusion.1
  154.3 1.1 broadcast_select_fusion
  (73 shorter events, 3.9 us)
Async XLA Ops:
  0.6 85.9 %copy-start = (bf16[256,1024]{1,0:T(8,128)(2,1)S(1)}, bf16[256,1024]{1,0:T(8,128)(2,1)}, u32[]{:S(2)}) copy-start(bf16[256,1024]{1,0:T(8,128)(2,1)} %param.20) | copy-start | bytes 1572868
  2.1 28.1 %collective-permute-start = (bf16[16,1280]{1,0:T(8,128)(2,1)S(1)}, bf16[16,1280]{1,0:T(8,128)(2,1)S(1)}, u32[]{:S(2)}, u32[]{:S(2)}) collective-permute-start(bf16[16,1280]{1,0:T(8,128)(2,1)S(1)} %pad_select_fusion), channel_id=1, source_target_pairs={{0,9},{1,8},{2,43},{3,42},{4,64},{5,74},{6,98},{7,108},{8,136},{9,... | collective-permute-start | bytes 122888 | tf_op jit(solution)/shard_map/ppermute | solution.py:262
  19.8 17.4 %all-to-all-start.1 = ((bf16[4,208,128]{2,1,0:T(8,128)(2,1)}), bf16[4,208,128]{2,1,0:T(8,128)(2,1)S(1)}, u32[]{:S(2)}, u32[]{:S(2)}) async-start(bf16[4,208,128]{2,1,0:T(8,128)(2,1)} %get-tuple-element.99), calls=%async_computation.1 | async-start | bytes 425984 | tf_op jit(solution)/shard_map/all_to_all | solution.py:267
  30.3 0.6 copy-start.1
  37.2 16.3 %all-to-all-start = ((bf16[8,16,512]{2,1,0:T(8,128)(2,1)}), bf16[8,16,512]{2,1,0:T(8,128)(2,1)S(1)}, u32[]{:S(2)}, u32[]{:S(2)}) async-start(bf16[8,16,512]{2,1,0:T(8,128)(2,1)} %shard_map.185), calls=%async_computation | async-start | bytes 262144 | tf_op jit(solution)/shard_map/all_to_all | solution.py:284
  47.1 6.4 %collective-permute-start.1 = (bf16[4,208,128]{2,1,0:T(8,128)(2,1)S(1)}, bf16[4,208,128]{2,1,0:T(8,128)(2,1)S(1)}, u32[]{:S(2)}, u32[]{:S(2)}) collective-permute-start(bf16[4,208,128]{2,1,0:T(8,128)(2,1)S(1)} %all-to-all-done.1), channel_id=1, source_target_pairs={{0,32},{32,0},{64,96},{96,64},{128,160},{160,128},{192,224},{224,1... | collective-permute-start | bytes 638984 | tf_op jit(solution)/shard_map/ppermute | solution.py:275
  65.6 20.9 %copy-start.2 = (f32[1024]{0:T(1024)S(1)}, f32[1024]{0:T(1024)}, u32[]{:S(2)}) copy-start(f32[1024]{0:T(1024)} %param.21) | copy-start | bytes 12292
  86.5 1.0 copy-start.3
  86.5 1.2 copy-start.4
  111.1 9.1 %collective-permute-start.2 = (bf16[272,1280]{1,0:T(8,128)(2,1)S(1)}, bf16[272,1280]{1,0:T(8,128)(2,1)S(1)}, u32[]{:S(2)}, u32[]{:S(2)}) collective-permute-start(bf16[272,1280]{1,0:T(8,128)(2,1)S(1)} %pad_maximum_fusion), channel_id=1, source_target_pairs={{0,32},{32,0},{64,96},{96,64},{128,160},{160,128},{192,224},{224,1... | collective-permute-start | bytes 2088968 | tf_op jit(solution)/shard_map/ppermute | solution.py:404
  148.0 6.3 %collective-permute-start.3 = (bf16[256,1024]{1,0:T(8,128)(2,1)S(1)}, bf16[256,1024]{1,0:T(8,128)(2,1)S(1)}, u32[]{:S(2)}, u32[]{:S(2)}) collective-permute-start(bf16[256,1024]{1,0:T(8,128)(2,1)S(1)} %bitcast.74), channel_id=1, source_target_pairs={{0,32},{32,0},{64,96},{96,64},{128,160},{160,128},{192,224},{224,1... | collective-permute-start | bytes 1572872 | tf_op jit(solution)/shard_map/ppermute | solution.py:439

commit v7 on v6

--- a/solution.py
+++ b/solution.py
@@ -149,7 +149,7 @@
         kept = jnp.where(low_core, rows[:, :half], rows[:, half:])
         for place in range(FAR):
             weights[place, start : start + rows.shape[0], :] = kept
-    normed = normed_rows(teacher_x[...].astype(jnp.float32), gain[...]).astype(jnp.bfloat16)
+    normed = normed_rows(teacher_x[...].astype(jnp.float32), gain[...])
     tensors = sent.shape[0] * FAR
     for dest in range(sent.shape[0]):
         sent[dest] = jnp.concatenate(near_columns(normed, tensors, dest), axis=1)
@@ -163,7 +163,7 @@
         prepare_kernel,
         out_shape=(
             jax.ShapeDtypeStruct((FAR, rows, teacher_w.shape[1] // 2), jnp.bfloat16),
-            jax.ShapeDtypeStruct((near, teacher_x.shape[0], teacher_x.shape[1] // near), jnp.bfloat16),
+            jax.ShapeDtypeStruct((near, teacher_x.shape[0], teacher_x.shape[1] // near), jnp.float32),
         ),
         in_specs=[whole] * 5,
         out_specs=(whole, whole),
@@ -183,7 +183,7 @@
             columns.append(jnp.zeros((2 * rows, sent.shape[2] // 2 - filled), jnp.float32))
             block = jnp.concatenate(columns, axis=1)
             block = jnp.concatenate([block[:rows], block[rows:]], axis=1)
-            block = jnp.concatenate([teacher[dest].astype(jnp.float32), block], axis=0)
+            block = jnp.concatenate([teacher[dest], block], axis=0)
             sent[dest] = block.astype(jnp.bfloat16)
 
     @pl.when(is_large)

time: 157 us -> 157 us (level)
  no operation moved by 1% of the time
where the time goes in v7:
time: 157 us; the launch traced here: 156 us
  blocking collectives  80.5 us (51%)
  starting transfers between devices  46.8 us (30%)
  waiting for transfers between devices  8 us (5%)
  other arithmetic  6.21 us (4%)
  local copies, waits for them, and re-layouts  5.24 us (3%)
  Pallas kernels  3.7 us (2%)
  between operations  3.47 us (2%)
  matrix products  2.6 us (2%)
    all_to_all x1, blocking collectives, to_tensor(): lax.all_to_all(values, 'tensor', split_axis=0, concat_axis=0, tiled=True)  21.4 us
    ppermute x1, starting transfers between devices, shards(): student_feat = lax.ppermute(student_feat, ('group', 'tensor'), swap)  15.9 us
    all_to_all x1, blocking collectives, to_ring(): lax.all_to_all(values, 'tensor', split_axis=0, concat_axis=0, tiled=True,...  15.4 us
    all_to_all x1, blocking collectives, shards(): lax.all_to_all(sent, 'group', split_axis=0, concat_axis=0, tiled=True, ax...  14.6 us
    all_to_all x1, blocking collectives, shards(): lax.all_to_all(jnp.broadcast_to(summed.astype(jnp.bfloat16)[None], (chips...  12.5 us
    all_to_all x1, blocking collectives, to_near(): lax.all_to_all(values, 'tensor', split_axis=0, concat_axis=0, tiled=True,...  11.4 us
    all_to_all x1, starting transfers between devices, to_near(): lax.all_to_all(values, 'tensor', split_axis=0, concat_axis=0, tiled=True,...  9.88 us
    ppermute x1, starting transfers between devices, shards(): lax.ppermute(jnp.concatenate([jnp.concatenate([deltas, student_units], ax...  7.33 us
  transfers between devices with their start and end apart: 6, of which 4 were waited for; matrix products, arithmetic and copies ran while one was open for 4% of the time, Pallas kernels for 2%

profile of v7, /device:TPU:1, one launch (start us, length us, event | category | flops | bytes accessed | tf_op | source)
XLA Modules:
  0.0 156.5 jit_solution(6198912061955228726)
XLA Ops:
  1.4 0.8 pad_select_fusion
  2.1 15.9 %collective-permute-start = (bf16[16,1280]{1,0:T(8,128)(2,1)S(1)}, bf16[16,1280]{1,0:T(8,128)(2,1)S(1)}, u32[]{:S(2)}, u32[]{:S(2)}) collective-permute-start(bf16[16,1280]{1,0:T(8,128)(2,1)S(1)} %pad_select_fusion), channel_id=1, source_target_pairs={{0,9},{1,8},{2,43},{3,42},{4,64},{5,74},{6,98},{7,108},{8,136},{9,... | collective-permute-start | bytes 122888 | tf_op jit(solution)/shard_map/ppermute | solution.py:262
  18.1 1.8 %shard_map.184 = (bf16[4,208,128]{2,1,0:T(8,128)(2,1)}, f32[8,8,512]{2,1,0:T(8,128)}) custom-call(bf16[128,256]{1,0:T(8,128)(2,1)} %teacher_w.1, bf16[32,256]{1,0:T(8,128)(2,1)} %large_w.1, bf16[40,256]{1,0:T(8,128)(2,1)} %huge_w.1, bf16[8,4096]{1,0:T(8,128)(2,1)} %teacher_x.1, f32[1,4096]{1,0:T(1,128)} %bitcast.80), custom_call_target="tpu_custom_call" | custom-call | tf_op jit(solution)/shard_map/pallas_call | solution.py:162
  19.9 4.6 %all-to-all-start.1 = ((bf16[4,208,128]{2,1,0:T(8,128)(2,1)}), bf16[4,208,128]{2,1,0:T(8,128)(2,1)S(1)}, u32[]{:S(2)}, u32[]{:S(2)}) async-start(bf16[4,208,128]{2,1,0:T(8,128)(2,1)} %get-tuple-element.99), calls=%async_computation.1 | async-start | bytes 425984 | tf_op jit(solution)/shard_map/all_to_all | solution.py:267
  24.5 0.7 fusion.58
  25.2 0.7 fusion.59
  26.0 0.6 broadcast.142
  26.6 1.4 reduce.14
  28.6 1.3 reshape.244.gain_huge
  30.4 0.6 copy-done.1
  31.1 1.9 %shard_map.185 = bf16[8,16,512]{2,1,0:T(8,128)(2,1)} custom-call(s32[1]{0:T(128)} %copy.40.large_groups, s32[16,32]{1,0:T(8,128)} %constant.104.clone.owners, bf16[16,1280]{1,0:T(8,128)(2,1)} %copy-done.1, f32[1,1024]{1,0:T(1,128)} %bitcast.81, f32[1,1280]{1,0:T(1,128)} %reshape.244.gain_huge, f32[8,8,512]{2,1,0:T(8,128)} %get-tuple-element.87.teacher), custom_call_target="tpu_custom_call" | custom-call | tf_op jit(solution)/shard_map/pallas_call | solution.py:202
  33.0 4.3 %all-to-all-done.1 = bf16[4,208,128]{2,1,0:T(8,128)(2,1)S(1)} async-done(((bf16[4,208,128]{2,1,0:T(8,128)(2,1)}), bf16[4,208,128]{2,1,0:T(8,128)(2,1)S(1)}, u32[]{:S(2)}, u32[]{:S(2)}) %all-to-all-start.1) | async-done | bytes 213024 | tf_op jit(solution)/shard_map/all_to_all | solution.py:267
  37.3 9.9 %all-to-all-start = ((bf16[8,16,512]{2,1,0:T(8,128)(2,1)}), bf16[8,16,512]{2,1,0:T(8,128)(2,1)S(1)}, u32[]{:S(2)}, u32[]{:S(2)}) async-start(bf16[8,16,512]{2,1,0:T(8,128)(2,1)} %shard_map.185), calls=%async_computation | async-start | bytes 262144 | tf_op jit(solution)/shard_map/all_to_all | solution.py:284
  47.1 4.2 %collective-permute-start.1 = (bf16[4,208,128]{2,1,0:T(8,128)(2,1)S(1)}, bf16[4,208,128]{2,1,0:T(8,128)(2,1)S(1)}, u32[]{:S(2)}, u32[]{:S(2)}) collective-permute-start(bf16[4,208,128]{2,1,0:T(8,128)(2,1)S(1)} %all-to-all-done.1), channel_id=1, source_target_pairs={{0,32},{32,0},{64,96},{96,64},{128,160},{160,128},{192,224},{224,1... | collective-permute-start | bytes 638984 | tf_op jit(solution)/shard_map/ppermute | solution.py:275
  51.4 2.1 %all-to-all-done = bf16[8,16,512]{2,1,0:T(8,128)(2,1)S(1)} async-done(((bf16[8,16,512]{2,1,0:T(8,128)(2,1)}), bf16[8,16,512]{2,1,0:T(8,128)(2,1)S(1)}, u32[]{:S(2)}, u32[]{:S(2)}) %all-to-all-start) | async-done | bytes 131104 | tf_op jit(solution)/shard_map/all_to_all | solution.py:284
  54.3 11.4 %all_to_all.35 = f32[8,24,256]{2,1,0:T(8,128)S(1)} all-to-all(f32[8,24,256]{2,1,0:T(8,128)S(1)} %pad_maximum_fusion.2), channel_id=1, replica_groups={{0,1,2,3,16,17,18,19},{4,5,6,7,20,21,22,23},{8,9,10,11,24,25,26,27},{12..., dimensions={0} | all-to-all | bytes 393216 | tf_op jit(solution)/shard_map/all_to_all | solution.py:284
  65.9 15.4 %all_to_all.36 = bf16[16,24,256]{2,1,0:T(8,128)(2,1)S(1)} all-to-all(bf16[16,24,256]{2,1,0:T(8,128)(2,1)S(1)} %broadcast_in_dim.137), channel_id=1, replica_groups={{0,1,2,3,4,5,6,7,8,9,10,11,12,13,14,15},{16,17,18,19,20,21,22,23,24,25,..., dimensions={0} | all-to-all | bytes 393216 | tf_op jit(solution)/shard_map/all_to_all | solution.py:342
  81.4 5.2 %all_gather.3 = bf16[32,24,256]{2,1,0:T(8,128)(2,1)S(1)} all-gather(bf16[16,24,256]{2,1,0:T(8,128)(2,1)S(1)} %all_to_all.36), channel_id=1, replica_groups={{0,16},{1,17},{2,18},{3,19},{4,20},{5,21},{6,22},{7,23},{8,24},{9,25},{..., dimensions={0}, use_global_device_ids=true | all-gather | bytes 589824 | tf_op jit(solution)/shard_map/all_gather | solution.py:350
  86.6 0.4 fusion.70
  87.8 0.5 fusion.69
  88.3 0.6 fusion.5
  88.9 21.4 %all_to_all.37 = f32[32,6,128]{2,1,0:T(8,128)S(1)} all-to-all(f32[32,6,128]{2,1,0:T(8,128)S(1)} %broadcast_in_dim.142), channel_id=1, replica_groups=mesh['group'=16,'tensor'=32] {'tensor'}, dimensions={0} | all-to-all | bytes 196608 | tf_op jit(solution)/shard_map/all_to_all | solution.py:347
  110.6 0.4 multiply_convert_fusion
  111.1 7.3 %collective-permute-start.2 = (bf16[272,1280]{1,0:T(8,128)(2,1)S(1)}, bf16[272,1280]{1,0:T(8,128)(2,1)S(1)}, u32[]{:S(2)}, u32[]{:S(2)}) collective-permute-start(bf16[272,1280]{1,0:T(8,128)(2,1)S(1)} %pad_maximum_fusion), channel_id=1, source_target_pairs={{0,32},{32,0},{64,96},{96,64},{128,160},{160,128},{192,224},{224,1... | collective-permute-start | bytes 2088968 | tf_op jit(solution)/shard_map/ppermute | solution.py:404
  118.5 0.4 fusion.13
  118.9 1.3 collective-permute-done.2
  120.3 0.4 fusion.1
  120.8 14.6 %all_to_all.38 = bf16[8,32,1152]{2,1,0:T(8,128)(2,1)S(1)} all-to-all(bf16[8,32,1152]{2,1,0:T(8,128)(2,1)S(1)} %pad_maximum_fusion.1), channel_id=1, replica_groups={{0,64,128,192,256,320,384,448},{32,96,160,224,288,352,416,480},{1,65,12..., dimensions={0} | all-to-all | bytes 1179648 | tf_op jit(solution)/shard_map/all_to_all | solution.py:424
  135.6 12.5 %all_to_all.39 = bf16[8,32,1024]{2,1,0:T(8,128)(2,1)S(1)} all-to-all(bf16[8,32,1024]{2,1,0:T(8,128)(2,1)S(1)} %broadcast_in_dim.148), channel_id=1, replica_groups={{0,64,128,192,256,320,384,448},{32,96,160,224,288,352,416,480},{1,65,12..., dimensions={0} | all-to-all | bytes 1048576 | tf_op jit(solution)/shard_map/all_to_all | solution.py:431
  148.0 4.7 %collective-permute-start.3 = (bf16[256,1024]{1,0:T(8,128)(2,1)S(1)}, bf16[256,1024]{1,0:T(8,128)(2,1)S(1)}, u32[]{:S(2)}, u32[]{:S(2)}) collective-permute-start(bf16[256,1024]{1,0:T(8,128)(2,1)S(1)} %bitcast.74), channel_id=1, source_target_pairs={{0,32},{32,0},{64,96},{96,64},{128,160},{160,128},{192,224},{224,1... | collective-permute-start | bytes 1572872 | tf_op jit(solution)/shard_map/ppermute | solution.py:439
  152.8 0.6 convert_reduce_fusion.1
  154.3 1.1 broadcast_select_fusion
  (73 shorter events, 3.9 us)
Async XLA Ops:
  0.6 85.9 %copy-start = (bf16[256,1024]{1,0:T(8,128)(2,1)S(1)}, bf16[256,1024]{1,0:T(8,128)(2,1)}, u32[]{:S(2)}) copy-start(bf16[256,1024]{1,0:T(8,128)(2,1)} %param.20) | copy-start | bytes 1572868
  2.1 28.3 %collective-permute-start = (bf16[16,1280]{1,0:T(8,128)(2,1)S(1)}, bf16[16,1280]{1,0:T(8,128)(2,1)S(1)}, u32[]{:S(2)}, u32[]{:S(2)}) collective-permute-start(bf16[16,1280]{1,0:T(8,128)(2,1)S(1)} %pad_select_fusion), channel_id=1, source_target_pairs={{0,9},{1,8},{2,43},{3,42},{4,64},{5,74},{6,98},{7,108},{8,136},{9,... | collective-permute-start | bytes 122888 | tf_op jit(solution)/shard_map/ppermute | solution.py:262
  19.9 17.4 %all-to-all-start.1 = ((bf16[4,208,128]{2,1,0:T(8,128)(2,1)}), bf16[4,208,128]{2,1,0:T(8,128)(2,1)S(1)}, u32[]{:S(2)}, u32[]{:S(2)}) async-start(bf16[4,208,128]{2,1,0:T(8,128)(2,1)} %get-tuple-element.99), calls=%async_computation.1 | async-start | bytes 425984 | tf_op jit(solution)/shard_map/all_to_all | solution.py:267
  30.4 0.6 copy-start.1
  37.3 16.3 %all-to-all-start = ((bf16[8,16,512]{2,1,0:T(8,128)(2,1)}), bf16[8,16,512]{2,1,0:T(8,128)(2,1)S(1)}, u32[]{:S(2)}, u32[]{:S(2)}) async-start(bf16[8,16,512]{2,1,0:T(8,128)(2,1)} %shard_map.185), calls=%async_computation | async-start | bytes 262144 | tf_op jit(solution)/shard_map/all_to_all | solution.py:284
  47.1 6.4 %collective-permute-start.1 = (bf16[4,208,128]{2,1,0:T(8,128)(2,1)S(1)}, bf16[4,208,128]{2,1,0:T(8,128)(2,1)S(1)}, u32[]{:S(2)}, u32[]{:S(2)}) collective-permute-start(bf16[4,208,128]{2,1,0:T(8,128)(2,1)S(1)} %all-to-all-done.1), channel_id=1, source_target_pairs={{0,32},{32,0},{64,96},{96,64},{128,160},{160,128},{192,224},{224,1... | collective-permute-start | bytes 638984 | tf_op jit(solution)/shard_map/ppermute | solution.py:275
  65.7 20.9 %copy-start.2 = (f32[1024]{0:T(1024)S(1)}, f32[1024]{0:T(1024)}, u32[]{:S(2)}) copy-start(f32[1024]{0:T(1024)} %param.21) | copy-start | bytes 12292
  86.6 1.0 copy-start.3
  86.6 1.2 copy-start.4
  111.1 9.1 %collective-permute-start.2 = (bf16[272,1280]{1,0:T(8,128)(2,1)S(1)}, bf16[272,1280]{1,0:T(8,128)(2,1)S(1)}, u32[]{:S(2)}, u32[]{:S(2)}) collective-permute-start(bf16[272,1280]{1,0:T(8,128)(2,1)S(1)} %pad_maximum_fusion), channel_id=1, source_target_pairs={{0,32},{32,0},{64,96},{96,64},{128,160},{160,128},{192,224},{224,1... | collective-permute-start | bytes 2088968 | tf_op jit(solution)/shard_map/ppermute | solution.py:404
  148.0 6.3 %collective-permute-start.3 = (bf16[256,1024]{1,0:T(8,128)(2,1)S(1)}, bf16[256,1024]{1,0:T(8,128)(2,1)S(1)}, u32[]{:S(2)}, u32[]{:S(2)}) collective-permute-start(bf16[256,1024]{1,0:T(8,128)(2,1)S(1)} %bitcast.74), channel_id=1, source_target_pairs={{0,32},{32,0},{64,96},{96,64},{128,160},{160,128},{192,224},{224,1... | collective-permute-start | bytes 1572872 | tf_op jit(solution)/shard_map/ppermute | solution.py:439

commit v8 on v6

--- a/solution.py
+++ b/solution.py
@@ -38,14 +38,13 @@
     return jnp.stack([high, middle, low]).astype(jnp.bfloat16)
 
 
-def crop_rows(routes, group, large, places):
+def crop_rows(routes, group, large, own_places):
     target_group = lax.dynamic_index_in_dim(routes[:, 0].reshape(-1, CG), group, 0, keepdims=False)
     earlier = jnp.arange(CG)[:, None] > jnp.arange(CG)[None, :]
     matching = target_group[:, None] == target_group[None, :]
     slot_rank = jnp.sum((matching & earlier).astype(jnp.int32), axis=1)
-    slots = places.shape[1]
-    own_places = lax.dynamic_index_in_dim(places, group, 0, keepdims=False)
-    crop_slot = target_group * (slots // places.shape[0]) + slot_rank
+    slots = own_places.shape[0]
+    crop_slot = target_group * (slots * CG // routes.shape[0]) + slot_rank
     named = crop_slot[:, None] == jnp.arange(slots, dtype=jnp.int32)[None, :]
     first_row = jnp.sum(jnp.where(named, own_places[None, :], 0), axis=1) * PATCH
     row_slot = (first_row[:, None] + jnp.arange(PATCH, dtype=jnp.int32)[None, :]).reshape(-1)
@@ -260,9 +259,10 @@
         for k in range(slots_per)
     ]
     student_feat = lax.ppermute(student_feat, ("group", "tensor"), swap)
-    places, owners = jnp.array(places, jnp.int32), jnp.array(owners, jnp.int32)
-    own_owners = lax.dynamic_index_in_dim(owners, own_group, 0, keepdims=False)
-    large_places = own_owners // slots_per < large_groups[0]
+    table = [[owners[g], places[g], places[g ^ 1]] for g in range(groups)]
+    owners = jnp.array(owners, jnp.int32)
+    table = lax.dynamic_index_in_dim(jnp.array(table, jnp.int32), own_group, 0, keepdims=False)
+    large_places = table[0] // slots_per < large_groups[0]
 
     held = lax.all_to_all(
         weights,
@@ -290,8 +290,8 @@
             axis_index_groups=near_groups,
         )
 
-    row_slot, crop_large = crop_rows(routes, own_group, large_groups[0], places)
-    _, other_large = crop_rows(routes, own_group ^ 1, large_groups[0], places)
+    row_slot, crop_large = crop_rows(routes, own_group, large_groups[0], table[1])
+    _, other_large = crop_rows(routes, own_group ^ 1, large_groups[0], table[2])
     near_large = lax.dynamic_index_in_dim(
         large_places.reshape(halves, FAR, FAR), own_far, 1, keepdims=False
     ).reshape(-1)
@@ -386,7 +386,7 @@
             student_top + jnp.log(student_sum),
         ]
     )
-    stats = jnp.broadcast_to(stats.reshape(1, -1, 128), (tensors, stats.size // 128, 128))
+    stats = jnp.broadcast_to(stats[None], (tensors, *stats.shape))
     live = (shifted, scores, student_units, kept_rows, other_rows, own_core)
     stats, live = alone(stats, live, to_tensor)
     shifted, scores, student_units, kept_rows, other_rows, own_core = live

time: 157 us -> 157 us (level)
  no operation moved by 1% of the time
where the time goes in v8:
time: 157 us; the launch traced here: 156 us
  blocking collectives  80.5 us (51%)
  starting transfers between devices  46.8 us (30%)
  waiting for transfers between devices  8.83 us (6%)
  other arithmetic  6.22 us (4%)
  local copies, waits for them, and re-layouts  4.44 us (3%)
  Pallas kernels  3.64 us (2%)
  between operations  3.47 us (2%)
  matrix products  2.59 us (2%)
    all_to_all x1, blocking collectives, to_tensor(): lax.all_to_all(values, 'tensor', split_axis=0, concat_axis=0, tiled=True)  21.4 us
    ppermute x1, starting transfers between devices, shards(): student_feat = lax.ppermute(student_feat, ('group', 'tensor'), swap)  15.9 us
    all_to_all x1, blocking collectives, to_ring(): lax.all_to_all(values, 'tensor', split_axis=0, concat_axis=0, tiled=True,...  15.4 us
    all_to_all x1, blocking collectives, shards(): lax.all_to_all(sent, 'group', split_axis=0, concat_axis=0, tiled=True, ax...  14.7 us
    all_to_all x1, blocking collectives, shards(): lax.all_to_all(jnp.broadcast_to(summed.astype(jnp.bfloat16)[None], (chips...  12.5 us
    all_to_all x1, blocking collectives, to_near(): lax.all_to_all(values, 'tensor', split_axis=0, concat_axis=0, tiled=True,...  11.4 us
    all_to_all x1, starting transfers between devices, to_near(): lax.all_to_all(values, 'tensor', split_axis=0, concat_axis=0, tiled=True,...  9.9 us
    ppermute x1, starting transfers between devices, shards(): lax.ppermute(jnp.concatenate([jnp.concatenate([deltas, student_units], ax...  7.33 us
  transfers between devices with their start and end apart: 6, of which 4 were waited for; matrix products, arithmetic and copies ran while one was open for 4% of the time, Pallas kernels for 2%

profile of v8, /device:TPU:1, one launch (start us, length us, event | category | flops | bytes accessed | tf_op | source)
XLA Modules:
  0.0 156.5 jit_solution(6817777303243313665)
XLA Ops:
  1.4 0.8 pad_select_fusion
  2.1 15.9 %collective-permute-start = (bf16[16,1280]{1,0:T(8,128)(2,1)S(1)}, bf16[16,1280]{1,0:T(8,128)(2,1)S(1)}, u32[]{:S(2)}, u32[]{:S(2)}) collective-permute-start(bf16[16,1280]{1,0:T(8,128)(2,1)S(1)} %pad_select_fusion), channel_id=1, source_target_pairs={{0,9},{1,8},{2,43},{3,42},{4,64},{5,74},{6,98},{7,108},{8,136},{9,... | collective-permute-start | bytes 122888 | tf_op jit(solution)/shard_map/ppermute | solution.py:261
  18.1 1.8 %shard_map.184 = (bf16[4,208,128]{2,1,0:T(8,128)(2,1)}, bf16[8,8,512]{2,1,0:T(8,128)(2,1)}) custom-call(bf16[128,256]{1,0:T(8,128)(2,1)} %teacher_w.1, bf16[32,256]{1,0:T(8,128)(2,1)} %large_w.1, bf16[40,256]{1,0:T(8,128)(2,1)} %huge_w.1, bf16[8,4096]{1,0:T(8,128)(2,1)} %teacher_x.1, f32[1,4096]{1,0:T(1,128)} %bitcast.85), custom_call_target="tpu_custom_call" | custom-call | tf_op jit(solution)/shard_map/pallas_call | solution.py:161
  19.8 4.6 %all-to-all-start.1 = ((bf16[4,208,128]{2,1,0:T(8,128)(2,1)}), bf16[4,208,128]{2,1,0:T(8,128)(2,1)S(1)}, u32[]{:S(2)}, u32[]{:S(2)}) async-start(bf16[4,208,128]{2,1,0:T(8,128)(2,1)} %get-tuple-element.99), calls=%async_computation.1 | async-start | bytes 425984 | tf_op jit(solution)/shard_map/all_to_all | solution.py:267
  24.5 0.7 constant_dynamic-slice_fusion.5
  25.3 0.5 broadcast.143
  25.8 1.3 reduce.14
  27.7 1.3 reshape.244.gain_huge
  29.6 0.6 copy-done.1
  30.2 1.9 %shard_map.185 = bf16[8,16,512]{2,1,0:T(8,128)(2,1)} custom-call(s32[1]{0:T(128)} %copy.36.large_groups, s32[16,32]{1,0:T(8,128)} %constant.101.clone.owners, bf16[16,1280]{1,0:T(8,128)(2,1)} %copy-done.1, f32[1,1024]{1,0:T(1,128)} %bitcast.86, f32[1,1280]{1,0:T(1,128)} %reshape.244.gain_huge, bf16[8,8,512]{2,1,0:T(8,128)(2,1)} %get-tuple-element.87.teacher), custom_call_target="tpu_custom_call" | custom-call | tf_op jit(solution)/shard_map/pallas_call | solution.py:201
  32.1 5.1 %all-to-all-done.1 = bf16[4,208,128]{2,1,0:T(8,128)(2,1)S(1)} async-done(((bf16[4,208,128]{2,1,0:T(8,128)(2,1)}), bf16[4,208,128]{2,1,0:T(8,128)(2,1)S(1)}, u32[]{:S(2)}, u32[]{:S(2)}) %all-to-all-start.1) | async-done | bytes 213024 | tf_op jit(solution)/shard_map/all_to_all | solution.py:267
  37.2 9.9 %all-to-all-start = ((bf16[8,16,512]{2,1,0:T(8,128)(2,1)}), bf16[8,16,512]{2,1,0:T(8,128)(2,1)S(1)}, u32[]{:S(2)}, u32[]{:S(2)}) async-start(bf16[8,16,512]{2,1,0:T(8,128)(2,1)} %shard_map.185), calls=%async_computation | async-start | bytes 262144 | tf_op jit(solution)/shard_map/all_to_all | solution.py:284
  47.1 4.2 %collective-permute-start.1 = (bf16[4,208,128]{2,1,0:T(8,128)(2,1)S(1)}, bf16[4,208,128]{2,1,0:T(8,128)(2,1)S(1)}, u32[]{:S(2)}, u32[]{:S(2)}) collective-permute-start(bf16[4,208,128]{2,1,0:T(8,128)(2,1)S(1)} %all-to-all-done.1), channel_id=1, source_target_pairs={{0,32},{32,0},{64,96},{96,64},{128,160},{160,128},{192,224},{224,1... | collective-permute-start | bytes 638984 | tf_op jit(solution)/shard_map/ppermute | solution.py:275
  51.3 2.1 %all-to-all-done = bf16[8,16,512]{2,1,0:T(8,128)(2,1)S(1)} async-done(((bf16[8,16,512]{2,1,0:T(8,128)(2,1)}), bf16[8,16,512]{2,1,0:T(8,128)(2,1)S(1)}, u32[]{:S(2)}, u32[]{:S(2)}) %all-to-all-start) | async-done | bytes 131104 | tf_op jit(solution)/shard_map/all_to_all | solution.py:284
  54.2 11.4 %all_to_all.35 = f32[8,24,256]{2,1,0:T(8,128)S(1)} all-to-all(f32[8,24,256]{2,1,0:T(8,128)S(1)} %pad_maximum_fusion.2), channel_id=1, replica_groups={{0,1,2,3,16,17,18,19},{4,5,6,7,20,21,22,23},{8,9,10,11,24,25,26,27},{12..., dimensions={0} | all-to-all | bytes 393216 | tf_op jit(solution)/shard_map/all_to_all | solution.py:284
  65.9 15.4 %all_to_all.36 = bf16[16,24,256]{2,1,0:T(8,128)(2,1)S(1)} all-to-all(bf16[16,24,256]{2,1,0:T(8,128)(2,1)S(1)} %broadcast_in_dim.135), channel_id=1, replica_groups={{0,1,2,3,4,5,6,7,8,9,10,11,12,13,14,15},{16,17,18,19,20,21,22,23,24,25,..., dimensions={0} | all-to-all | bytes 393216 | tf_op jit(solution)/shard_map/all_to_all | solution.py:342
  81.3 5.2 %all_gather.3 = bf16[32,24,256]{2,1,0:T(8,128)(2,1)S(1)} all-gather(bf16[16,24,256]{2,1,0:T(8,128)(2,1)S(1)} %all_to_all.36), channel_id=1, replica_groups={{0,16},{1,17},{2,18},{3,19},{4,20},{5,21},{6,22},{7,23},{8,24},{9,25},{..., dimensions={0}, use_global_device_ids=true | all-gather | bytes 589824 | tf_op jit(solution)/shard_map/all_gather | solution.py:350
  86.6 0.4 fusion.72
  87.3 0.3 copy-done.3
  87.7 0.5 fusion.71
  88.3 0.6 fusion.5
  88.9 21.4 %all_to_all.37 = f32[32,3,256]{2,1,0:T(4,128)S(1)} all-to-all(f32[32,3,256]{2,1,0:T(4,128)S(1)} %broadcast_in_dim.139), channel_id=1, replica_groups=mesh['group'=16,'tensor'=32] {'tensor'}, dimensions={0} | all-to-all | bytes 196608 | tf_op jit(solution)/shard_map/all_to_all | solution.py:347
  110.6 0.4 multiply_convert_fusion
  111.1 7.3 %collective-permute-start.2 = (bf16[272,1280]{1,0:T(8,128)(2,1)S(1)}, bf16[272,1280]{1,0:T(8,128)(2,1)S(1)}, u32[]{:S(2)}, u32[]{:S(2)}) collective-permute-start(bf16[272,1280]{1,0:T(8,128)(2,1)S(1)} %pad_maximum_fusion), channel_id=1, source_target_pairs={{0,32},{32,0},{64,96},{96,64},{128,160},{160,128},{192,224},{224,1... | collective-permute-start | bytes 2088968 | tf_op jit(solution)/shard_map/ppermute | solution.py:404
  118.5 0.4 fusion.13
  118.9 1.3 collective-permute-done.2
  120.2 0.4 fusion.1
  120.7 14.7 %all_to_all.38 = bf16[8,32,1152]{2,1,0:T(8,128)(2,1)S(1)} all-to-all(bf16[8,32,1152]{2,1,0:T(8,128)(2,1)S(1)} %pad_maximum_fusion.1), channel_id=1, replica_groups={{0,64,128,192,256,320,384,448},{32,96,160,224,288,352,416,480},{1,65,12..., dimensions={0} | all-to-all | bytes 1179648 | tf_op jit(solution)/shard_map/all_to_all | solution.py:424
  135.5 12.5 %all_to_all.39 = bf16[8,32,1024]{2,1,0:T(8,128)(2,1)S(1)} all-to-all(bf16[8,32,1024]{2,1,0:T(8,128)(2,1)S(1)} %broadcast_in_dim.145), channel_id=1, replica_groups={{0,64,128,192,256,320,384,448},{32,96,160,224,288,352,416,480},{1,65,12..., dimensions={0} | all-to-all | bytes 1048576 | tf_op jit(solution)/shard_map/all_to_all | solution.py:431
  148.0 4.7 %collective-permute-start.3 = (bf16[256,1024]{1,0:T(8,128)(2,1)S(1)}, bf16[256,1024]{1,0:T(8,128)(2,1)S(1)}, u32[]{:S(2)}, u32[]{:S(2)}) collective-permute-start(bf16[256,1024]{1,0:T(8,128)(2,1)S(1)} %bitcast.79), channel_id=1, source_target_pairs={{0,32},{32,0},{64,96},{96,64},{128,160},{160,128},{192,224},{224,1... | collective-permute-start | bytes 1572872 | tf_op jit(solution)/shard_map/ppermute | solution.py:439
  152.8 0.6 convert_reduce_fusion.1
  154.3 1.1 broadcast_select_fusion
  (73 shorter events, 3.5 us)
Async XLA Ops:
  0.6 85.9 %copy-start = (bf16[256,1024]{1,0:T(8,128)(2,1)S(1)}, bf16[256,1024]{1,0:T(8,128)(2,1)}, u32[]{:S(2)}) copy-start(bf16[256,1024]{1,0:T(8,128)(2,1)} %param.20) | copy-start | bytes 1572868
  2.1 27.4 %collective-permute-start = (bf16[16,1280]{1,0:T(8,128)(2,1)S(1)}, bf16[16,1280]{1,0:T(8,128)(2,1)S(1)}, u32[]{:S(2)}, u32[]{:S(2)}) collective-permute-start(bf16[16,1280]{1,0:T(8,128)(2,1)S(1)} %pad_select_fusion), channel_id=1, source_target_pairs={{0,9},{1,8},{2,43},{3,42},{4,64},{5,74},{6,98},{7,108},{8,136},{9,... | collective-permute-start | bytes 122888 | tf_op jit(solution)/shard_map/ppermute | solution.py:261
  19.8 17.4 %all-to-all-start.1 = ((bf16[4,208,128]{2,1,0:T(8,128)(2,1)}), bf16[4,208,128]{2,1,0:T(8,128)(2,1)S(1)}, u32[]{:S(2)}, u32[]{:S(2)}) async-start(bf16[4,208,128]{2,1,0:T(8,128)(2,1)} %get-tuple-element.99), calls=%async_computation.1 | async-start | bytes 425984 | tf_op jit(solution)/shard_map/all_to_all | solution.py:267
  29.6 0.6 copy-start.1
  37.2 16.3 %all-to-all-start = ((bf16[8,16,512]{2,1,0:T(8,128)(2,1)}), bf16[8,16,512]{2,1,0:T(8,128)(2,1)S(1)}, u32[]{:S(2)}, u32[]{:S(2)}) async-start(bf16[8,16,512]{2,1,0:T(8,128)(2,1)} %shard_map.185), calls=%async_computation | async-start | bytes 262144 | tf_op jit(solution)/shard_map/all_to_all | solution.py:284
  47.1 6.4 %collective-permute-start.1 = (bf16[4,208,128]{2,1,0:T(8,128)(2,1)S(1)}, bf16[4,208,128]{2,1,0:T(8,128)(2,1)S(1)}, u32[]{:S(2)}, u32[]{:S(2)}) collective-permute-start(bf16[4,208,128]{2,1,0:T(8,128)(2,1)S(1)} %all-to-all-done.1), channel_id=1, source_target_pairs={{0,32},{32,0},{64,96},{96,64},{128,160},{160,128},{192,224},{224,1... | collective-permute-start | bytes 638984 | tf_op jit(solution)/shard_map/ppermute | solution.py:275
  65.6 20.9 %copy-start.2 = (f32[1024]{0:T(1024)S(1)}, f32[1024]{0:T(1024)}, u32[]{:S(2)}) copy-start(f32[1024]{0:T(1024)} %param.21) | copy-start | bytes 12292
  86.5 1.0 copy-start.3
  86.5 1.2 copy-start.4
  111.1 9.1 %collective-permute-start.2 = (bf16[272,1280]{1,0:T(8,128)(2,1)S(1)}, bf16[272,1280]{1,0:T(8,128)(2,1)S(1)}, u32[]{:S(2)}, u32[]{:S(2)}) collective-permute-start(bf16[272,1280]{1,0:T(8,128)(2,1)S(1)} %pad_maximum_fusion), channel_id=1, source_target_pairs={{0,32},{32,0},{64,96},{96,64},{128,160},{160,128},{192,224},{224,1... | collective-permute-start | bytes 2088968 | tf_op jit(solution)/shard_map/ppermute | solution.py:404
  148.0 6.3 %collective-permute-start.3 = (bf16[256,1024]{1,0:T(8,128)(2,1)S(1)}, bf16[256,1024]{1,0:T(8,128)(2,1)S(1)}, u32[]{:S(2)}, u32[]{:S(2)}) collective-permute-start(bf16[256,1024]{1,0:T(8,128)(2,1)S(1)} %bitcast.79), channel_id=1, source_target_pairs={{0,32},{32,0},{64,96},{96,64},{128,160},{160,128},{192,224},{224,1... | collective-permute-start | bytes 1572872 | tf_op jit(solution)/shard_map/ppermute | solution.py:439
